TPU v7x, 512 devices: a whole 4x8x8 slice. The times are simulated.
512 devices in a mesh: dp: 16 (over y_hi, z), clip: 32 (over y_lo, x, core).
Axes of the slice: x: 4, y: 8 (y_hi: 2, y_lo: 4; y = y_hi * 4 + y_lo), z: 8, core: 2. Of those that a mesh axis runs over, the one named last changes fastest.
Arguments:
- clip_embed: bfloat16 [4096, 16, 1408], P(('dp', 'clip')), may hold values from -8 to 8
- clip_counts: int32 [4096], P(('dp', 'clip')), may hold values from 1 to 16
- pool_query: bfloat16 [1408], replicated, as said below
- proj_weight: bfloat16 [1408, 768], P('clip'), may hold values from -0.3 to 0.3
- text_embed: bfloat16 [4096, 768], P(('dp', 'clip')), may hold values from -8 to 8
- pair_index: int32 [4096], replicated, may hold values from 0 to 4095, each once
- logit_scale: float32 [1], replicated, may hold values from 10 to 40
Outputs:
- d_clips: bfloat16 [4096, 16, 1408], P(('dp', 'clip'))
- d_weight: float32 [1408, 768], P('clip')
- d_texts: float32 [4096, 768], P(('dp', 'clip'))
Inputs may be any that keep to these rules, and one draw needn't show every extreme that they name: `pool_query`: independent normal values with standard deviation 2 / sqrt(1408).
All inputs are finite; a program needn't handle non-finite values.
Results may differ from a plain program's by a relative error of at most 0.022.
Values may be sent and summed in bfloat16 or wider, within the bound.
No kernel may reach another device: no remote copies, remote signals or barrier semaphores. Data moves between devices by JAX's collectives and lax.ppermute only.
A program may use at most 64 MiB of HBM per device.

v0:
```python
import jax
import jax.numpy as jnp
from jax import lax
from jax.sharding import PartitionSpec as P

EPS = 1e-06


def unit_rows(values):
    norm_value = jnp.sqrt(jnp.sum(values * values, axis=1, keepdims=True) + EPS)
    return (values / norm_value, norm_value)


def shards(clip_embed, clip_counts, pool_query, proj_weight, text_embed, pair_index, logit_scale):
    videos_dev = clip_embed.shape[0]
    clips_all = clip_embed.shape[1]
    n_groups = lax.axis_size("dp")
    n_lanes = lax.axis_size("clip")
    group_id = lax.axis_index("dp")
    lane_id = lax.axis_index("clip")
    query_f = pool_query.astype(jnp.float32)
    embed_f = clip_embed.astype(jnp.float32)
    scores = jnp.einsum("vce,e->vc", embed_f, query_f)
    position = jnp.arange(clips_all, dtype=jnp.int32)
    usable = position[None, :] < clip_counts[:, None]
    masked = jnp.where(usable, scores, -1e30)
    top_score = jnp.max(masked, axis=1, keepdims=True)
    raised = jnp.where(usable, jnp.exp(masked - top_score), 0.0)
    weights = raised / jnp.sum(raised, axis=1, keepdims=True)
    summary = jnp.einsum("vc,vce->ve", weights, embed_f)
    summary_b = summary.astype(jnp.bfloat16)
    full_weight = lax.all_gather(proj_weight, "clip", axis=0, tiled=True)
    projected = jnp.dot(summary_b, full_weight, preferred_element_type=jnp.float32)
    unit_video, video_norm = unit_rows(projected)
    unit_text, text_norm = unit_rows(text_embed.astype(jnp.float32))
    video_b = unit_video.astype(jnp.bfloat16)
    text_b = unit_text.astype(jnp.bfloat16)
    logit_mult = logit_scale[0]
    own_slots = jnp.arange(videos_dev, dtype=jnp.int32)
    lane_block = group_id * n_lanes * videos_dev + jnp.arange(n_lanes * videos_dev, dtype=jnp.int32)
    group_block = (
        (jnp.arange(n_groups, dtype=jnp.int32)[:, None] * n_lanes + lane_id) * videos_dev
        + own_slots[None, :]
    ).reshape(-1)
    row_embed = lax.all_gather(video_b, "clip", axis=0, tiled=True)
    col_embed = lax.all_gather(text_b, "dp", axis=0, tiled=True)
    expo = jnp.exp(logit_mult * jnp.dot(row_embed, col_embed.T, preferred_element_type=jnp.float32))
    row_part = jnp.sum(expo, axis=1)
    col_part = jnp.sum(expo, axis=0)
    lane_part, group_part = (row_part, col_part)
    lane_sum = lax.psum(lane_part, "clip")
    group_sum = lax.psum(group_part, "dp")
    row_total, col_total = (lane_sum, group_sum)
    row_pairs = pair_index[lane_block]
    positive = (group_block[None, :] == row_pairs[:, None]).astype(jnp.float32)
    grad_logits = ((expo / row_total[:, None] + expo / col_total[None, :]) * 0.5 - positive).astype(
        jnp.bfloat16
    )
    block = grad_logits
    d_video = lax.psum_scatter(
        logit_mult * jnp.dot(block, col_embed, preferred_element_type=jnp.float32),
        "clip",
        scatter_dimension=0,
        tiled=True,
    )
    block = grad_logits
    d_text = lax.psum_scatter(
        logit_mult
        * lax.dot_general(
            block, row_embed, (((0,), (0,)), ((), ())), preferred_element_type=jnp.float32
        ),
        "dp",
        scatter_dimension=0,
        tiled=True,
    )
    d_projected = (
        (d_video - unit_video * jnp.sum(unit_video * d_video, axis=1, keepdims=True)) / video_norm
    ).astype(jnp.bfloat16)
    d_texts = (d_text - unit_text * jnp.sum(unit_text * d_text, axis=1, keepdims=True)) / text_norm
    summary_cols = lax.all_to_all(summary_b, "clip", split_axis=1, concat_axis=0, tiled=True)
    weight_term = lax.dot_general(
        summary_cols,
        lax.all_gather(d_projected, "clip", axis=0, tiled=True),
        (((0,), (0,)), ((), ())),
        preferred_element_type=jnp.float32,
    )
    d_weight = lax.psum(weight_term, "dp")
    d_summary = jnp.dot(d_projected, full_weight.T, preferred_element_type=jnp.float32)
    aligned = jnp.einsum("vce,ve->vc", embed_f, d_summary)
    baseline = jnp.sum(d_summary * summary, axis=1, keepdims=True)
    d_scores = weights * (aligned - baseline)
    d_clips = (
        weights[:, :, None] * d_summary[:, None, :] + d_scores[:, :, None] * query_f[None, None, :]
    ).astype(jnp.bfloat16)
    return (d_clips, d_weight, d_texts)


def solution(mesh):
    return jax.shard_map(
        shards,
        mesh=mesh,
        in_specs=(
            P(("dp", "clip"), None, None),
            P(("dp", "clip")),
            P(),
            P("clip", None),
            P(("dp", "clip"), None),
            P(),
            P(),
        ),
        out_specs=(P(("dp", "clip"), None, None), P("clip", None), P(("dp", "clip"), None)),
        check_vma=False,
    )
```

profile of v0, /device:TPU:1, one launch (start us, length us, event | category | flops | bytes accessed | tf_op | source)
XLA Modules:
  0.0 823.2 jit_solution(15839699523008020178)
XLA Ops:
  10.0 0.9 fusion.8
  10.9 0.8 fusion.10
  12.7 2.0 gather_fusion
  14.7 0.8 fusion.6
  16.3 55.0 %all_gather.14 = bf16[128,768]{1,0:T(8,128)(2,1)S(1)} all-gather(bf16[8,768]{1,0:T(8,128)(2,1)S(1)} %fusion.11), channel_id=1, replica_groups=mesh['dp'=16,'clip'=32] {'dp'}, dimensions={0}, use_global_device_ids=true | all-gather | bytes 208896 | tf_op jit(solution)/shard_map/all_gather | solution.py:46
  71.3 8.4 %all-gather.3.cloned.1.call-done = bf16[32,44,768]{2,1,0:T(8,128)(2,1)} async-done(((bf16[1,44,768]{2,1,0:T(8,128)(2,1)}), bf16[32,44,768]{2,1,0:T(8,128)(2,1)}) %all-gather.3.cloned.1.call-update) | async-done | bytes 2162704 | tf_op jit(solution)/shard_map/all_gather | solution.py:32
  79.6 2.6 reshape.82
  82.8 41.7 %all_gather.13 = bf16[256,768]{1,0:T(8,128)(2,1)S(1)} all-gather(bf16[8,768]{1,0:T(8,128)(2,1)S(1)} %fusion.12), channel_id=1, replica_groups=mesh['dp'=16,'clip'=32] {'clip'}, dimensions={0}, use_global_device_ids=true | all-gather | bytes 405504 | tf_op jit(solution)/shard_map/all_gather | solution.py:45
  124.8 66.9 %psum.21 = f32[256]{0:T(256)S(1)} all-reduce(f32[256]{0:T(256)S(1)} %get-tuple-element.3), channel_id=1, replica_groups=mesh['dp'=16,'clip'=32] {'clip'}, use_global_device_ids=true, to_apply=%region_5.6 | all-reduce | flops 256 | bytes 2048 | tf_op jit(solution)/shard_map/psum | solution.py:51
  191.7 46.5 %psum.22 = f32[128]{0:T(128)S(1)} all-reduce(f32[128]{0:T(128)S(1)} %get-tuple-element.4), channel_id=1, replica_groups=mesh['dp'=16,'clip'=32] {'dp'}, use_global_device_ids=true, to_apply=%region_7.8 | all-reduce | flops 128 | bytes 1024 | tf_op jit(solution)/shard_map/psum | solution.py:52
  238.2 1.1 convolution_multiply_fusion.1
  239.4 1.2 convolution_multiply_fusion
  241.6 11.9 %all-to-all-start = ((bf16[32,2,176]{2,1,0:T(2,128)(2,1)}), bf16[32,2,176]{2,1,0:T(2,128)(2,1)S(1)}, u32[]{:S(2)}, u32[]{:S(2)}) async-start(bf16[32,2,176]{2,1,0:T(2,128)(2,1)} %reshape.89), calls=%async_computation.1 | async-start | bytes 65536 | tf_op jit(solution)/shard_map/all_to_all | solution.py:80
  253.5 7.7 all-to-all-done
  261.3 189.6 %reduce-scatter.5.cloned.1.call-done = f32[8,768]{1,0:T(8,128)} async-done(((f32[128,768]{1,0:T(8,128)}), f32[8,768]{1,0:T(8,128)}) %reduce-scatter.5.cloned.1.call-update) | async-done | bytes 24592 | tf_op jit(solution)/shard_map/reduce_scatter | solution.py:67
  450.9 0.9 multiply_reduce_fusion
  451.8 1.4 subtract_divide_fusion
  453.2 143.2 %reduce-scatter.3.cloned.1.call-done = f32[8,768]{1,0:T(8,128)} async-done(((f32[256,768]{1,0:T(8,128)}), f32[8,768]{1,0:T(8,128)}) %reduce-scatter.3.cloned.1.call-update) | async-done | bytes 24592 | tf_op jit(solution)/shard_map/reduce_scatter | solution.py:60
  596.4 0.9 multiply_reduce_fusion.1
  598.9 43.5 %all_gather.15 = bf16[256,768]{1,0:T(8,128)(2,1)S(1)} all-gather(bf16[8,768]{1,0:T(8,128)(2,1)S(1)} %divide_convert_fusion), channel_id=1, replica_groups=mesh['dp'=16,'clip'=32] {'clip'}, dimensions={0}, use_global_device_ids=true | all-gather | bytes 405504 | tf_op jit(solution)/shard_map/all_gather | solution.py:83
  642.6 0.9 fusion.1
  643.6 0.9 add_convert_fusion
  644.5 170.6 %all-reduce.2.cloned.1.call-done = f32[44,768]{1,0:T(8,128)} async-done(((f32[44,768]{1,0:T(8,128)}), f32[44,768]{1,0:T(8,128)}) %all-reduce.2.cloned.1.call-update) | async-done | bytes 135184 | tf_op jit(solution)/shard_map/psum | solution.py:87
  815.1 1.6 copy.26
  (41 shorter events, 7.9 us)
Async XLA Ops:
  7.2 2.3 copy-start
  7.2 72.5 %all-gather.3.cloned.1.call-start = ((), (), s32[]{:S(2)}) async-start(), calls=%async_computation.6 | async-start | bytes 2433024 | tf_op jit(solution)/shard_map/all_gather | solution.py:32
  7.9 442.9 %reduce-scatter.5.cloned.1.call-start = ((), (), s32[]{:S(2)}) async-start(), calls=%async_computation.5 | async-start | bytes 417792 | tf_op jit(solution)/shard_map/reduce_scatter | solution.py:67
  124.8 128.7 %copy-start.2 = (bf16[1408]{0:T(1024)(128)(2,1)S(1)}, bf16[1408]{0:T(1024)(128)(2,1)}, u32[]{:S(2)}) copy-start(bf16[1408]{0:T(1024)(128)(2,1)} %param.9) | copy-start | bytes 8452
  238.2 212.7 %copy-start.1 = (bf16[8,768]{1,0:T(8,128)(2,1)S(1)}, bf16[8,768]{1,0:T(8,128)(2,1)}, u32[]{:S(2)}) copy-start(bf16[8,768]{1,0:T(8,128)(2,1)} %param.11) | copy-start | bytes 36868
  239.3 357.0 %reduce-scatter.3.cloned.1.call-start = ((), (), s32[]{:S(2)}) async-start(), calls=%async_computation.3 | async-start | bytes 811008 | tf_op jit(solution)/shard_map/reduce_scatter | solution.py:60
  241.6 401.9 %copy-start.3 = (s32[8]{0:T(128)S(1)}, s32[8]{0:T(128)}, u32[]{:S(2)}) copy-start(s32[8]{0:T(128)} %param.8) | copy-start | bytes 100
  241.6 19.6 %all-to-all-start = ((bf16[32,2,176]{2,1,0:T(2,128)(2,1)}), bf16[32,2,176]{2,1,0:T(2,128)(2,1)S(1)}, u32[]{:S(2)}, u32[]{:S(2)}) async-start(bf16[32,2,176]{2,1,0:T(2,128)(2,1)} %reshape.89), calls=%async_computation.1 | async-start | bytes 65536 | tf_op jit(solution)/shard_map/all_to_all | solution.py:80
  253.4 561.6 %all-reduce.2.cloned.1.call-start = ((), (), s32[]{:S(2)}) async-start(), calls=%async_computation.4 | async-start | bytes 294912 | tf_op jit(solution)/shard_map/psum | solution.py:87
Sparse Core Ops, SparseCore 0:
  10.2 69.4 all-gather.2
  239.4 211.3 reduce-scatter.4
  453.9 142.4 reduce-scatter.2
  643.6 171.4 all-reduce.1
where the time goes:
time: 830 us; the launch traced here: 823 us
  waiting for transfers between devices  520 us (63%)
  blocking collectives  253 us (30%)
  between operations  14.6 us (2%)
  starting transfers between devices  12 us (1%)
  other arithmetic  9.33 us (1%)
    reduce_scatter x1, waiting for transfers between devices, shards(): lax.psum_scatter(logit_mult * lax.dot_general(block, row_embed, (((0,), (...  190 us
    psum x1, waiting for transfers between devices, shards(): d_weight = lax.psum(weight_term, 'dp')  171 us
    reduce_scatter x1, waiting for transfers between devices, shards(): lax.psum_scatter(logit_mult * jnp.dot(block, col_embed, preferred_element...  143 us
    psum x1, blocking collectives, shards(): lane_sum = lax.psum(lane_part, 'clip')  66.9 us
    all_gather x1, blocking collectives, shards(): col_embed = lax.all_gather(text_b, 'dp', axis=0, tiled=True)  55 us
    psum x1, blocking collectives, shards(): group_sum = lax.psum(group_part, 'dp')  46.5 us
    all_gather x1, blocking collectives, shards(): lax.all_gather(d_projected, 'clip', axis=0, tiled=True)  43.5 us
    all_gather x1, blocking collectives, shards(): row_embed = lax.all_gather(video_b, 'clip', axis=0, tiled=True)  41.7 us
  transfers between devices with their start and end apart: 5, of which 5 were waited for; matrix products, arithmetic and copies ran while one was open for 2% of the time, Pallas kernels for 0%

commit v1 on v0

v1 whole, which is shorter than its diff:
```python
import jax
import jax.numpy as jnp
from jax import lax
from jax.sharding import Mesh, PartitionSpec as P

EPS = 1e-06
F32 = jnp.float32
BF16 = jnp.bfloat16
DP = ("yh", "z")
CLIP = ("yl", "x", "core")
NEAR = ("x", "core")


def unit_rows(values):
    norm_value = jnp.sqrt(jnp.sum(values * values, axis=1, keepdims=True) + EPS)
    return (values / norm_value, norm_value)


def exchange(blocks, axes):
    return lax.all_to_all(blocks, axes, split_axis=0, concat_axis=0, tiled=True)


def gather(block, axes):
    return exchange(jnp.broadcast_to(block[None], (lax.axis_size(axes), *block.shape)), axes)


def shards(clip_embed, clip_counts, pool_query, proj_weight, text_embed, pair_index, logit_scale):
    n_loc, n_clips, width = clip_embed.shape
    joint = proj_weight.shape[1]
    w_rows = proj_weight.shape[0]
    n_dp = lax.axis_size(DP)
    group_id = lax.axis_index(DP)
    lane_id = lax.axis_index(CLIP)
    yl_id = lax.axis_index("yl")
    near_id = lax.axis_index(NEAR)
    core_id = lax.axis_index("core")
    scale = logit_scale[0]

    unit_text, text_norm = unit_rows(text_embed.astype(F32))
    text_b = unit_text.astype(BF16)
    lane_texts = gather(text_b, DP).reshape(n_dp * n_loc, joint)

    query_f = pool_query.astype(F32)
    embed_f = clip_embed.astype(F32)
    scores = jnp.einsum("vce,e->vc", embed_f, query_f)
    usable = jnp.arange(n_clips, dtype=jnp.int32)[None, :] < clip_counts[:, None]
    masked = jnp.where(usable, scores, -1e30)
    raised = jnp.where(usable, jnp.exp(masked - jnp.max(masked, axis=1, keepdims=True)), 0.0)
    weights = raised / jnp.sum(raised, axis=1, keepdims=True)
    summary = jnp.einsum("vc,vce->ve", weights, embed_f)
    summary_b = summary.astype(BF16)

    w_pad = -(-w_rows // 16) * 16
    payload = jnp.concatenate(
        [
            lane_texts,
            jnp.pad(proj_weight, ((0, w_pad - w_rows), (0, 0))),
            summary_b[:, :joint],
            jnp.pad(summary_b[:, joint:], ((0, 0), (0, 2 * joint - width))),
        ],
        axis=0,
    )
    n_lane = lane_texts.shape[0]
    over_y = gather(payload, "yl")
    texts = over_y[:, :n_lane].reshape(-1, joint)
    over_x = gather(over_y[:, n_lane:], "x")
    other = lax.ppermute(over_x, "core", [(0, 1), (1, 0)])
    both = jnp.where(
        core_id == 0, jnp.stack([over_x, other], axis=1), jnp.stack([other, over_x], axis=1)
    )
    full_weight = both[..., :w_rows, :].transpose(2, 0, 1, 3, 4).reshape(width, joint)
    low = both[..., w_pad : w_pad + n_loc, :]
    high = both[..., w_pad + n_loc :, : width - joint]
    summaries = jnp.concatenate([low, high], axis=-1).reshape(-1, width)

    projected = jnp.dot(summaries, full_weight, preferred_element_type=F32)
    unit_video, video_norm = unit_rows(projected)
    video_b = unit_video.astype(BF16)
    expo = jnp.exp(
        scale * lax.dot_general(video_b, texts, (((1,), (1,)), ((), ())), preferred_element_type=F32)
    )
    row_part = jnp.sum(expo, axis=1)
    col_part = jnp.sum(expo, axis=0)
    row_total = jnp.sum(gather(row_part[None], NEAR), axis=(0, 1))
    col_total = jnp.sum(gather(col_part[None], DP), axis=(0, 1))

    n_yl = lax.axis_size("yl")
    n_x = lax.axis_size("x")
    group_rows = n_loc * n_yl * n_x * 2
    pairs = lax.dynamic_slice(pair_index, (group_id * group_rows,), (group_rows,))
    pairs = pairs.reshape(n_yl, n_x * 2, n_loc).transpose(1, 0, 2).reshape(-1)
    col_id = (
        (
            jnp.arange(n_dp, dtype=jnp.int32)[None, :, None] * (n_yl * n_x * 2)
            + jnp.arange(n_yl, dtype=jnp.int32)[:, None, None] * (n_x * 2)
            + near_id
        )
        * n_loc
        + jnp.arange(n_loc, dtype=jnp.int32)[None, None, :]
    ).reshape(-1)
    positive = (col_id[None, :] == pairs[:, None]).astype(F32)
    grad_logits = ((expo / row_total[:, None] + expo / col_total[None, :]) * 0.5 - positive).astype(BF16)

    video_part = scale * jnp.dot(grad_logits, texts, preferred_element_type=F32)
    n_near = lax.axis_size(NEAR)
    near_rows = group_rows // n_near
    received = exchange(video_part.astype(BF16).reshape(n_near, near_rows, joint), NEAR)
    d_video = jnp.sum(received.astype(F32), axis=0)
    unit_near = lax.dynamic_slice(unit_video, (near_id * near_rows, 0), (near_rows, joint))
    norm_near = lax.dynamic_slice(video_norm, (near_id * near_rows, 0), (near_rows, 1))
    d_near = (
        (d_video - unit_near * jnp.sum(unit_near * d_video, axis=1, keepdims=True)) / norm_near
    ).astype(BF16)
    d_projected = gather(d_near, NEAR).reshape(group_rows, joint)

    own_cols = lax.dynamic_slice(grad_logits, (0, yl_id * n_lane), (group_rows, n_lane))
    text_part = scale * lax.dot_general(
        own_cols, video_b, (((0,), (0,)), ((), ())), preferred_element_type=F32
    )
    summary_cols = lax.dynamic_slice(summaries, (0, lane_id * w_rows), (group_rows, w_rows))
    weight_part = lax.dot_general(
        summary_cols, d_projected, (((0,), (0,)), ((), ())), preferred_element_type=F32
    )
    piece = -(-w_rows // n_dp)
    weight_part = jnp.pad(weight_part, ((0, piece * n_dp - w_rows), (0, 0)))
    sums = exchange(
        jnp.concatenate(
            [
                text_part.astype(BF16).reshape(n_dp, n_loc, joint),
                weight_part.astype(BF16).reshape(n_dp, piece, joint),
            ],
            axis=1,
        ),
        DP,
    )
    sums = jnp.sum(sums.astype(F32), axis=0)
    d_text = sums[:n_loc]
    d_texts = (d_text - unit_text * jnp.sum(unit_text * d_text, axis=1, keepdims=True)) / text_norm
    d_weight = gather(sums[n_loc:], DP).reshape(piece * n_dp, joint)[:w_rows]

    d_own = lax.dynamic_slice(d_near, (yl_id * n_loc, 0), (n_loc, joint))
    d_summary = lax.dot_general(
        d_own, full_weight, (((1,), (1,)), ((), ())), preferred_element_type=F32
    )
    aligned = jnp.einsum("vce,ve->vc", embed_f, d_summary)
    baseline = jnp.sum(d_summary * summary, axis=1, keepdims=True)
    d_scores = weights * (aligned - baseline)
    d_clips = (
        weights[:, :, None] * d_summary[:, None, :] + d_scores[:, :, None] * query_f[None, None, :]
    ).astype(BF16)
    return (d_clips, d_weight, d_texts)


def solution(mesh):
    fine = Mesh(mesh.devices.reshape(2, 8, 4, 4, 2), DP + CLIP)
    everywhere = DP + CLIP
    return jax.shard_map(
        shards,
        mesh=fine,
        in_specs=(
            P(everywhere, None, None),
            P(everywhere),
            P(),
            P(CLIP, None),
            P(everywhere, None),
            P(),
            P(),
        ),
        out_specs=(P(everywhere, None, None), P(CLIP, None), P(everywhere, None)),
        check_vma=False,
    )
```

time: 830 us -> 205 us (0.25)
  waiting for transfers between devices: 520 us -> 59.1 us
  blocking collectives: 253 us -> 53.3 us
  starting transfers between devices: 12 us -> 50.7 us
  between operations: 14.6 us -> 1.71 us
    reduce_scatter x2 -> x0, waiting for transfers between devices: 333 us -> none  [the longest x1 190 us: shards(): lax.psum_scatter(logit_mult * lax.dot_general(block, row_embed, (((0,), (...]
    psum x1 -> x0, waiting for transfers between devices: 171 us -> none  [shards(): d_weight = lax.psum(weight_term, 'dp')]
    all_gather x3 -> x0, blocking collectives: 140 us -> none  [the longest x1 55 us: shards(): col_embed = lax.all_gather(text_b, 'dp', axis=0, tiled=True)]
    psum x2 -> x0, blocking collectives: 113 us -> none  [the longest x1 66.9 us: shards(): lane_sum = lax.psum(lane_part, 'clip')]
    all_to_all x0 -> x2, blocking collectives: none -> 53.3 us  [exchange(): return lax.all_to_all(blocks, axes, split_axis=0, concat_axis=0, tiled=True)]
    all_to_all x1 -> x7, waiting for transfers between devices: 7.67 us -> 58.6 us  [exchange(): return lax.all_to_all(blocks, axes, split_axis=0, concat_axis=0, tiled=True)]
    all_to_all x1 -> x7, starting transfers between devices: 11.9 us -> 45.5 us  [exchange(): return lax.all_to_all(blocks, axes, split_axis=0, concat_axis=0, tiled=True)]
    all_gather x1 -> x0, waiting for transfers between devices: 8.38 us -> none  [shards(): full_weight = lax.all_gather(proj_weight, 'clip', axis=0, tiled=True)]
  transfers between devices with their start and end apart: 5 -> 8, of which waited for: 5 -> 8; matrix products, arithmetic and copies ran while one was open for 2% -> 6% of each run, Pallas kernels for 0% -> 0%
where the time goes in v1:
time: 205 us; the launch traced here: 204 us
  waiting for transfers between devices  59.1 us (29%)
  blocking collectives  53.3 us (26%)
  starting transfers between devices  50.7 us (25%)
  other arithmetic  15.5 us (8%)
  local copies, waits for them, and re-layouts  15.4 us (8%)
  matrix products  8.01 us (4%)
    all_to_all x7, waiting for transfers between devices, exchange(): return lax.all_to_all(blocks, axes, split_axis=0, concat_axis=0, tiled=True)  58.6 us
    all_to_all x2, blocking collectives, exchange(): return lax.all_to_all(blocks, axes, split_axis=0, concat_axis=0, tiled=True)  53.3 us
    all_to_all x7, starting transfers between devices, exchange(): return lax.all_to_all(blocks, axes, split_axis=0, concat_axis=0, tiled=True)  45.5 us
    ppermute x1, starting transfers between devices, shards(): other = lax.ppermute(over_x, 'core', [(0, 1), (1, 0)])  5.17 us
  transfers between devices with their start and end apart: 8, of which 8 were waited for; matrix products, arithmetic and copies ran while one was open for 6% of the time, Pallas kernels for 0%

profile of v1, /device:TPU:1, one launch (start us, length us, event | category | flops | bytes accessed | tf_op | source)
XLA Modules:
  0.0 203.6 jit_solution(2520629185331055133)
XLA Ops:
  3.6 16.2 %all-to-all-start = ((bf16[16,8,768]{2,1,0:T(8,128)(2,1)}), bf16[16,8,768]{2,1,0:T(8,128)(2,1)S(1)}, u32[]{:S(2)}, u32[]{:S(2)}) async-start(bf16[16,8,768]{2,1,0:T(8,128)(2,1)} %broadcast_in_dim.23), calls=%async_computation | async-start | bytes 393216 | tf_op jit(solution)/shard_map/all_to_all | solution.py:20
  24.4 7.1 %all-to-all-done = bf16[16,8,768]{2,1,0:T(8,128)(2,1)S(1)} async-done(((bf16[16,8,768]{2,1,0:T(8,128)(2,1)}), bf16[16,8,768]{2,1,0:T(8,128)(2,1)S(1)}, u32[]{:S(2)}, u32[]{:S(2)}) %all-to-all-start) | async-done | bytes 196640 | tf_op jit(solution)/shard_map/all_to_all | solution.py:20
  32.4 31.1 %all_to_all.45 = bf16[4,192,768]{2,1,0:T(8,128)(2,1)S(1)} all-to-all(bf16[4,192,768]{2,1,0:T(8,128)(2,1)S(1)} %broadcast_in_dim.24), channel_id=1, replica_groups=mesh['yh'=2,'z'=8,'yl'=4,'x'=4,'core'=2] {'yl'}, dimensions={0} | all-to-all | bytes 2359296 | tf_op jit(solution)/shard_map/all_to_all | solution.py:20
  63.7 22.2 %all_to_all.46 = bf16[4,4,64,768]{3,2,1,0:T(8,128)(2,1)S(1)} all-to-all(bf16[4,4,64,768]{3,2,1,0:T(8,128)(2,1)S(1)} %broadcast_in_dim.25), channel_id=1, replica_groups=mesh['yh'=2,'z'=8,'yl'=4,'x'=4,'core'=2] {'x'}, dimensions={0} | all-to-all | bytes 3145728 | tf_op jit(solution)/shard_map/all_to_all | solution.py:20
  85.9 5.2 %collective-permute-start = (bf16[4,4,64,768]{3,2,1,0:T(8,128)(2,1)S(1)}, bf16[4,4,64,768]{3,2,1,0:T(8,128)(2,1)}, u32[]{:S(2)}, u32[]{:S(2)}) collective-permute-start(bf16[4,4,64,768]{3,2,1,0:T(8,128)(2,1)S(1)} %all_to_all.46), channel_id=1, source_target_pairs={{0,1},{1,0},{2,3},{3,2},{4,5},{5,4},{6,7},{7,6},{8,9},{9,8},{10,11... | collective-permute-start | bytes 4718600 | tf_op jit(solution)/shard_map/ppermute | solution.py:67
  94.2 3.4 %maximum_select_fusion = bf16[4,2,4,64,768]{4,3,2,1,0:T(8,128)(2,1)S(1)} fusion(bf16[4,1,4,64,768]{4,3,2,1,0:T(8,128)(2,1)} %bitcast.8, bf16[4,1,4,64,768]{4,3,2,1,0:T(8,128)(2,1)} %bitcast.45, pred[]{:T(512)S(6)} %eq.18), kind=kLoop, calls=%fused_computation | loop fusion | flops 4718592 | bytes 6291457 | tf_op jit(solution)/shard_map/jit(_where)/select_n | solution.py:68
  99.3 1.7 copy.14
  101.0 2.6 %reshape.145 = bf16[1408,768]{1,0:T(8,128)(2,1)S(1)} reshape(bf16[4,4,2,44,768]{4,3,2,1,0:T(8,128)(2,1)} %copy.14) | data formatting | bytes 4325376 | tf_op jit(solution)/shard_map/reshape | solution.py:71
  106.8 3.6 %all-to-all-start.3 = ((f32[8,1,256]{2,1,0:T(1,128)}), f32[8,1,256]{2,1,0:T(1,128)S(1)}, u32[]{:S(2)}, u32[]{:S(2)}) async-start(f32[8,1,256]{2,1,0:T(1,128)} %broadcast_in_dim.26), calls=%async_computation.3 | async-start | bytes 16384 | tf_op jit(solution)/shard_map/all_to_all | solution.py:20
  110.5 4.6 %all-to-all-done.3 = f32[8,1,256]{2,1,0:T(1,128)S(1)} async-done(((f32[8,1,256]{2,1,0:T(1,128)}), f32[8,1,256]{2,1,0:T(1,128)S(1)}, u32[]{:S(2)}, u32[]{:S(2)}) %all-to-all-start.3) | async-done | bytes 8224 | tf_op jit(solution)/shard_map/all_to_all | solution.py:20
  115.7 5.2 %all-to-all-start.4 = ((f32[16,1,512]{2,1,0:T(1,128)}), f32[16,1,512]{2,1,0:T(1,128)S(1)}, u32[]{:S(2)}, u32[]{:S(2)}) async-start(f32[16,1,512]{2,1,0:T(1,128)} %broadcast_in_dim.27), calls=%async_computation.4 | async-start | bytes 65536 | tf_op jit(solution)/shard_map/all_to_all | solution.py:20
  122.1 10.1 %all-to-all-done.4 = f32[16,1,512]{2,1,0:T(1,128)S(1)} async-done(((f32[16,1,512]{2,1,0:T(1,128)}), f32[16,1,512]{2,1,0:T(1,128)S(1)}, u32[]{:S(2)}, u32[]{:S(2)}) %all-to-all-start.4) | async-done | bytes 32800 | tf_op jit(solution)/shard_map/all_to_all | solution.py:20
  132.4 2.3 %fusion = bf16[256,768]{1,0:T(8,128)(2,1)} fusion(bf16[256,512]{1,0:T(8,128)(2,1)S(1)} %subtract_convert_fusion, bf16[512,768]{1,0:T(8,128)(2,1)} %bitcast.43, f32[]{:T(128)} %bitcast.40), kind=kOutput, calls=%fused_computation.3 | convolution fusion | flops 201719808 | bytes 1441796 | tf_op jit(solution)/shard_map/dot_general | solution.py:104
  134.8 5.5 %all-to-all-start.5 = ((bf16[8,32,768]{2,1,0:T(8,128)(2,1)}), bf16[8,32,768]{2,1,0:T(8,128)(2,1)S(1)}, u32[]{:S(2)}, u32[]{:S(2)}) async-start(bf16[8,32,768]{2,1,0:T(8,128)(2,1)} %bitcast.13), calls=%async_computation.5 | async-start | bytes 786432 | tf_op jit(solution)/shard_map/all_to_all | solution.py:20
  141.0 1.4 fusion.3
  142.5 5.9 %all-to-all-done.5 = bf16[8,32,768]{2,1,0:T(8,128)(2,1)S(1)} async-done(((bf16[8,32,768]{2,1,0:T(8,128)(2,1)}), bf16[8,32,768]{2,1,0:T(8,128)(2,1)S(1)}, u32[]{:S(2)}, u32[]{:S(2)}) %all-to-all-start.5) | async-done | bytes 393248 | tf_op jit(solution)/shard_map/all_to_all | solution.py:20
  148.4 1.0 multiply_reduce_fusion.1
  151.2 4.2 %all-to-all-start.6 = ((bf16[8,32,768]{2,1,0:T(8,128)(2,1)}), bf16[8,32,768]{2,1,0:T(8,128)(2,1)S(1)}, u32[]{:S(2)}, u32[]{:S(2)}) async-start(bf16[8,32,768]{2,1,0:T(8,128)(2,1)} %broadcast_in_dim.28), calls=%async_computation.6 | async-start | bytes 786432 | tf_op jit(solution)/shard_map/all_to_all | solution.py:20
  156.5 7.0 %all-to-all-done.6 = bf16[8,32,768]{2,1,0:T(8,128)(2,1)S(1)} async-done(((bf16[8,32,768]{2,1,0:T(8,128)(2,1)}), bf16[8,32,768]{2,1,0:T(8,128)(2,1)S(1)}, u32[]{:S(2)}, u32[]{:S(2)}) %all-to-all-start.6) | async-done | bytes 393248 | tf_op jit(solution)/shard_map/all_to_all | solution.py:20
  163.5 1.2 convolution_convert_fusion
  165.6 3.6 %all-to-all-start.7 = ((bf16[16,11,768]{2,1,0:T(8,128)(2,1)}), bf16[16,11,768]{2,1,0:T(8,128)(2,1)S(1)}, u32[]{:S(2)}, u32[]{:S(2)}) async-start(bf16[16,11,768]{2,1,0:T(8,128)(2,1)} %pad_maximum_fusion.1), calls=%async_computation.7 | async-start | bytes 786432 | tf_op jit(solution)/shard_map/all_to_all | solution.py:20
  170.2 13.3 %all-to-all-done.7 = bf16[16,11,768]{2,1,0:T(8,128)(2,1)S(1)} async-done(((bf16[16,11,768]{2,1,0:T(8,128)(2,1)}), bf16[16,11,768]{2,1,0:T(8,128)(2,1)S(1)}, u32[]{:S(2)}, u32[]{:S(2)}) %all-to-all-start.7) | async-done | bytes 270368 | tf_op jit(solution)/shard_map/all_to_all | solution.py:20
  184.2 7.1 %all-to-all-start.8 = ((f32[16,3,768]{2,1,0:T(4,128)}), f32[16,3,768]{2,1,0:T(4,128)S(1)}, u32[]{:S(2)}, u32[]{:S(2)}) async-start(f32[16,3,768]{2,1,0:T(4,128)} %broadcast_in_dim.29), calls=%async_computation.8 | async-start | bytes 393216 | tf_op jit(solution)/shard_map/all_to_all | solution.py:20
  192.3 10.6 %all-to-all-done.8 = f32[16,3,768]{2,1,0:T(4,128)S(1)} async-done(((f32[16,3,768]{2,1,0:T(4,128)}), f32[16,3,768]{2,1,0:T(4,128)S(1)}, u32[]{:S(2)}, u32[]{:S(2)}) %all-to-all-start.8) | async-done | bytes 147488 | tf_op jit(solution)/shard_map/all_to_all | solution.py:20
  (104 shorter events, 25.8 us)
Async XLA Ops:
  0.6 19.9 %copy-start = (bf16[8,16,1408]{2,1,0:T(8,128)(2,1)S(1)}, bf16[8,16,1408]{2,1,0:T(8,128)(2,1)}, u32[]{:S(2)}) copy-start(bf16[8,16,1408]{2,1,0:T(8,128)(2,1)} %param.7) | copy-start | bytes 1081348
  3.6 27.8 %all-to-all-start = ((bf16[16,8,768]{2,1,0:T(8,128)(2,1)}), bf16[16,8,768]{2,1,0:T(8,128)(2,1)S(1)}, u32[]{:S(2)}, u32[]{:S(2)}) async-start(bf16[16,8,768]{2,1,0:T(8,128)(2,1)} %broadcast_in_dim.23), calls=%async_computation | async-start | bytes 393216 | tf_op jit(solution)/shard_map/all_to_all | solution.py:20
  85.9 8.3 %copy-start.4 = (bf16[4,4,64,768]{3,2,1,0:T(8,128)(2,1)}, bf16[4,4,64,768]{3,2,1,0:T(8,128)(2,1)S(1)}, u32[]{:S(2)}) copy-start(bf16[4,4,64,768]{3,2,1,0:T(8,128)(2,1)S(1)} %all_to_all.46) | copy-start | bytes 4718596
  85.9 8.3 %collective-permute-start = (bf16[4,4,64,768]{3,2,1,0:T(8,128)(2,1)S(1)}, bf16[4,4,64,768]{3,2,1,0:T(8,128)(2,1)}, u32[]{:S(2)}, u32[]{:S(2)}) collective-permute-start(bf16[4,4,64,768]{3,2,1,0:T(8,128)(2,1)S(1)} %all_to_all.46), channel_id=1, source_target_pairs={{0,1},{1,0},{2,3},{3,2},{4,5},{5,4},{6,7},{7,6},{8,9},{9,8},{10,11... | collective-permute-start | bytes 4718600 | tf_op jit(solution)/shard_map/ppermute | solution.py:67
  97.6 1.7 copy-start.1
  101.0 2.6 %slice-start = ((bf16[4,2,4,64,768]{4,3,2,1,0:T(8,128)(2,1)}), bf16[4,2,4,8,768]{4,3,2,1,0:T(8,128)(2,1)S(1)}, s32[]{:S(2)}) async-start(bf16[4,2,4,64,768]{4,3,2,1,0:T(8,128)(2,1)} %copy-done.1), calls=%async_computation.9 | async-start | bytes 786432 | tf_op jit(solution)/shard_map/slice | solution.py:72
  101.0 2.7 %copy-start.6 = (bf16[4,2,4,8,640]{4,3,2,1,0:T(8,128)(2,1)S(1)}, bf16[4,2,4,8,640]{4,3,2,1,0:T(8,128)(2,1)}, u32[]{:S(2)}) copy-start(bf16[4,2,4,8,640]{4,3,2,1,0:T(8,128)(2,1)} %slice.44) | copy-start | bytes 983044
  103.7 1.9 copy-start.3
  104.6 5.8 %copy-start.20 = (s32[16]{0:T(128)S(1)}, s32[16]{0:T(128)}, u32[]{:S(2)}) copy-start(s32[16]{0:T(128)} %iota_multiply_fusion.1) | copy-start | bytes 196
  104.6 5.8 %copy-start.21 = (s32[4]{0:T(128)S(1)}, s32[4]{0:T(128)}, u32[]{:S(2)}) copy-start(s32[4]{0:T(128)} %iota_multiply_fusion) | copy-start | bytes 52
  106.8 8.2 %all-to-all-start.3 = ((f32[8,1,256]{2,1,0:T(1,128)}), f32[8,1,256]{2,1,0:T(1,128)S(1)}, u32[]{:S(2)}, u32[]{:S(2)}) async-start(f32[8,1,256]{2,1,0:T(1,128)} %broadcast_in_dim.26), calls=%async_computation.3 | async-start | bytes 16384 | tf_op jit(solution)/shard_map/all_to_all | solution.py:20
  115.7 16.5 %all-to-all-start.4 = ((f32[16,1,512]{2,1,0:T(1,128)}), f32[16,1,512]{2,1,0:T(1,128)S(1)}, u32[]{:S(2)}, u32[]{:S(2)}) async-start(f32[16,1,512]{2,1,0:T(1,128)} %broadcast_in_dim.27), calls=%async_computation.4 | async-start | bytes 65536 | tf_op jit(solution)/shard_map/all_to_all | solution.py:20
  122.1 18.9 %copy-start.19 = (f32[256]{0:T(256)S(1)}, f32[256]{0:T(256)}, u32[]{:S(2)}) copy-start(f32[256]{0:T(256)} %copy-done.18) | copy-start | bytes 3076
  132.4 2.4 %copy-start.5 = (bf16[256,512]{1,0:T(8,128)(2,1)}, bf16[256,512]{1,0:T(8,128)(2,1)S(1)}, u32[]{:S(2)}) copy-start(bf16[256,512]{1,0:T(8,128)(2,1)S(1)} %subtract_convert_fusion) | copy-start | bytes 786436
  134.8 13.6 %all-to-all-start.5 = ((bf16[8,32,768]{2,1,0:T(8,128)(2,1)}), bf16[8,32,768]{2,1,0:T(8,128)(2,1)S(1)}, u32[]{:S(2)}, u32[]{:S(2)}) async-start(bf16[8,32,768]{2,1,0:T(8,128)(2,1)} %bitcast.13), calls=%async_computation.5 | async-start | bytes 786432 | tf_op jit(solution)/shard_map/all_to_all | solution.py:20
  151.2 12.3 %all-to-all-start.6 = ((bf16[8,32,768]{2,1,0:T(8,128)(2,1)}), bf16[8,32,768]{2,1,0:T(8,128)(2,1)S(1)}, u32[]{:S(2)}, u32[]{:S(2)}) async-start(bf16[8,32,768]{2,1,0:T(8,128)(2,1)} %broadcast_in_dim.28), calls=%async_computation.6 | async-start | bytes 786432 | tf_op jit(solution)/shard_map/all_to_all | solution.py:20
  155.4 13.7 %copy-start.11 = (s32[8]{0:T(128)S(1)}, s32[8]{0:T(128)}, u32[]{:S(2)}) copy-start(s32[8]{0:T(128)} %param.8) | copy-start | bytes 100
  155.5 13.7 %copy-start.13 = (f32[8]{0:T(128)S(1)}, f32[8]{0:T(128)}, u32[]{:S(2)}) copy-start(f32[8]{0:T(128)} %copy-done.12) | copy-start | bytes 100
  155.5 13.7 %copy-start.17 = (f32[8]{0:T(128)S(1)}, f32[8]{0:T(128)}, u32[]{:S(2)}) copy-start(f32[8]{0:T(128)} %copy-done.16) | copy-start | bytes 100
  155.5 13.8 %copy-start.10 = (f32[8,16]{1,0:T(8,128)S(1)}, f32[8,16]{1,0:T(8,128)}, u32[]{:S(2)}) copy-start(f32[8,16]{1,0:T(8,128)} %copy-done.9) | copy-start | bytes 1540
  156.3 35.1 %copy-start.8 = (bf16[8,768]{1,0:T(8,128)(2,1)S(1)}, bf16[8,768]{1,0:T(8,128)(2,1)}, u32[]{:S(2)}) copy-start(bf16[8,768]{1,0:T(8,128)(2,1)} %param.11) | copy-start | bytes 36868
  156.3 35.1 %copy-start.15 = (f32[8]{0:T(128)S(1)}, f32[8]{0:T(128)}, u32[]{:S(2)}) copy-start(f32[8]{0:T(128)} %copy-done.14) | copy-start | bytes 100
  165.6 17.9 %all-to-all-start.7 = ((bf16[16,11,768]{2,1,0:T(8,128)(2,1)}), bf16[16,11,768]{2,1,0:T(8,128)(2,1)S(1)}, u32[]{:S(2)}, u32[]{:S(2)}) async-start(bf16[16,11,768]{2,1,0:T(8,128)(2,1)} %pad_maximum_fusion.1), calls=%async_computation.7 | async-start | bytes 786432 | tf_op jit(solution)/shard_map/all_to_all | solution.py:20
  184.2 18.7 %all-to-all-start.8 = ((f32[16,3,768]{2,1,0:T(4,128)}), f32[16,3,768]{2,1,0:T(4,128)S(1)}, u32[]{:S(2)}, u32[]{:S(2)}) async-start(f32[16,3,768]{2,1,0:T(4,128)} %broadcast_in_dim.29), calls=%async_computation.8 | async-start | bytes 393216 | tf_op jit(solution)/shard_map/all_to_all | solution.py:20
  (7 other events, 7.0 us)

commit v2 on v1

v2 whole, which is shorter than its diff:
```python
import functools

import jax
import jax.numpy as jnp
from jax import lax
from jax.experimental import pallas as pl
from jax.experimental.pallas import tpu as pltpu
from jax.sharding import Mesh, PartitionSpec as P

EPS = 1e-06
F32 = jnp.float32
BF16 = jnp.bfloat16
DP = ("yh", "z")
CLIP = ("yl", "x", "core")
PLANE = ("yl", "x")
SWAP = [(0, 1), (1, 0)]


def unit_rows(values):
    norm_value = jnp.sqrt(jnp.sum(values * values, axis=1, keepdims=True) + EPS)
    return (values / norm_value, norm_value)


def exchange(blocks, axes):
    return lax.all_to_all(blocks, axes, split_axis=0, concat_axis=0, tiled=True)


def dot(a, b, contract):
    return lax.dot_general(a, b, (contract, ((), ())), preferred_element_type=F32)


def local(body, outs, n_scalars, n_args, scratch=(), flops=1e6, moved=1e6):
    vmem = pl.BlockSpec(memory_space=pltpu.VMEM)
    smem = pl.BlockSpec(memory_space=pltpu.SMEM)
    return pl.pallas_call(
        body,
        out_shape=tuple(jax.ShapeDtypeStruct(shape, dtype) for shape, dtype in outs),
        in_specs=[smem] * n_scalars + [vmem] * n_args,
        out_specs=tuple(vmem for _ in outs),
        scratch_shapes=list(scratch),
        compiler_params=pltpu.CompilerParams(vmem_limit_bytes=40 * 1024 * 1024),
        cost_estimate=pl.CostEstimate(flops=int(flops), bytes_accessed=int(moved), transcendentals=0),
    )


def text_body(text_ref, out_ref):
    unit, _ = unit_rows(text_ref[...].astype(F32))
    out_ref[...] = jnp.broadcast_to(unit[None], out_ref.shape).astype(BF16)


def column(row):
    return jnp.broadcast_to(row, (128, row.shape[1])).T[:, :1]


def logits_body(
    n_loc, w_rows, pos_ref, scale_ref, own_ref, other_ref, text_own_ref, text_other_ref,
    weight_ref, summary_ref, video_ref, unit_ref, norm_ref, expo_ref, rows_ref, cols_ref,
    weight_f, summary_f, unit_f, norm_f,
):
    n_x, n_yl, _, joint = own_ref.shape
    width = weight_ref.shape[0]
    half = n_x * n_yl * n_loc
    w_pad = -(-w_rows // 16) * 16
    first = pos_ref[0] == 0
    for x in range(n_x):
        for yl in range(n_yl):
            own = own_ref[x, yl].astype(F32)
            other = other_ref[x, yl].astype(F32)
            pair = (jnp.where(first, own, other), jnp.where(first, other, own))
            for core in range(2):
                at = ((yl * n_x + x) * 2 + core) * w_rows
                weight_f[at : at + w_rows, :] = pair[core][:w_rows]
                row = core * half + (yl * n_x + x) * n_loc
                summary_f[row : row + n_loc, :joint] = pair[core][w_pad : w_pad + n_loc]
                summary_f[row : row + n_loc, joint:] = pair[core][w_pad + n_loc :, : width - joint]
    weight_b = weight_f[...].astype(BF16)
    summary_b = summary_f[...].astype(BF16)
    weight_ref[...] = weight_b
    summary_ref[...] = summary_b
    unit, norm = unit_rows(dot(summary_b, weight_b, ((1,), (0,))))
    video_b = unit.astype(BF16)
    video_ref[...] = video_b
    unit_f[...] = unit
    norm_f[...] = jnp.broadcast_to(norm, norm_f.shape)
    mine = pl.ds(pl.multiple_of(pos_ref[1] * n_loc, n_loc), n_loc)
    unit_ref[...] = unit_f[mine, :]
    norm_ref[...] = norm_f[mine, :]
    n_lane = text_own_ref.shape[0]
    scale = scale_ref[0]
    expo_ref[:, :n_lane] = jnp.exp(scale * dot(video_b, text_own_ref[...], ((1,), (1,))))
    expo_ref[:, n_lane:] = jnp.exp(scale * dot(video_b, text_other_ref[...], ((1,), (1,))))
    expo = expo_ref[...]
    row_part = jnp.broadcast_to(jnp.sum(expo, axis=1, keepdims=True), (2 * half, 128)).T[:1]
    col_part = jnp.sum(expo, axis=0, keepdims=True)
    rows_ref[...] = jnp.broadcast_to(row_part[None], rows_ref.shape)
    cols_ref[...] = jnp.broadcast_to(col_part[None], cols_ref.shape)


def grad_body(
    n_loc, n_clip, pos_ref, scale_ref, expo_ref, rows_ref, cols_ref, pairs_ref, text_own_ref,
    text_other_ref, grad_ref, part_ref,
):
    n_lane = text_own_ref.shape[0]
    rows = jnp.sum(rows_ref[...], axis=0)
    cols = jnp.sum(cols_ref[...], axis=0)
    core = pos_ref[0]
    at = lax.broadcasted_iota(jnp.int32, (1, 2 * n_lane), 1)
    lane = jnp.where(at < n_lane, pos_ref[2], pos_ref[3])
    slot = jnp.where(at < n_lane, at, at - n_lane)
    col_id = ((slot // n_loc) * n_clip + lane) * n_loc + slot % n_loc
    positive = jnp.where(pairs_ref[...] == col_id, 1.0, 0.0)
    expo = expo_ref[...]
    grad = (expo / column(rows) + expo / cols) * 0.5 - positive
    grad_ref[...] = grad.astype(BF16)
    half = expo.shape[0] // 2
    mine = grad_ref[pl.ds(pl.multiple_of(core * half, half), half), :]
    part = dot(mine[:, :n_lane], text_own_ref[...], ((1,), (0,)))
    part = part + dot(mine[:, n_lane:], text_other_ref[...], ((1,), (0,)))
    part_ref[...] = (scale_ref[0] * part).astype(BF16)


def text_part_body(scale_ref, grad_ref, video_ref, out_ref):
    n_lane = out_ref.shape[0]
    part = dot(grad_ref[:, :n_lane], video_ref[...], ((0,), (0,)))
    out_ref[...] = (scale_ref[0] * part).astype(BF16)


def projected_body(part_ref, unit_ref, norm_ref, out_ref, own_ref):
    d_video = jnp.sum(part_ref[...].astype(F32), axis=0)
    unit = unit_ref[...]
    norm = norm_ref[:, :1]
    value = (d_video - unit * jnp.sum(unit * d_video, axis=1, keepdims=True)) / norm
    out_ref[...] = jnp.broadcast_to(value[None], out_ref.shape).astype(BF16)
    own_ref[...] = value.astype(BF16)


def weight_body(pos_ref, cols_ref, own_ref, other_ref, text_ref, send_ref, part_ref):
    half = own_ref.shape[0]
    core = pos_ref[0]
    own_cols = cols_ref[pl.ds(pl.multiple_of(core * half, half), half), :]
    other_cols = cols_ref[pl.ds(pl.multiple_of((1 - core) * half, half), half), :]
    part = dot(own_cols, own_ref[...], ((0,), (0,))) + dot(other_cols, other_ref[...], ((0,), (0,)))
    part_ref[...] = part
    n_text = text_ref.shape[0] // 2
    away = (1 - pos_ref[4]) * n_text
    send_ref[:n_text, :] = text_ref[pl.ds(pl.multiple_of(away, n_text), n_text), :]
    send_ref[n_text:, :] = part.astype(BF16)


def near_sum_body(pos_ref, part_ref, text_ref, got_ref, out_ref):
    n_text = text_ref.shape[0] // 2
    here = pl.ds(pl.multiple_of(pos_ref[4] * n_text, n_text), n_text)
    got = got_ref[...].astype(F32)
    text = text_ref[here, :].astype(F32) + got[:n_text]
    weight = part_ref[...] + got[n_text:]
    n_z = out_ref.shape[0]
    n_loc = n_text // n_z
    for z in range(n_z):
        rows = jnp.concatenate([text[z * n_loc : (z + 1) * n_loc], weight], axis=0)
        out_ref[z] = rows.astype(BF16)


def last_body(got_ref, text_ref, d_weight_ref, d_texts_ref):
    total = jnp.sum(got_ref[...].astype(F32), axis=0)
    n_loc = text_ref.shape[0]
    unit, norm = unit_rows(text_ref[...].astype(F32))
    d_text = total[:n_loc]
    d_texts_ref[...] = (d_text - unit * jnp.sum(unit * d_text, axis=1, keepdims=True)) / norm
    d_weight_ref[...] = total[n_loc : n_loc + d_weight_ref.shape[0]]


def shards(clip_embed, clip_counts, pool_query, proj_weight, text_embed, pair_index, logit_scale):
    n_loc, n_clips, width = clip_embed.shape
    w_rows, joint = proj_weight.shape
    n_dp, n_yh, n_z = lax.axis_size(DP), lax.axis_size("yh"), lax.axis_size("z")
    n_yl, n_x, n_clip = lax.axis_size("yl"), lax.axis_size("x"), lax.axis_size(CLIP)
    n_plane = n_yl * n_x
    group_rows = n_loc * n_clip
    half = group_rows // 2
    n_lane = n_dp * n_loc
    core_id = lax.axis_index("core")
    plane_id = lax.axis_index(PLANE)
    lane_id = lax.axis_index(CLIP)
    group_id = lax.axis_index(DP)
    pos = jnp.stack(
        [
            core_id,
            core_id * n_plane + plane_id,
            lane_id,
            plane_id * 2 + (1 - core_id),
            lax.axis_index("yh"),
        ]
    ).astype(jnp.int32)

    (text_send,) = local(text_body, [((n_dp, n_loc, joint), BF16)], 0, 1)(text_embed)
    text_own = exchange(text_send, DP).reshape(n_lane, joint)
    text_other = lax.ppermute(text_own, "core", SWAP)

    query_f = pool_query.astype(F32)
    embed_f = clip_embed.astype(F32)
    scores = jnp.einsum("vce,e->vc", embed_f, query_f)
    usable = jnp.arange(n_clips, dtype=jnp.int32)[None, :] < clip_counts[:, None]
    masked = jnp.where(usable, scores, -1e30)
    raised = jnp.where(usable, jnp.exp(masked - jnp.max(masked, axis=1, keepdims=True)), 0.0)
    weights = raised / jnp.sum(raised, axis=1, keepdims=True)
    summary = jnp.einsum("vc,vce->ve", weights, embed_f)
    summary_b = summary.astype(BF16)

    w_pad = -(-w_rows // 16) * 16
    payload = jnp.concatenate(
        [
            jnp.pad(proj_weight, ((0, w_pad - w_rows), (0, 0))),
            summary_b[:, :joint],
            jnp.pad(summary_b[:, joint:], ((0, 0), (0, 2 * joint - width))),
        ],
        axis=0,
    )
    over_y = exchange(jnp.broadcast_to(payload[None], (n_yl, *payload.shape)), "yl")
    over_x = exchange(jnp.broadcast_to(over_y[None], (n_x, *over_y.shape)), "x")
    over_x_other = lax.ppermute(over_x, "core", SWAP)

    full_weight, summaries, video_b, unit_own, norm_own, expo, row_send, col_send = local(
        functools.partial(logits_body, n_loc, w_rows),
        [
            ((width, joint), BF16),
            ((group_rows, width), BF16),
            ((group_rows, joint), BF16),
            ((n_loc, joint), F32),
            ((n_loc, 128), F32),
            ((group_rows, 2 * n_lane), F32),
            ((n_plane, 1, group_rows), F32),
            ((n_dp, 1, 2 * n_lane), F32),
        ],
        2,
        4,
        scratch=[
            pltpu.VMEM((width, joint), F32),
            pltpu.VMEM((group_rows, width), F32),
            pltpu.VMEM((group_rows, joint), F32),
            pltpu.VMEM((group_rows, 128), F32),
        ],
        flops=7e8,
        moved=8e6,
    )(pos, logit_scale, over_x, over_x_other, text_own, text_other)
    rows = exchange(row_send, PLANE)
    cols = exchange(col_send, DP)

    pairs = lax.dynamic_slice(pair_index, (group_id * group_rows,), (group_rows,))
    pairs = pairs.reshape(n_plane, 2, n_loc).transpose(1, 0, 2).reshape(group_rows, 1)
    grad_logits, video_part = local(
        functools.partial(grad_body, n_loc, n_clip),
        [((group_rows, 2 * n_lane), BF16), ((half, joint), BF16)],
        2,
        6,
        flops=1e8,
    )(pos, logit_scale, expo, rows, cols, pairs, text_own, text_other)

    got_video = exchange(video_part.reshape(n_plane, n_loc, joint), PLANE)
    (text_part,) = local(text_part_body, [((n_lane, joint), BF16)], 1, 2, flops=1e8)(
        logit_scale, grad_logits, video_b
    )
    d_send, d_own = local(
        projected_body, [((n_plane, n_loc, joint), BF16), ((n_loc, joint), BF16)], 0, 3
    )(got_video, unit_own, norm_own)
    d_half = exchange(d_send, PLANE).reshape(half, joint)
    d_half_other = lax.ppermute(d_half, "core", SWAP)

    d_summary = dot(d_own, full_weight, ((1,), (1,)))
    aligned = jnp.einsum("vce,ve->vc", embed_f, d_summary)
    baseline = jnp.sum(d_summary * summary, axis=1, keepdims=True)
    d_scores = weights * (aligned - baseline)
    d_clips = (
        weights[:, :, None] * d_summary[:, None, :] + d_scores[:, :, None] * query_f[None, None, :]
    ).astype(BF16)

    summary_cols = lax.dynamic_slice(summaries, (0, lane_id * w_rows), (group_rows, w_rows))
    summary_cols = jnp.pad(summary_cols, ((0, 0), (0, w_pad - w_rows)))
    n_text = n_z * n_loc
    send, weight_part = local(
        weight_body, [((n_text + w_pad, joint), BF16), ((w_pad, joint), F32)], 1, 4, flops=3e7
    )(pos, summary_cols, d_half, d_half_other, text_part)
    got = lax.ppermute(send, "yh", SWAP)
    (sums,) = local(near_sum_body, [((n_z, n_loc + w_pad, joint), BF16)], 1, 3)(
        pos, weight_part, text_part, got
    )
    d_weight, d_texts = local(
        last_body, [((w_rows, joint), F32), ((n_loc, joint), F32)], 0, 2
    )(exchange(sums, "z"), text_embed)
    return (d_clips, d_weight, d_texts)


def solution(mesh):
    fine = Mesh(mesh.devices.reshape(2, 8, 4, 4, 2), DP + CLIP)
    everywhere = DP + CLIP
    return jax.shard_map(
        shards,
        mesh=fine,
        in_specs=(
            P(everywhere, None, None),
            P(everywhere),
            P(),
            P(CLIP, None),
            P(everywhere, None),
            P(),
            P(),
        ),
        out_specs=(P(everywhere, None, None), P(CLIP, None), P(everywhere, None)),
        check_vma=False,
    )
```

time: 205 us -> 187 us (0.912)
  blocking collectives: 53.3 us -> 95.1 us
  starting transfers between devices: 50.7 us -> 27 us
  waiting for transfers between devices: 59.1 us -> 41.1 us
  other arithmetic: 15.5 us -> 4.34 us
  local copies, waits for them, and re-layouts: 15.4 us -> 6.35 us
  Pallas kernels: 0 us -> 8.58 us
  matrix products: 8.01 us -> 1.73 us
    all_to_all x2 -> x6, blocking collectives: 53.3 us -> 95.1 us  [exchange(): return lax.all_to_all(blocks, axes, split_axis=0, concat_axis=0, tiled=True)]
    all_to_all x7 -> x2, starting transfers between devices: 45.5 us -> 8.44 us  [exchange(): return lax.all_to_all(blocks, axes, split_axis=0, concat_axis=0, tiled=True)]
    all_to_all x7 -> x2, waiting for transfers between devices: 58.6 us -> 29.6 us  [exchange(): return lax.all_to_all(blocks, axes, split_axis=0, concat_axis=0, tiled=True)]
    ppermute x1 -> x4, starting transfers between devices: 5.17 us -> 18.5 us  [the longest x1 7.66 us: shards(): d_half_other = lax.ppermute(d_half, 'core', SWAP)]
    ppermute x1 -> x4, waiting for transfers between devices: 0.51 us -> 11.5 us  [the longest x1 11.2 us: shards(): got = lax.ppermute(send, 'yh', SWAP)]
    pallas_call x0 -> x8, Pallas kernels: none -> 8.58 us  [the longest x1 4.03 us: shards(): local(functools.partial(logits_body, n_loc, w_rows), [((width, joint), BF...]
    dot_general x6 -> x1, matrix products: 7.09 us -> 0.79 us  [dot(): lax.dot_general(a, b, (contract, ((), ())), preferred_element_type=F32)]
    broadcast_in_dim x7 -> x2, local copies, waits for them, and re-layouts: 3.64 us -> 0.17 us  [the longest x1 0.15 us: shards(): over_x = exchange(jnp.broadcast_to(over_y[None], (n_x, *over_y.shape)), 'x')]
  transfers between devices with their start and end apart: 8 -> 6, of which waited for: 8 -> 4; matrix products, arithmetic and copies ran while one was open for 6% -> 2% of each run, Pallas kernels for 0% -> 0%
where the time goes in v2:
time: 187 us; the launch traced here: 186 us
  blocking collectives  95.1 us (51%)
  waiting for transfers between devices  41.1 us (22%)
  starting transfers between devices  27 us (14%)
  Pallas kernels  8.58 us (5%)
  local copies, waits for them, and re-layouts  6.35 us (3%)
  other arithmetic  4.34 us (2%)
    all_to_all x6, blocking collectives, exchange(): return lax.all_to_all(blocks, axes, split_axis=0, concat_axis=0, tiled=True)  95.1 us
    all_to_all x2, waiting for transfers between devices, exchange(): return lax.all_to_all(blocks, axes, split_axis=0, concat_axis=0, tiled=True)  29.6 us
    ppermute x1, waiting for transfers between devices, shards(): got = lax.ppermute(send, 'yh', SWAP)  11.2 us
    all_to_all x2, starting transfers between devices, exchange(): return lax.all_to_all(blocks, axes, split_axis=0, concat_axis=0, tiled=True)  8.44 us
    ppermute x1, starting transfers between devices, shards(): d_half_other = lax.ppermute(d_half, 'core', SWAP)  7.66 us
    ppermute x1, starting transfers between devices, shards(): over_x_other = lax.ppermute(over_x, 'core', SWAP)  5.2 us
    unnamed x19, local copies, waits for them, and re-layouts  4.11 us
    pallas_call x1, Pallas kernels, shards(): local(functools.partial(logits_body, n_loc, w_rows), [((width, joint), BF...  4.03 us
  transfers between devices with their start and end apart: 6, of which 4 were waited for; matrix products, arithmetic and copies ran while one was open for 2% of the time, Pallas kernels for 0%

profile of v2, /device:TPU:1, one launch (start us, length us, event | category | flops | bytes accessed | tf_op | source)
XLA Modules:
  0.0 185.8 jit_solution(11216330362518823775)
XLA Ops:
  2.2 0.9 fusion.8
  4.9 0.9 fusion.2
  5.8 13.0 %all_to_all.40 = bf16[4,64,768]{2,1,0:T(8,128)(2,1)S(1)} all-to-all(bf16[4,64,768]{2,1,0:T(8,128)(2,1)S(1)} %broadcast_in_dim.13), channel_id=1, replica_groups=mesh['yh'=2,'z'=8,'yl'=4,'x'=4,'core'=2] {'yl'}, dimensions={0} | all-to-all | bytes 786432 | tf_op jit(solution)/shard_map/all_to_all | solution.py:25
  18.9 25.3 %all_to_all.41.own_ref = bf16[4,4,64,768]{3,2,1,0:T(8,128)(2,1)S(1)} all-to-all(bf16[4,4,64,768]{3,2,1,0:T(8,128)(2,1)S(1)} %broadcast_in_dim.14), channel_id=1, replica_groups=mesh['yh'=2,'z'=8,'yl'=4,'x'=4,'core'=2] {'x'}, dimensions={0} | all-to-all | bytes 3145728 | tf_op jit(solution)/shard_map/all_to_all | solution.py:25
  44.2 5.2 %collective-permute-start = (bf16[4,4,64,768]{3,2,1,0:T(8,128)(2,1)S(1)}, bf16[4,4,64,768]{3,2,1,0:T(8,128)(2,1)}, u32[]{:S(2)}, u32[]{:S(2)}) collective-permute-start(bf16[4,4,64,768]{3,2,1,0:T(8,128)(2,1)S(1)} %all_to_all.41.own_ref), channel_id=1, source_target_pairs={{0,1},{1,0},{2,3},{3,2},{4,5},{5,4},{6,7},{7,6},{8,9},{9,8},{10,11... | collective-permute-start | bytes 4718600 | tf_op jit(solution)/shard_map/ppermute | solution.py:220
  49.5 25.0 %all_to_all.42 = bf16[16,8,768]{2,1,0:T(8,128)(2,1)S(1)} all-to-all(bf16[16,8,768]{2,1,0:T(8,128)(2,1)S(1)} %shard_map.94), channel_id=1, replica_groups=mesh['yh'=2,'z'=8,'yl'=4,'x'=4,'core'=2] {'yh','z'}, dimensions={0} | all-to-all | bytes 393216 | tf_op jit(solution)/shard_map/all_to_all | solution.py:25
  74.5 3.5 %collective-permute-start.1 = (bf16[128,768]{1,0:T(8,128)(2,1)S(1)}, bf16[128,768]{1,0:T(8,128)(2,1)S(1)}, u32[]{:S(2)}, u32[]{:S(2)}) collective-permute-start(bf16[128,768]{1,0:T(8,128)(2,1)S(1)} %bitcast.30), channel_id=1, source_target_pairs={{0,1},{1,0},{2,3},{3,2},{4,5},{5,4},{6,7},{7,6},{8,9},{9,8},{10,11... | collective-permute-start | bytes 589832 | tf_op jit(solution)/shard_map/ppermute | solution.py:197
  79.1 4.0 %shard_map.95 = (bf16[1408,768]{1,0:T(8,128)(2,1)S(1)}, bf16[256,1408]{1,0:T(8,128)(2,1)S(1)}, bf16[256,768]{1,0:T(8,128)(2,1)S(1)}, f32[8,768]{1,0:T(8,128)S(1)...) custom-call(s32[5]{0:T(128)S(1)} %stack.23.pos_ref, ...), custom_call_target="tpu_custom_call" | custom-call | flops 700000000 | bytes 8000000 | tf_op jit(solution)/shard_map/pallas_call | solution.py:222
  83.1 1.4 copy-done.1
  85.2 10.1 %all_to_all.43.rows_ref = f32[16,1,256]{2,1,0:T(1,128)S(1)} all-to-all(f32[16,1,256]{2,1,0:T(1,128)S(1)} %get-tuple-element.20), channel_id=1, replica_groups=mesh['yh'=2,'z'=8,'yl'=4,'x'=4,'core'=2] {'yl','x'}, dimensions={0} | all-to-all | bytes 32768 | tf_op jit(solution)/shard_map/all_to_all | solution.py:25
  95.3 4.8 %all-to-all-start.4 = ((f32[16,1,256]{2,1,0:T(1,128)}), f32[16,1,256]{2,1,0:T(1,128)S(1)}, u32[]{:S(2)}, u32[]{:S(2)}) async-start(f32[16,1,256]{2,1,0:T(1,128)} %get-tuple-element.21), calls=%async_computation.4 | async-start | bytes 32768 | tf_op jit(solution)/shard_map/all_to_all | solution.py:25
  101.1 10.3 %all-to-all-done.4.cols_ref = f32[16,1,256]{2,1,0:T(1,128)S(1)} async-done(((f32[16,1,256]{2,1,0:T(1,128)}), f32[16,1,256]{2,1,0:T(1,128)S(1)}, u32[]{:S(2)}, u32[]{:S(2)}) %all-to-all-start.4) | async-done | bytes 16416 | tf_op jit(solution)/shard_map/all_to_all | solution.py:25
  111.3 1.0 shard_map.96
  112.3 10.9 %all_to_all.44.part_ref = bf16[16,8,768]{2,1,0:T(8,128)(2,1)S(1)} all-to-all(bf16[16,8,768]{2,1,0:T(8,128)(2,1)S(1)} %bitcast.35), channel_id=1, replica_groups=mesh['yh'=2,'z'=8,'yl'=4,'x'=4,'core'=2] {'yl','x'}, dimensions={0} | all-to-all | bytes 393216 | tf_op jit(solution)/shard_map/all_to_all | solution.py:25
  123.4 10.9 %all_to_all.45 = bf16[16,8,768]{2,1,0:T(8,128)(2,1)S(1)} all-to-all(bf16[16,8,768]{2,1,0:T(8,128)(2,1)S(1)} %get-tuple-element.28), channel_id=1, replica_groups=mesh['yh'=2,'z'=8,'yl'=4,'x'=4,'core'=2] {'yl','x'}, dimensions={0} | all-to-all | bytes 393216 | tf_op jit(solution)/shard_map/all_to_all | solution.py:25
  134.3 7.7 %collective-permute-start.2 = (bf16[128,768]{1,0:T(8,128)(2,1)S(1)}, bf16[128,768]{1,0:T(8,128)(2,1)S(1)}, u32[]{:S(2)}, u32[]{:S(2)}) collective-permute-start(bf16[128,768]{1,0:T(8,128)(2,1)S(1)} %bitcast.33), channel_id=1, source_target_pairs={{0,1},{1,0},{2,3},{3,2},{4,5},{5,4},{6,7},{7,6},{8,9},{9,8},{10,11... | collective-permute-start | bytes 589832 | tf_op jit(solution)/shard_map/ppermute | solution.py:266
  142.0 1.0 constant_dynamic-slice_fusion
  143.0 1.0 copy-done.4
  145.0 2.2 %collective-permute-start.3 = (bf16[112,768]{1,0:T(8,128)(2,1)S(1)}, bf16[112,768]{1,0:T(8,128)(2,1)S(1)}, u32[]{:S(2)}, u32[]{:S(2)}) collective-permute-start(bf16[112,768]{1,0:T(8,128)(2,1)S(1)} %get-tuple-element.32), channel_id=1, source_target_pairs={{0,256},{256,0},{1,257},{257,1},{2,258},{258,2},{3,259},{259,3},{4... | collective-permute-start | bytes 516104 | tf_op jit(solution)/shard_map/ppermute | solution.py:282
  147.2 11.2 %collective-permute-done.3.got_ref = bf16[112,768]{1,0:T(8,128)(2,1)S(1)} collective-permute-done((bf16[112,768]{1,0:T(8,128)(2,1)S(1)}, bf16[112,768]{1,0:T(8,128)(2,1)S(1)}, u32[]{:S(2)}, u32[]{:S(2)}) %collective-permute-start.3) | collective-permute-done | bytes 172064 | tf_op jit(solution)/shard_map/ppermute | solution.py:282
  158.5 1.5 shard_map.100
  159.9 3.7 %all-to-all-start.7 = ((bf16[8,56,768]{2,1,0:T(8,128)(2,1)}), bf16[8,56,768]{2,1,0:T(8,128)(2,1)S(1)}, u32[]{:S(2)}, u32[]{:S(2)}) async-start(bf16[8,56,768]{2,1,0:T(8,128)(2,1)} %shard_map.100), calls=%async_computation.7 | async-start | bytes 1376256 | tf_op jit(solution)/shard_map/all_to_all | solution.py:25
  164.7 0.9 add_convert_fusion
  165.6 19.3 %all-to-all-done.7.got_ref = bf16[8,56,768]{2,1,0:T(8,128)(2,1)S(1)} async-done(((bf16[8,56,768]{2,1,0:T(8,128)(2,1)}), bf16[8,56,768]{2,1,0:T(8,128)(2,1)S(1)}, u32[]{:S(2)}, u32[]{:S(2)}) %all-to-all-start.7) | async-done | bytes 688160 | tf_op jit(solution)/shard_map/all_to_all | solution.py:25
  (44 shorter events, 8.8 us)
Async XLA Ops:
  0.6 1.0 copy-start
  18.8 30.6 %copy-start.5 = (bf16[8,768]{1,0:T(8,128)(2,1)S(1)}, bf16[8,768]{1,0:T(8,128)(2,1)}, u32[]{:S(2)}) copy-start(bf16[8,768]{1,0:T(8,128)(2,1)} %text_ref.3) | copy-start | bytes 36868
  44.2 34.9 %collective-permute-start = (bf16[4,4,64,768]{3,2,1,0:T(8,128)(2,1)S(1)}, bf16[4,4,64,768]{3,2,1,0:T(8,128)(2,1)}, u32[]{:S(2)}, u32[]{:S(2)}) collective-permute-start(bf16[4,4,64,768]{3,2,1,0:T(8,128)(2,1)S(1)} %all_to_all.41.own_ref), channel_id=1, source_target_pairs={{0,1},{1,0},{2,3},{3,2},{4,5},{5,4},{6,7},{7,6},{8,9},{9,8},{10,11... | collective-permute-start | bytes 4718600 | tf_op jit(solution)/shard_map/ppermute | solution.py:220
  74.5 4.5 %collective-permute-start.1 = (bf16[128,768]{1,0:T(8,128)(2,1)S(1)}, bf16[128,768]{1,0:T(8,128)(2,1)S(1)}, u32[]{:S(2)}, u32[]{:S(2)}) collective-permute-start(bf16[128,768]{1,0:T(8,128)(2,1)S(1)} %bitcast.30), channel_id=1, source_target_pairs={{0,1},{1,0},{2,3},{3,2},{4,5},{5,4},{6,7},{7,6},{8,9},{9,8},{10,11... | collective-permute-start | bytes 589832 | tf_op jit(solution)/shard_map/ppermute | solution.py:197
  83.1 1.4 copy-start.1
  84.5 0.7 copy-start.3
  85.2 10.1 %copy-start.6 = (bf16[256,1408]{1,0:T(8,128)(2,1)}, bf16[256,1408]{1,0:T(8,128)(2,1)S(1)}, u32[]{:S(2)}) copy-start(bf16[256,1408]{1,0:T(8,128)(2,1)S(1)} %get-tuple-element.27) | copy-start | bytes 2162692
  95.3 16.0 %all-to-all-start.4 = ((f32[16,1,256]{2,1,0:T(1,128)}), f32[16,1,256]{2,1,0:T(1,128)S(1)}, u32[]{:S(2)}, u32[]{:S(2)}) async-start(f32[16,1,256]{2,1,0:T(1,128)} %get-tuple-element.21), calls=%async_computation.4 | async-start | bytes 32768 | tf_op jit(solution)/shard_map/all_to_all | solution.py:25
  123.4 40.2 %copy-start.7 = (bf16[1408]{0:T(1024)(128)(2,1)S(1)}, bf16[1408]{0:T(1024)(128)(2,1)}, u32[]{:S(2)}) copy-start(bf16[1408]{0:T(1024)(128)(2,1)} %param.9) | copy-start | bytes 8452
  134.3 29.3 %copy-start.2 = (bf16[1408,768]{1,0:T(8,128)(2,1)S(1)}, bf16[1408,768]{1,0:T(8,128)(2,1)}, u32[]{:S(2)}) copy-start(bf16[1408,768]{1,0:T(8,128)(2,1)} %copy-done.1) | copy-start | bytes 6488068
  134.3 9.9 %collective-permute-start.2 = (bf16[128,768]{1,0:T(8,128)(2,1)S(1)}, bf16[128,768]{1,0:T(8,128)(2,1)S(1)}, u32[]{:S(2)}, u32[]{:S(2)}) collective-permute-start(bf16[128,768]{1,0:T(8,128)(2,1)S(1)} %bitcast.33), channel_id=1, source_target_pairs={{0,1},{1,0},{2,3},{3,2},{4,5},{5,4},{6,7},{7,6},{8,9},{9,8},{10,11... | collective-permute-start | bytes 589832 | tf_op jit(solution)/shard_map/ppermute | solution.py:266
  143.0 1.0 copy-start.4
  145.0 13.4 %collective-permute-start.3 = (bf16[112,768]{1,0:T(8,128)(2,1)S(1)}, bf16[112,768]{1,0:T(8,128)(2,1)S(1)}, u32[]{:S(2)}, u32[]{:S(2)}) collective-permute-start(bf16[112,768]{1,0:T(8,128)(2,1)S(1)} %get-tuple-element.32), channel_id=1, source_target_pairs={{0,256},{256,0},{1,257},{257,1},{2,258},{258,2},{3,259},{259,3},{4... | collective-permute-start | bytes 516104 | tf_op jit(solution)/shard_map/ppermute | solution.py:282
  159.9 4.7 %copy-start.8 = (s32[8]{0:T(128)S(1)}, s32[8]{0:T(128)}, u32[]{:S(2)}) copy-start(s32[8]{0:T(128)} %param.8) | copy-start | bytes 100
  159.9 25.1 %all-to-all-start.7 = ((bf16[8,56,768]{2,1,0:T(8,128)(2,1)}), bf16[8,56,768]{2,1,0:T(8,128)(2,1)S(1)}, u32[]{:S(2)}, u32[]{:S(2)}) async-start(bf16[8,56,768]{2,1,0:T(8,128)(2,1)} %shard_map.100), calls=%async_computation.7 | async-start | bytes 1376256 | tf_op jit(solution)/shard_map/all_to_all | solution.py:25

commit v3 on v2

v3 whole, which is shorter than its diff:
```python
import functools

import jax
import jax.numpy as jnp
from jax import lax
from jax.experimental import pallas as pl
from jax.experimental.pallas import tpu as pltpu
from jax.sharding import Mesh, PartitionSpec as P

EPS = 1e-06
F32 = jnp.float32
BF16 = jnp.bfloat16
DP = ("yh", "z")
CLIP = ("yl", "x", "core")
PLANE = ("yl", "x")
SWAP = [(0, 1), (1, 0)]


def unit_rows(values):
    norm_value = jnp.sqrt(jnp.sum(values * values, axis=1, keepdims=True) + EPS)
    return (values / norm_value, norm_value)


def exchange(blocks, axes):
    return lax.all_to_all(blocks, axes, split_axis=0, concat_axis=0, tiled=True)


def dot(a, b, contract):
    return lax.dot_general(a, b, (contract, ((), ())), preferred_element_type=F32)


def local(body, outs, n_scalars, n_args, n_far=0, scratch=(), flops=1e6, moved=1e6, mib=8):
    vmem = pl.BlockSpec(memory_space=pltpu.VMEM)
    smem = pl.BlockSpec(memory_space=pltpu.SMEM)
    far = pl.BlockSpec(memory_space=pltpu.HBM)
    return pl.pallas_call(
        body,
        out_shape=tuple(jax.ShapeDtypeStruct(shape, dtype) for shape, dtype in outs),
        in_specs=[smem] * n_scalars + [vmem] * n_args + [far] * n_far,
        out_specs=tuple(vmem for _ in outs),
        scratch_shapes=list(scratch),
        compiler_params=pltpu.CompilerParams(vmem_limit_bytes=mib * 1024 * 1024),
        cost_estimate=pl.CostEstimate(flops=int(flops), bytes_accessed=int(moved), transcendentals=0),
    )


def text_body(text_ref, out_ref):
    unit, _ = unit_rows(text_ref[...].astype(F32))
    out_ref[...] = jnp.broadcast_to(unit[None], out_ref.shape).astype(BF16)


def pool(counts_ref, embed, query):
    n_loc, n_clips, _ = embed.shape
    scores = jnp.sum(embed * query[None], axis=2, keepdims=True)
    video = lax.broadcasted_iota(jnp.int32, (n_loc, n_clips, 1), 0)
    clip = lax.broadcasted_iota(jnp.int32, (n_loc, n_clips, 1), 1)
    count = jnp.zeros((n_loc, n_clips, 1), jnp.int32)
    for v in range(n_loc):
        count = jnp.where(video == v, counts_ref[v], count)
    usable = clip < count
    masked = jnp.where(usable, scores, -1e30)
    raised = jnp.where(usable, jnp.exp(masked - jnp.max(masked, axis=1, keepdims=True)), 0.0)
    weights = raised / jnp.sum(raised, axis=1, keepdims=True)
    return weights, jnp.sum(weights * embed, axis=1)


def fetch(sources, targets, sems):
    copies = [
        pltpu.make_async_copy(source, target, sems.at[i])
        for i, (source, target) in enumerate(zip(sources, targets))
    ]
    for copy in copies:
        copy.start()
    for copy in copies:
        copy.wait()


def pool_body(
    query_ref, counts_hbm, clips_hbm, rows_hbm, payload_ref, counts_ref, clips_ref, rows_ref, sems
):
    fetch((counts_hbm, clips_hbm, rows_hbm), (counts_ref, clips_ref, rows_ref), sems)
    n_loc, _, width = clips_ref.shape
    w_rows, joint = rows_ref.shape
    w_pad = payload_ref.shape[0] - 2 * n_loc
    _, summary = pool(counts_ref, clips_ref[...].astype(F32), query_ref[...].astype(F32))
    high = jnp.concatenate(
        [summary[:, joint:], jnp.zeros((n_loc, 2 * joint - width), F32)], axis=1
    )
    tail = jnp.zeros((w_pad - w_rows, joint), F32)
    payload_ref[...] = jnp.concatenate(
        [rows_ref[...].astype(F32), tail, summary[:, :joint], high], axis=0
    ).astype(BF16)


def clips_body(
    d_own_ref, query_ref, counts_hbm, clips_hbm, weight_hbm, out_ref,
    counts_ref, clips_ref, weight_ref, sems,
):
    fetch((counts_hbm, clips_hbm, weight_hbm), (counts_ref, clips_ref, weight_ref), sems)
    embed = clips_ref[...].astype(F32)
    query = query_ref[...].astype(F32)
    weights, summary = pool(counts_ref, embed, query)
    d_summary = dot(d_own_ref[...], weight_ref[...], ((1,), (1,)))
    aligned = jnp.sum(embed * d_summary[:, None, :], axis=2, keepdims=True)
    baseline = jnp.sum(d_summary * summary, axis=1, keepdims=True)
    d_scores = weights * (aligned - baseline[:, None, :])
    out_ref[...] = (weights * d_summary[:, None, :] + d_scores * query[None]).astype(BF16)


def column(row):
    return jnp.broadcast_to(row, (128, row.shape[1])).T[:, :1]


def logits_body(
    n_loc, w_rows, scale_ref, own_ref, other_ref, text_own_ref, text_other_ref,
    _, weight_ref, summary_ref, video_ref, unit_ref, norm_ref, expo_ref, rows_ref, cols_ref,
    weight_f, summary_f, unit_f, norm_f,
):
    n_x, n_yl, _, joint = own_ref.shape
    width = weight_ref.shape[0]
    half = n_x * n_yl * n_loc
    w_pad = -(-w_rows // 16) * 16
    first = lax.axis_index("core") == 0
    yl_id = lax.axis_index("yl")
    for x in range(n_x):
        for yl in range(n_yl):
            slot = jnp.bitwise_xor(yl_id, yl)
            own = own_ref[x, slot].astype(F32)
            other = other_ref[x, slot].astype(F32)
            pair = (jnp.where(first, own, other), jnp.where(first, other, own))
            for core in range(2):
                at = ((yl * n_x + x) * 2 + core) * w_rows
                weight_f[at : at + w_rows, :] = pair[core][:w_rows]
                row = core * half + (yl * n_x + x) * n_loc
                summary_f[row : row + n_loc, :joint] = pair[core][w_pad : w_pad + n_loc]
                summary_f[row : row + n_loc, joint:] = pair[core][w_pad + n_loc :, : width - joint]
    weight_b = weight_f[...].astype(BF16)
    summary_b = summary_f[...].astype(BF16)
    weight_ref[...] = weight_b
    summary_ref[...] = summary_b
    unit, norm = unit_rows(dot(summary_b, weight_b, ((1,), (0,))))
    video_b = unit.astype(BF16)
    video_ref[...] = video_b
    unit_f[...] = unit
    norm_f[...] = jnp.broadcast_to(norm, norm_f.shape)
    place = (lax.axis_index("core") * n_yl + yl_id) * n_x + lax.axis_index("x")
    mine = pl.ds(pl.multiple_of(place * n_loc, n_loc), n_loc)
    unit_ref[...] = unit_f[mine, :]
    norm_ref[...] = norm_f[mine, :]
    n_lane = text_own_ref.shape[0]
    scale = scale_ref[0]
    expo_ref[:, :n_lane] = jnp.exp(scale * dot(video_b, text_own_ref[...], ((1,), (1,))))
    expo_ref[:, n_lane:] = jnp.exp(scale * dot(video_b, text_other_ref[...], ((1,), (1,))))
    expo = expo_ref[...]
    row_part = jnp.broadcast_to(jnp.sum(expo, axis=1, keepdims=True), (2 * half, 128)).T[:1]
    col_part = jnp.sum(expo, axis=0, keepdims=True)
    rows_ref[...] = jnp.broadcast_to(row_part[None], rows_ref.shape)
    cols_ref[...] = jnp.broadcast_to(col_part[None], cols_ref.shape)


def grad_body(
    n_loc, n_clip, scale_ref, expo_ref, rows_ref, cols_ref, pairs_ref, text_own_ref,
    text_other_ref, video_ref, part_ref, text_part_ref, grad_ref,
):
    n_lane = text_own_ref.shape[0]
    rows = jnp.sum(rows_ref[...], axis=0)
    cols = jnp.sum(cols_ref[...], axis=0)
    core = lax.axis_index("core")
    plane = lax.axis_index("yl") * lax.axis_size("x") + lax.axis_index("x")
    at = lax.broadcasted_iota(jnp.int32, (1, 2 * n_lane), 1)
    lane = jnp.where(at < n_lane, plane * 2 + core, plane * 2 + (1 - core))
    slot = jnp.where(at < n_lane, at, at - n_lane)
    col_id = ((slot // n_loc) * n_clip + lane) * n_loc + slot % n_loc
    group = lax.axis_index("yh") * lax.axis_size("z") + lax.axis_index("z")
    pairs = column(pairs_ref[pl.ds(group, 1), :].astype(F32)).astype(jnp.int32)
    pairs = pairs.reshape(-1, 2, n_loc, 1)
    pairs = jnp.concatenate([pairs[:, 0], pairs[:, 1]], axis=0).reshape(-1, 1)
    positive = jnp.where(pairs == col_id, 1.0, 0.0)
    expo = expo_ref[...]
    grad = (expo / column(rows) + expo / cols) * 0.5 - positive
    grad_ref[...] = grad.astype(BF16)
    half = expo.shape[0] // 2
    mine = grad_ref[pl.ds(pl.multiple_of(core * half, half), half), :]
    part = dot(mine[:, :n_lane], text_own_ref[...], ((1,), (0,)))
    part = part + dot(mine[:, n_lane:], text_other_ref[...], ((1,), (0,)))
    part_ref[...] = (scale_ref[0] * part).astype(BF16)
    text_part = dot(grad_ref[:, :n_lane], video_ref[...], ((0,), (0,)))
    text_part_ref[...] = (scale_ref[0] * text_part).astype(BF16)


def projected_body(part_ref, unit_ref, norm_ref, out_ref, own_ref):
    d_video = jnp.sum(part_ref[...].astype(F32), axis=0)
    unit = unit_ref[...]
    norm = norm_ref[:, :1]
    value = (d_video - unit * jnp.sum(unit * d_video, axis=1, keepdims=True)) / norm
    out_ref[...] = jnp.broadcast_to(value[None], out_ref.shape).astype(BF16)
    own_ref[...] = value.astype(BF16)


def weight_body(cols_ref, own_ref, other_ref, text_ref, out_ref):
    n_z, _, joint = out_ref.shape
    half = own_ref.shape[0]
    core = lax.axis_index("core")
    yh_id = lax.axis_index("yh")
    own_cols = cols_ref[pl.ds(pl.multiple_of(core * half, half), half), :]
    other_cols = cols_ref[pl.ds(pl.multiple_of((1 - core) * half, half), half), :]
    part = dot(own_cols, own_ref[...], ((0,), (0,))) + dot(other_cols, other_ref[...], ((0,), (0,)))
    n_text = text_ref.shape[0] // 2
    n_loc = n_text // n_z
    piece = part.shape[0] // n_z
    spare = out_ref.shape[1] - 2 * n_loc - piece
    here = text_ref[pl.ds(pl.multiple_of(yh_id * n_text, n_text), n_text), :].astype(F32)
    away = text_ref[pl.ds(pl.multiple_of((1 - yh_id) * n_text, n_text), n_text), :].astype(F32)
    for z in range(n_z):
        rows = jnp.concatenate(
            [
                here[z * n_loc : (z + 1) * n_loc],
                away[z * n_loc : (z + 1) * n_loc],
                part[z * piece : (z + 1) * piece],
                jnp.zeros((spare, joint), F32),
            ],
            axis=0,
        )
        out_ref[z] = rows.astype(BF16)


def z_sum_body(got_ref, here_ref, away_ref):
    total = jnp.sum(got_ref[...].astype(F32), axis=0)
    n_loc = here_ref.shape[0] // 2
    piece = total[2 * n_loc :]
    here_ref[...] = jnp.concatenate([total[:n_loc], piece], axis=0)
    away_ref[...] = jnp.concatenate([total[n_loc : 2 * n_loc], piece], axis=0).astype(BF16)


def yh_sum_body(here_ref, got_ref, text_ref, out_ref, d_texts_ref):
    total = here_ref[...] + got_ref[...].astype(F32)
    n_loc = text_ref.shape[0]
    unit, norm = unit_rows(text_ref[...].astype(F32))
    d_text = total[:n_loc]
    d_texts_ref[...] = (d_text - unit * jnp.sum(unit * d_text, axis=1, keepdims=True)) / norm
    out_ref[...] = jnp.broadcast_to(total[None, n_loc:], out_ref.shape)


def last_body(piece, got_ref, out_ref):
    rows = [got_ref[z, :piece, :] for z in range(got_ref.shape[0])]
    out_ref[...] = jnp.concatenate(rows, axis=0)[: out_ref.shape[0]]


def shards(clip_embed, clip_counts, pool_query, proj_weight, text_embed, pair_index, logit_scale):
    n_loc, n_clips, width = clip_embed.shape
    w_rows, joint = proj_weight.shape
    n_dp, n_yh, n_z = lax.axis_size(DP), lax.axis_size("yh"), lax.axis_size("z")
    n_yl, n_x, n_clip = lax.axis_size("yl"), lax.axis_size("x"), lax.axis_size(CLIP)
    n_plane = n_yl * n_x
    group_rows = n_loc * n_clip
    half = group_rows // 2
    n_lane = n_dp * n_loc
    core_id = lax.axis_index("core")
    plane_id = lax.axis_index(PLANE)
    lane_id = lax.axis_index(CLIP)
    group_id = lax.axis_index(DP)
    (text_send,) = local(text_body, [((n_dp, n_loc, joint), BF16)], 0, 1)(text_embed)
    text_own = exchange(text_send, DP).reshape(n_lane, joint)
    text_other = lax.ppermute(text_own, "core", SWAP)

    w_pad = -(-w_rows // 16) * 16
    query = pool_query.reshape(1, width)
    stage = [
        pltpu.SMEM((n_loc,), jnp.int32),
        pltpu.VMEM((n_loc, n_clips, width), BF16),
    ]
    (payload,) = local(
        pool_body,
        [((w_pad + 2 * n_loc, joint), BF16)],
        0,
        1,
        3,
        scratch=stage + [pltpu.VMEM((w_rows, joint), BF16), pltpu.SemaphoreType.DMA((3,))],
    )(query, clip_counts, clip_embed, proj_weight)

    near = [payload] + [
        lax.ppermute(payload, "yl", [(i, i ^ k) for i in range(n_yl)]) for k in range(1, n_yl)
    ]
    over_y = jnp.stack(near)
    over_y, text_own, text_other = lax.optimization_barrier((over_y, text_own, text_other))
    over_x = exchange(jnp.broadcast_to(over_y[None], (n_x, *over_y.shape)), "x")

    pairs = pair_index.reshape(n_dp, group_rows)
    over_x_other = lax.ppermute(over_x, "core", SWAP)

    full_weight, summaries, video_b, unit_own, norm_own, expo, row_send, col_send = local(
        functools.partial(logits_body, n_loc, w_rows),
        [
            ((width, joint), BF16),
            ((group_rows, width), BF16),
            ((group_rows, joint), BF16),
            ((n_loc, joint), F32),
            ((n_loc, 128), F32),
            ((group_rows, 2 * n_lane), F32),
            ((n_plane, 1, group_rows), F32),
            ((n_dp, 1, 2 * n_lane), F32),
        ],
        1,
        5,
        scratch=[
            pltpu.VMEM((width, joint), F32),
            pltpu.VMEM((group_rows, width), F32),
            pltpu.VMEM((group_rows, joint), F32),
            pltpu.VMEM((group_rows, 128), F32),
        ],
        flops=7e8,
        moved=8e6,
        mib=20,
    )(logit_scale, over_x, over_x_other, text_own, text_other, pairs)
    rows = exchange(row_send, PLANE)
    cols = exchange(col_send, DP)

    video_part, text_part = local(
        functools.partial(grad_body, n_loc, n_clip),
        [((half, joint), BF16), ((n_lane, joint), BF16)],
        1,
        7,
        scratch=[pltpu.VMEM((group_rows, 2 * n_lane), BF16)],
        flops=2e8,
    )(logit_scale, expo, rows, cols, pairs, text_own, text_other, video_b)

    got_video = exchange(video_part.reshape(n_plane, n_loc, joint), PLANE)
    d_send, d_own = local(
        projected_body, [((n_plane, n_loc, joint), BF16), ((n_loc, joint), BF16)], 0, 3
    )(got_video, unit_own, norm_own)
    d_half, d_own = lax.optimization_barrier((exchange(d_send, PLANE).reshape(half, joint), d_own))
    d_half_other = lax.ppermute(d_half, "core", SWAP)

    summary_cols = lax.dynamic_slice(summaries, (0, lane_id * w_rows), (group_rows, w_rows))
    summary_cols = jnp.pad(summary_cols, ((0, 0), (0, w_pad - w_rows)))
    d_half, summary_cols = lax.optimization_barrier((d_half, summary_cols))
    piece = w_pad // n_z
    spare = -(-piece // 8) * 8
    (parts,) = local(weight_body, [((n_z, 2 * n_loc + spare, joint), BF16)], 0, 4, flops=3e7)(
        summary_cols, d_half, d_half_other, text_part
    )
    got_z, d_own = lax.optimization_barrier((exchange(parts, "z"), d_own))
    here, away = local(
        z_sum_body, [((n_loc + spare, joint), F32), ((n_loc + spare, joint), BF16)], 0, 1
    )(got_z)
    got_yh = lax.ppermute(away, "yh", SWAP)

    (d_clips,) = local(
        clips_body,
        [((n_loc, n_clips, width), BF16)],
        0,
        2,
        3,
        scratch=stage + [pltpu.VMEM((width, joint), BF16), pltpu.SemaphoreType.DMA((3,))],
        flops=2e7,
        moved=3e6,
    )(d_own, query, clip_counts, clip_embed, full_weight)
    piece_send, d_texts = local(
        yh_sum_body, [((n_z, spare, joint), F32), ((n_loc, joint), F32)], 0, 3
    )(here, got_yh, text_embed)
    piece_send, d_clips = lax.optimization_barrier((piece_send, d_clips))
    (d_weight,) = local(functools.partial(last_body, piece), [((w_rows, joint), F32)], 0, 1)(
        exchange(piece_send, "z")
    )
    return (d_clips, d_weight, d_texts)


def solution(mesh):
    fine = Mesh(mesh.devices.reshape(2, 8, 4, 4, 2), DP + CLIP)
    everywhere = DP + CLIP
    return jax.shard_map(
        shards,
        mesh=fine,
        in_specs=(
            P(everywhere, None, None),
            P(everywhere),
            P(),
            P(CLIP, None),
            P(everywhere, None),
            P(),
            P(),
        ),
        out_specs=(P(everywhere, None, None), P(CLIP, None), P(everywhere, None)),
        check_vma=False,
    )
```

time: 187 us -> 173 us (0.925)
  waiting for transfers between devices: 41.1 us -> 6.69 us
  starting transfers between devices: 27 us -> 43.4 us
  blocking collectives: 95.1 us -> 104 us
  other arithmetic: 4.34 us -> 0.05 us
    all_to_all x2 -> x1, waiting for transfers between devices: 29.6 us -> 0.01 us  [exchange(): return lax.all_to_all(blocks, axes, split_axis=0, concat_axis=0, tiled=True)]
    ppermute x1 -> x4, starting transfers between devices: 2.2 us -> 11.5 us  [the longest x3 9.27 us: shards(): lax.ppermute(payload, 'yl', [(i, i ^ k) for i in range(n_yl)])]
    all_to_all x6 -> x7, blocking collectives: 95.1 us -> 104 us  [exchange(): return lax.all_to_all(blocks, axes, split_axis=0, concat_axis=0, tiled=True)]
    all_to_all x2 -> x1, starting transfers between devices: 8.44 us -> 16.2 us  [exchange(): return lax.all_to_all(blocks, axes, split_axis=0, concat_axis=0, tiled=True)]
    ppermute x1 -> x4, waiting for transfers between devices: 11.2 us -> 4.08 us  [the longest x1 4.08 us: shards(): got_yh = lax.ppermute(away, 'yh', SWAP)]
    pallas_call x1, Pallas kernels: 4.03 us -> 2.11 us  [shards(): local(functools.partial(logits_body, n_loc, w_rows), [((width, joint), BF...]
    pallas_call x5 -> x7, Pallas kernels: 4.31 us -> 5.29 us  [the longest x1 2.15 us: shards(): local(clips_body, [((n_loc, n_clips, width), BF16)], 0, 2, 3, scratch=sta...]
    unnamed x19 -> x24, local copies, waits for them, and re-layouts: 4.11 us -> 4.62 us
  transfers between devices with their start and end apart: 6 -> 8, of which waited for: 4 -> 3; matrix products, arithmetic and copies ran while one was open for 2% -> 1% of each run, Pallas kernels for 0% -> 2%
where the time goes in v3:
time: 173 us; the launch traced here: 171 us
  blocking collectives  104 us (60%)
  starting transfers between devices  43.4 us (25%)
  Pallas kernels  8.32 us (5%)
  local copies, waits for them, and re-layouts  7.22 us (4%)
  waiting for transfers between devices  6.69 us (4%)
    all_to_all x7, blocking collectives, exchange(): return lax.all_to_all(blocks, axes, split_axis=0, concat_axis=0, tiled=True)  104 us
    all_to_all x1, starting transfers between devices, exchange(): return lax.all_to_all(blocks, axes, split_axis=0, concat_axis=0, tiled=True)  16.2 us
    ppermute x3, starting transfers between devices, shards(): lax.ppermute(payload, 'yl', [(i, i ^ k) for i in range(n_yl)])  9.27 us
    ppermute x1, starting transfers between devices, shards(): d_half_other = lax.ppermute(d_half, 'core', SWAP)  7.54 us
    unnamed x24, local copies, waits for them, and re-layouts  4.62 us
    ppermute x1, starting transfers between devices, shards(): over_x_other = lax.ppermute(over_x, 'core', SWAP)  4.49 us
    ppermute x1, waiting for transfers between devices, shards(): got_yh = lax.ppermute(away, 'yh', SWAP)  4.08 us
    ppermute x1, starting transfers between devices, shards(): text_other = lax.ppermute(text_own, 'core', SWAP)  3.7 us
  transfers between devices with their start and end apart: 8, of which 3 were waited for; matrix products, arithmetic and copies ran while one was open for 1% of the time, Pallas kernels for 2%

profile of v3, /device:TPU:1, one launch (start us, length us, event | category | flops | bytes accessed | tf_op | source)
XLA Modules:
  0.0 171.0 jit_solution(17688377583826371873)
XLA Ops:
  2.1 16.2 %all-to-all-start = ((bf16[16,8,768]{2,1,0:T(8,128)(2,1)}), bf16[16,8,768]{2,1,0:T(8,128)(2,1)S(1)}, u32[]{:S(2)}, u32[]{:S(2)}) async-start(bf16[16,8,768]{2,1,0:T(8,128)(2,1)} %shard_map.95), calls=%async_computation | async-start | bytes 393216 | tf_op jit(solution)/shard_map/all_to_all | solution.py:25
  19.1 1.0 copy-done.2
  20.0 0.9 copy-done.4
  22.4 2.3 %collective-permute-start = (bf16[64,768]{1,0:T(8,128)(2,1)S(1)}, bf16[64,768]{1,0:T(8,128)(2,1)S(1)}, u32[]{:S(2)}, u32[]{:S(2)}) collective-permute-start(bf16[64,768]{1,0:T(8,128)(2,1)S(1)} %shard_map.94), channel_id=1, source_target_pairs={{0,8},{8,0},{16,24},{24,16},{1,9},{9,1},{17,25},{25,17},{2,10},{10... | collective-permute-start | bytes 294920 | tf_op jit(solution)/shard_map/ppermute | solution.py:282
  24.8 2.4 %collective-permute-start.1 = (bf16[64,768]{1,0:T(8,128)(2,1)S(1)}, bf16[64,768]{1,0:T(8,128)(2,1)S(1)}, u32[]{:S(2)}, u32[]{:S(2)}) collective-permute-start(bf16[64,768]{1,0:T(8,128)(2,1)S(1)} %shard_map.94), channel_id=1, source_target_pairs={{0,16},{8,24},{16,0},{24,8},{1,17},{9,25},{17,1},{25,9},{2,18},{10... | collective-permute-start | bytes 294920 | tf_op jit(solution)/shard_map/ppermute | solution.py:282
  27.2 4.5 %collective-permute-start.2 = (bf16[64,768]{1,0:T(8,128)(2,1)S(1)}, bf16[64,768]{1,0:T(8,128)(2,1)S(1)}, u32[]{:S(2)}, u32[]{:S(2)}) collective-permute-start(bf16[64,768]{1,0:T(8,128)(2,1)S(1)} %shard_map.94), channel_id=1, source_target_pairs={{0,24},{8,16},{16,8},{24,0},{1,25},{9,17},{17,9},{25,1},{2,26},{10... | collective-permute-start | bytes 294920 | tf_op jit(solution)/shard_map/ppermute | solution.py:282
  31.7 3.7 %collective-permute-start.3 = (bf16[128,768]{1,0:T(8,128)(2,1)S(1)}, bf16[128,768]{1,0:T(8,128)(2,1)S(1)}, u32[]{:S(2)}, u32[]{:S(2)}) collective-permute-start(bf16[128,768]{1,0:T(8,128)(2,1)S(1)} %bitcast.7), channel_id=1, source_target_pairs={{0,1},{1,0},{2,3},{3,2},{4,5},{5,4},{6,7},{7,6},{8,9},{9,8},{10,11... | collective-permute-start | bytes 589832 | tf_op jit(solution)/shard_map/ppermute | solution.py:264
  35.5 1.0 collective-permute-done.3.text_other_ref
  36.7 22.9 %all_to_all.40.own_ref = bf16[4,4,64,768]{3,2,1,0:T(8,128)(2,1)S(1)} all-to-all(bf16[4,4,64,768]{3,2,1,0:T(8,128)(2,1)S(1)} %broadcast_in_dim.2), channel_id=1, replica_groups=mesh['yh'=2,'z'=8,'yl'=4,'x'=4,'core'=2] {'x'}, dimensions={0} | all-to-all | bytes 3145728 | tf_op jit(solution)/shard_map/all_to_all | solution.py:25
  59.6 4.5 %collective-permute-start.4 = (bf16[4,4,64,768]{3,2,1,0:T(8,128)(2,1)S(1)}, bf16[4,4,64,768]{3,2,1,0:T(8,128)(2,1)S(1)}, u32[]{:S(2)}, u32[]{:S(2)}) collective-permute-start(bf16[4,4,64,768]{3,2,1,0:T(8,128)(2,1)S(1)} %all_to_all.40.own_ref), channel_id=1, source_target_pairs={{0,1},{1,0},{2,3},{3,2},{4,5},{5,4},{6,7},{7,6},{8,9},{9,8},{10,11... | collective-permute-start | bytes 4718600 | tf_op jit(solution)/shard_map/ppermute | solution.py:289
  65.4 1.6 collective-permute-done.4.other_ref
  67.1 2.1 %shard_map.96 = (bf16[1408,768]{1,0:T(8,128)(2,1)S(1)}, bf16[256,1408]{1,0:T(8,128)(2,1)S(1)}, bf16[256,768]{1,0:T(8,128)(2,1)S(1)}, f32[8,768]{1,0:T(8,128)S(1)...) custom-call(f32[1]{0:T(128)S(6)} %copy.10.scale_ref, ...), custom_call_target="tpu_custom_call" | custom-call | flops 700000000 | bytes 8000000 | tf_op jit(solution)/shard_map/pallas_call | solution.py:291
  69.2 1.4 copy-done
  70.5 10.3 %all_to_all.41.rows_ref = f32[16,1,256]{2,1,0:T(1,128)S(1)} all-to-all(f32[16,1,256]{2,1,0:T(1,128)S(1)} %get-tuple-element.34), channel_id=1, replica_groups=mesh['yh'=2,'z'=8,'yl'=4,'x'=4,'core'=2] {'yl','x'}, dimensions={0} | all-to-all | bytes 32768 | tf_op jit(solution)/shard_map/all_to_all | solution.py:25
  80.9 22.5 %all_to_all.42.cols_ref = f32[16,1,256]{2,1,0:T(1,128)S(1)} all-to-all(f32[16,1,256]{2,1,0:T(1,128)S(1)} %get-tuple-element.35), channel_id=1, replica_groups=mesh['yh'=2,'z'=8,'yl'=4,'x'=4,'core'=2] {'yh','z'}, dimensions={0} | all-to-all | bytes 32768 | tf_op jit(solution)/shard_map/all_to_all | solution.py:25
  104.0 11.0 %all_to_all.43.part_ref = bf16[16,8,768]{2,1,0:T(8,128)(2,1)S(1)} all-to-all(bf16[16,8,768]{2,1,0:T(8,128)(2,1)S(1)} %bitcast.13), channel_id=1, replica_groups=mesh['yh'=2,'z'=8,'yl'=4,'x'=4,'core'=2] {'yl','x'}, dimensions={0} | all-to-all | bytes 393216 | tf_op jit(solution)/shard_map/all_to_all | solution.py:25
  115.1 10.9 %all_to_all.44 = bf16[16,8,768]{2,1,0:T(8,128)(2,1)S(1)} all-to-all(bf16[16,8,768]{2,1,0:T(8,128)(2,1)S(1)} %get-tuple-element.40), channel_id=1, replica_groups=mesh['yh'=2,'z'=8,'yl'=4,'x'=4,'core'=2] {'yl','x'}, dimensions={0} | all-to-all | bytes 393216 | tf_op jit(solution)/shard_map/all_to_all | solution.py:25
  126.0 7.5 %collective-permute-start.5 = (bf16[128,768]{1,0:T(8,128)(2,1)S(1)}, bf16[128,768]{1,0:T(8,128)(2,1)S(1)}, u32[]{:S(2)}, u32[]{:S(2)}) collective-permute-start(bf16[128,768]{1,0:T(8,128)(2,1)S(1)} %bitcast.10), channel_id=1, source_target_pairs={{0,1},{1,0},{2,3},{3,2},{4,5},{5,4},{6,7},{7,6},{8,9},{9,8},{10,11... | collective-permute-start | bytes 589832 | tf_op jit(solution)/shard_map/ppermute | solution.py:332
  133.6 1.0 constant_dynamic-slice_fusion
  134.9 15.0 %all_to_all.45.got_ref = bf16[8,24,768]{2,1,0:T(8,128)(2,1)S(1)} all-to-all(bf16[8,24,768]{2,1,0:T(8,128)(2,1)S(1)} %shard_map.99), channel_id=1, replica_groups=mesh['yh'=2,'z'=8,'yl'=4,'x'=4,'core'=2] {'z'}, dimensions={0} | all-to-all | bytes 589824 | tf_op jit(solution)/shard_map/all_to_all | solution.py:25
  149.9 2.2 %collective-permute-start.6 = (bf16[16,768]{1,0:T(8,128)(2,1)S(1)}, bf16[16,768]{1,0:T(8,128)(2,1)S(1)}, u32[]{:S(2)}, u32[]{:S(2)}) collective-permute-start(bf16[16,768]{1,0:T(8,128)(2,1)S(1)} %get-tuple-element.50), channel_id=1, source_target_pairs={{0,256},{256,0},{1,257},{257,1},{2,258},{258,2},{3,259},{259,3},{4... | collective-permute-start | bytes 73736 | tf_op jit(solution)/shard_map/ppermute | solution.py:346
  152.2 2.2 %shard_map.102 = bf16[8,16,1408]{2,1,0:T(8,128)(2,1)} custom-call(bf16[8,768]{1,0:T(8,128)(2,1)S(1)} %get-tuple-element.52.d_own_ref, bf16[1,1408]{1,0:T(2,128)(2,1)S(1)} %copy-done.6, s32[8]{0:T(128)S(1)} %copy-done.11, bf16[8,16,1408]{2,1,0:T(8,128)(2,1)S(1)} %copy-done.3, bf16[1408,768]{1,0:T(8,128)(2,1)S(1)} %copy-done.1), custom_call_target="tpu_custom_call" | custom-call | flops 20000000 | bytes 3000000 | tf_op jit(solution)/shard_map/pallas_call | solution.py:348
  154.4 4.1 %collective-permute-done.6.got_ref = bf16[16,768]{1,0:T(8,128)(2,1)S(1)} collective-permute-done((bf16[16,768]{1,0:T(8,128)(2,1)S(1)}, bf16[16,768]{1,0:T(8,128)(2,1)S(1)}, u32[]{:S(2)}, u32[]{:S(2)}) %collective-permute-start.6) | collective-permute-done | bytes 24608 | tf_op jit(solution)/shard_map/ppermute | solution.py:346
  159.2 11.1 %all_to_all.46.got_ref = f32[8,8,768]{2,1,0:T(8,128)S(1)} all-to-all(f32[8,8,768]{2,1,0:T(8,128)S(1)} %get-tuple-element.55), channel_id=1, replica_groups=mesh['yh'=2,'z'=8,'yl'=4,'x'=4,'core'=2] {'z'}, dimensions={0} | all-to-all | bytes 393216 | tf_op jit(solution)/shard_map/all_to_all | solution.py:25
  (39 shorter events, 7.1 us)
Async XLA Ops:
  0.6 0.7 copy-start.7
  2.1 29.6 %all-to-all-start = ((bf16[16,8,768]{2,1,0:T(8,128)(2,1)}), bf16[16,8,768]{2,1,0:T(8,128)(2,1)S(1)}, u32[]{:S(2)}, u32[]{:S(2)}) async-start(bf16[16,8,768]{2,1,0:T(8,128)(2,1)} %shard_map.95), calls=%async_computation | async-start | bytes 393216 | tf_op jit(solution)/shard_map/all_to_all | solution.py:25
  19.1 1.0 copy-start.2
  20.0 0.9 copy-start.4
  20.9 0.7 copy-start.10
  21.6 14.9 %copy-start.5 = (bf16[1,1408]{1,0:T(2,128)(2,1)}, bf16[1,1408]{1,0:T(2,128)(2,1)S(1)}, u32[]{:S(2)}) copy-start(bf16[1,1408]{1,0:T(2,128)(2,1)S(1)} %reshape.22.query_ref) | copy-start | bytes 8452
  22.4 13.0 %collective-permute-start = (bf16[64,768]{1,0:T(8,128)(2,1)S(1)}, bf16[64,768]{1,0:T(8,128)(2,1)S(1)}, u32[]{:S(2)}, u32[]{:S(2)}) collective-permute-start(bf16[64,768]{1,0:T(8,128)(2,1)S(1)} %shard_map.94), channel_id=1, source_target_pairs={{0,8},{8,0},{16,24},{24,16},{1,9},{9,1},{17,25},{25,17},{2,10},{10... | collective-permute-start | bytes 294920 | tf_op jit(solution)/shard_map/ppermute | solution.py:282
  24.8 10.7 %collective-permute-start.1 = (bf16[64,768]{1,0:T(8,128)(2,1)S(1)}, bf16[64,768]{1,0:T(8,128)(2,1)S(1)}, u32[]{:S(2)}, u32[]{:S(2)}) collective-permute-start(bf16[64,768]{1,0:T(8,128)(2,1)S(1)} %shard_map.94), channel_id=1, source_target_pairs={{0,16},{8,24},{16,0},{24,8},{1,17},{9,25},{17,1},{25,9},{2,18},{10... | collective-permute-start | bytes 294920 | tf_op jit(solution)/shard_map/ppermute | solution.py:282
  27.2 8.3 %collective-permute-start.2 = (bf16[64,768]{1,0:T(8,128)(2,1)S(1)}, bf16[64,768]{1,0:T(8,128)(2,1)S(1)}, u32[]{:S(2)}, u32[]{:S(2)}) collective-permute-start(bf16[64,768]{1,0:T(8,128)(2,1)S(1)} %shard_map.94), channel_id=1, source_target_pairs={{0,24},{8,16},{16,8},{24,0},{1,25},{9,17},{17,9},{25,1},{2,26},{10... | collective-permute-start | bytes 294920 | tf_op jit(solution)/shard_map/ppermute | solution.py:282
  31.7 4.8 %collective-permute-start.3 = (bf16[128,768]{1,0:T(8,128)(2,1)S(1)}, bf16[128,768]{1,0:T(8,128)(2,1)S(1)}, u32[]{:S(2)}, u32[]{:S(2)}) collective-permute-start(bf16[128,768]{1,0:T(8,128)(2,1)S(1)} %bitcast.7), channel_id=1, source_target_pairs={{0,1},{1,0},{2,3},{3,2},{4,5},{5,4},{6,7},{7,6},{8,9},{9,8},{10,11... | collective-permute-start | bytes 589832 | tf_op jit(solution)/shard_map/ppermute | solution.py:264
  59.6 7.5 %collective-permute-start.4 = (bf16[4,4,64,768]{3,2,1,0:T(8,128)(2,1)S(1)}, bf16[4,4,64,768]{3,2,1,0:T(8,128)(2,1)S(1)}, u32[]{:S(2)}, u32[]{:S(2)}) collective-permute-start(bf16[4,4,64,768]{3,2,1,0:T(8,128)(2,1)S(1)} %all_to_all.40.own_ref), channel_id=1, source_target_pairs={{0,1},{1,0},{2,3},{3,2},{4,5},{5,4},{6,7},{7,6},{8,9},{9,8},{10,11... | collective-permute-start | bytes 4718600 | tf_op jit(solution)/shard_map/ppermute | solution.py:289
  69.2 1.4 copy-start
  70.5 55.5 %copy-start.9 = (bf16[256,1408]{1,0:T(8,128)(2,1)}, bf16[256,1408]{1,0:T(8,128)(2,1)S(1)}, u32[]{:S(2)}) copy-start(bf16[256,1408]{1,0:T(8,128)(2,1)S(1)} %get-tuple-element.43) | copy-start | bytes 2162692
  103.9 48.2 %copy-start.1 = (bf16[1408,768]{1,0:T(8,128)(2,1)S(1)}, bf16[1408,768]{1,0:T(8,128)(2,1)}, u32[]{:S(2)}) copy-start(bf16[1408,768]{1,0:T(8,128)(2,1)} %copy-done) | copy-start | bytes 6488068
  103.9 48.2 %copy-start.3 = (bf16[8,16,1408]{2,1,0:T(8,128)(2,1)S(1)}, bf16[8,16,1408]{2,1,0:T(8,128)(2,1)}, u32[]{:S(2)}) copy-start(bf16[8,16,1408]{2,1,0:T(8,128)(2,1)} %clips_hbm.3) | copy-start | bytes 1081348
  103.9 48.2 %copy-start.6 = (bf16[1,1408]{1,0:T(2,128)(2,1)S(1)}, bf16[1,1408]{1,0:T(2,128)(2,1)}, u32[]{:S(2)}) copy-start(bf16[1,1408]{1,0:T(2,128)(2,1)} %copy-done.5) | copy-start | bytes 8452
  103.9 48.2 %copy-start.11 = (s32[8]{0:T(128)S(1)}, s32[8]{0:T(128)}, u32[]{:S(2)}) copy-start(s32[8]{0:T(128)} %counts_hbm.3) | copy-start | bytes 100
  126.0 8.6 %collective-permute-start.5 = (bf16[128,768]{1,0:T(8,128)(2,1)S(1)}, bf16[128,768]{1,0:T(8,128)(2,1)S(1)}, u32[]{:S(2)}, u32[]{:S(2)}) collective-permute-start(bf16[128,768]{1,0:T(8,128)(2,1)S(1)} %bitcast.10), channel_id=1, source_target_pairs={{0,1},{1,0},{2,3},{3,2},{4,5},{5,4},{6,7},{7,6},{8,9},{9,8},{10,11... | collective-permute-start | bytes 589832 | tf_op jit(solution)/shard_map/ppermute | solution.py:332
  149.9 8.5 %copy-start.8 = (bf16[8,768]{1,0:T(8,128)(2,1)S(1)}, bf16[8,768]{1,0:T(8,128)(2,1)}, u32[]{:S(2)}) copy-start(bf16[8,768]{1,0:T(8,128)(2,1)} %text_ref.3) | copy-start | bytes 36868
  149.9 8.5 %collective-permute-start.6 = (bf16[16,768]{1,0:T(8,128)(2,1)S(1)}, bf16[16,768]{1,0:T(8,128)(2,1)S(1)}, u32[]{:S(2)}, u32[]{:S(2)}) collective-permute-start(bf16[16,768]{1,0:T(8,128)(2,1)S(1)} %get-tuple-element.50), channel_id=1, source_target_pairs={{0,256},{256,0},{1,257},{257,1},{2,258},{258,2},{3,259},{259,3},{4... | collective-permute-start | bytes 73736 | tf_op jit(solution)/shard_map/ppermute | solution.py:346

commit v4 on v3

--- a/solution.py
+++ b/solution.py
@@ -42,11 +42,6 @@
         compiler_params=pltpu.CompilerParams(vmem_limit_bytes=mib * 1024 * 1024),
         cost_estimate=pl.CostEstimate(flops=int(flops), bytes_accessed=int(moved), transcendentals=0),
     )
-
-
-def text_body(text_ref, out_ref):
-    unit, _ = unit_rows(text_ref[...].astype(F32))
-    out_ref[...] = jnp.broadcast_to(unit[None], out_ref.shape).astype(BF16)
 
 
 def pool(counts_ref, embed, query):
@@ -76,13 +71,20 @@
 
 
 def pool_body(
-    query_ref, counts_hbm, clips_hbm, rows_hbm, payload_ref, counts_ref, clips_ref, rows_ref, sems
+    query_hbm, counts_hbm, clips_hbm, rows_hbm, text_hbm, payload_ref, send_ref,
+    query_ref, counts_ref, clips_ref, rows_ref, text_ref, sems,
 ):
-    fetch((counts_hbm, clips_hbm, rows_hbm), (counts_ref, clips_ref, rows_ref), sems)
+    fetch(
+        (query_hbm, counts_hbm, clips_hbm, rows_hbm, text_hbm),
+        (query_ref, counts_ref, clips_ref, rows_ref, text_ref),
+        sems,
+    )
+    unit, _ = unit_rows(text_ref[...].astype(F32))
+    send_ref[...] = jnp.broadcast_to(unit[None], send_ref.shape).astype(BF16)
     n_loc, _, width = clips_ref.shape
     w_rows, joint = rows_ref.shape
     w_pad = payload_ref.shape[0] - 2 * n_loc
-    _, summary = pool(counts_ref, clips_ref[...].astype(F32), query_ref[...].astype(F32))
+    _, summary = pool(counts_ref, clips_ref[...].astype(F32), query_ref[...].astype(F32).reshape(1, width))
     high = jnp.concatenate(
         [summary[:, joint:], jnp.zeros((n_loc, 2 * joint - width), F32)], axis=1
     )
@@ -93,12 +95,16 @@
 
 
 def clips_body(
-    d_own_ref, query_ref, counts_hbm, clips_hbm, weight_hbm, out_ref,
-    counts_ref, clips_ref, weight_ref, sems,
+    d_own_ref, query_hbm, counts_hbm, clips_hbm, weight_hbm, out_ref,
+    query_ref, counts_ref, clips_ref, weight_ref, sems,
 ):
-    fetch((counts_hbm, clips_hbm, weight_hbm), (counts_ref, clips_ref, weight_ref), sems)
+    fetch(
+        (query_hbm, counts_hbm, clips_hbm, weight_hbm),
+        (query_ref, counts_ref, clips_ref, weight_ref),
+        sems,
+    )
     embed = clips_ref[...].astype(F32)
-    query = query_ref[...].astype(F32)
+    query = query_ref[...].astype(F32).reshape(1, embed.shape[2])
     weights, summary = pool(counts_ref, embed, query)
     d_summary = dot(d_own_ref[...], weight_ref[...], ((1,), (1,)))
     aligned = jnp.sum(embed * d_summary[:, None, :], axis=2, keepdims=True)
@@ -259,24 +265,28 @@
     plane_id = lax.axis_index(PLANE)
     lane_id = lax.axis_index(CLIP)
     group_id = lax.axis_index(DP)
-    (text_send,) = local(text_body, [((n_dp, n_loc, joint), BF16)], 0, 1)(text_embed)
-    text_own = exchange(text_send, DP).reshape(n_lane, joint)
-    text_other = lax.ppermute(text_own, "core", SWAP)
-
     w_pad = -(-w_rows // 16) * 16
-    query = pool_query.reshape(1, width)
     stage = [
+        pltpu.VMEM((width,), BF16),
         pltpu.SMEM((n_loc,), jnp.int32),
         pltpu.VMEM((n_loc, n_clips, width), BF16),
     ]
-    (payload,) = local(
+    payload, text_send = local(
         pool_body,
-        [((w_pad + 2 * n_loc, joint), BF16)],
+        [((w_pad + 2 * n_loc, joint), BF16), ((n_dp, n_loc, joint), BF16)],
         0,
-        1,
-        3,
-        scratch=stage + [pltpu.VMEM((w_rows, joint), BF16), pltpu.SemaphoreType.DMA((3,))],
-    )(query, clip_counts, clip_embed, proj_weight)
+        0,
+        5,
+        scratch=stage
+        + [
+            pltpu.VMEM((w_rows, joint), BF16),
+            pltpu.VMEM((n_loc, joint), BF16),
+            pltpu.SemaphoreType.DMA((5,)),
+        ],
+        mib=56,
+    )(pool_query, clip_counts, clip_embed, proj_weight, text_embed)
+    text_own = exchange(text_send, DP).reshape(n_lane, joint)
+    text_other = lax.ppermute(text_own, "core", SWAP)
 
     near = [payload] + [
         lax.ppermute(payload, "yl", [(i, i ^ k) for i in range(n_yl)]) for k in range(1, n_yl)
@@ -349,12 +359,12 @@
         clips_body,
         [((n_loc, n_clips, width), BF16)],
         0,
-        2,
-        3,
-        scratch=stage + [pltpu.VMEM((width, joint), BF16), pltpu.SemaphoreType.DMA((3,))],
+        1,
+        4,
+        scratch=stage + [pltpu.VMEM((width, joint), BF16), pltpu.SemaphoreType.DMA((4,))],
         flops=2e7,
         moved=3e6,
-    )(d_own, query, clip_counts, clip_embed, full_weight)
+    )(d_own, pool_query, clip_counts, clip_embed, full_weight)
     piece_send, d_texts = local(
         yh_sum_body, [((n_z, spare, joint), F32), ((n_loc, joint), F32)], 0, 3
     )(here, got_yh, text_embed)

time: 173 us -> 170 us (0.983)
  local copies, waits for them, and re-layouts: 7.22 us -> 3.28 us
  blocking collectives: 104 us -> 102 us
    unnamed x24 -> x14, local copies, waits for them, and re-layouts: 4.62 us -> 1.39 us
    all_to_all x1, waiting for transfers between devices: 0.01 us -> 2.31 us  [exchange(): return lax.all_to_all(blocks, axes, split_axis=0, concat_axis=0, tiled=True)]
    pallas_call x3 -> x2, Pallas kernels: 3.78 us -> 4.21 us  [the longest x1 2.16 us: shards(): local(clips_body, [((n_loc, n_clips, width), BF16)], 0, 1, 4, scratch=sta...]
  transfers between devices with their start and end apart: 8 -> 8, of which waited for: 3 -> 4; matrix products, arithmetic and copies ran while one was open for 1% -> 2% of each run, Pallas kernels for 2% -> 1%
where the time goes in v4:
time: 170 us; the launch traced here: 169 us
  blocking collectives  102 us (60%)
  starting transfers between devices  43.7 us (26%)
  Pallas kernels  8.75 us (5%)
  waiting for transfers between devices  8.14 us (5%)
  local copies, waits for them, and re-layouts  3.28 us (2%)
    all_to_all x7, blocking collectives, exchange(): return lax.all_to_all(blocks, axes, split_axis=0, concat_axis=0, tiled=True)  102 us
    all_to_all x1, starting transfers between devices, exchange(): return lax.all_to_all(blocks, axes, split_axis=0, concat_axis=0, tiled=True)  16.2 us
    ppermute x3, starting transfers between devices, shards(): lax.ppermute(payload, 'yl', [(i, i ^ k) for i in range(n_yl)])  9.27 us
    ppermute x1, starting transfers between devices, shards(): d_half_other = lax.ppermute(d_half, 'core', SWAP)  7.53 us
    ppermute x1, starting transfers between devices, shards(): over_x_other = lax.ppermute(over_x, 'core', SWAP)  4.67 us
    ppermute x1, waiting for transfers between devices, shards(): got_yh = lax.ppermute(away, 'yh', SWAP)  4.07 us
    ppermute x1, starting transfers between devices, shards(): text_other = lax.ppermute(text_own, 'core', SWAP)  3.8 us
  transfers between devices with their start and end apart: 8, of which 4 were waited for; matrix products, arithmetic and copies ran while one was open for 2% of the time, Pallas kernels for 1%

profile of v4, /device:TPU:1, one launch (start us, length us, event | category | flops | bytes accessed | tf_op | source)
XLA Modules:
  0.0 168.6 jit_solution(111646848573059000)
XLA Ops:
  0.6 2.0 %shard_map.94 = (bf16[64,768]{1,0:T(8,128)(2,1)}, bf16[16,8,768]{2,1,0:T(8,128)(2,1)}) custom-call(bf16[1408]{0:T(1024)(128)(2,1)} %query_hbm.3, s32[8]{0:T(128)} %counts_hbm.3, bf16[8,16,1408]{2,1,0:T(8,128)(2,1)} %clips_hbm.3, bf16[44,768]{1,0:T(8,128)(2,1)} %rows_hbm.1, bf16[8,768]{1,0:T(8,128)(2,1)} %text_ref.1), custom_call_target="tpu_custom_call" | custom-call | flops 1000000 | bytes 1000000 | tf_op jit(solution)/shard_map/pallas_call | solution.py:274
  2.7 16.2 %all-to-all-start = ((bf16[16,8,768]{2,1,0:T(8,128)(2,1)}), bf16[16,8,768]{2,1,0:T(8,128)(2,1)S(1)}, u32[]{:S(2)}, u32[]{:S(2)}) async-start(bf16[16,8,768]{2,1,0:T(8,128)(2,1)} %get-tuple-element.33), calls=%async_computation | async-start | bytes 393216 | tf_op jit(solution)/shard_map/all_to_all | solution.py:25
  18.9 2.3 %collective-permute-start = (bf16[64,768]{1,0:T(8,128)(2,1)}, bf16[64,768]{1,0:T(8,128)(2,1)S(1)}, u32[]{:S(2)}, u32[]{:S(2)}) collective-permute-start(bf16[64,768]{1,0:T(8,128)(2,1)} %get-tuple-element.32), channel_id=1, source_target_pairs={{0,8},{8,0},{16,24},{24,16},{1,9},{9,1},{17,25},{25,17},{2,10},{10... | collective-permute-start | bytes 294920 | tf_op jit(solution)/shard_map/ppermute | solution.py:292
  21.2 2.4 %collective-permute-start.1 = (bf16[64,768]{1,0:T(8,128)(2,1)}, bf16[64,768]{1,0:T(8,128)(2,1)S(1)}, u32[]{:S(2)}, u32[]{:S(2)}) collective-permute-start(bf16[64,768]{1,0:T(8,128)(2,1)} %get-tuple-element.32), channel_id=1, source_target_pairs={{0,16},{8,24},{16,0},{24,8},{1,17},{9,25},{17,1},{25,9},{2,18},{10... | collective-permute-start | bytes 294920 | tf_op jit(solution)/shard_map/ppermute | solution.py:292
  23.7 4.5 %collective-permute-start.2 = (bf16[64,768]{1,0:T(8,128)(2,1)}, bf16[64,768]{1,0:T(8,128)(2,1)S(1)}, u32[]{:S(2)}, u32[]{:S(2)}) collective-permute-start(bf16[64,768]{1,0:T(8,128)(2,1)} %get-tuple-element.32), channel_id=1, source_target_pairs={{0,24},{8,16},{16,8},{24,0},{1,25},{9,17},{17,9},{25,1},{2,26},{10... | collective-permute-start | bytes 294920 | tf_op jit(solution)/shard_map/ppermute | solution.py:292
  28.2 2.3 %all-to-all-done = bf16[16,8,768]{2,1,0:T(8,128)(2,1)S(1)} async-done(((bf16[16,8,768]{2,1,0:T(8,128)(2,1)}), bf16[16,8,768]{2,1,0:T(8,128)(2,1)S(1)}, u32[]{:S(2)}, u32[]{:S(2)}) %all-to-all-start) | async-done | bytes 196640 | tf_op jit(solution)/shard_map/all_to_all | solution.py:25
  30.5 3.8 %collective-permute-start.3 = (bf16[128,768]{1,0:T(8,128)(2,1)S(1)}, bf16[128,768]{1,0:T(8,128)(2,1)S(1)}, u32[]{:S(2)}, u32[]{:S(2)}) collective-permute-start(bf16[128,768]{1,0:T(8,128)(2,1)S(1)} %bitcast.7), channel_id=1, source_target_pairs={{0,1},{1,0},{2,3},{3,2},{4,5},{5,4},{6,7},{7,6},{8,9},{9,8},{10,11... | collective-permute-start | bytes 589832 | tf_op jit(solution)/shard_map/ppermute | solution.py:289
  34.5 0.9 pad_maximum_fusion
  35.6 22.7 %all_to_all.40.own_ref = bf16[4,4,64,768]{3,2,1,0:T(8,128)(2,1)S(1)} all-to-all(bf16[4,4,64,768]{3,2,1,0:T(8,128)(2,1)S(1)} %broadcast_in_dim.2), channel_id=1, replica_groups=mesh['yh'=2,'z'=8,'yl'=4,'x'=4,'core'=2] {'x'}, dimensions={0} | all-to-all | bytes 3145728 | tf_op jit(solution)/shard_map/all_to_all | solution.py:25
  58.3 4.7 %collective-permute-start.4 = (bf16[4,4,64,768]{3,2,1,0:T(8,128)(2,1)S(1)}, bf16[4,4,64,768]{3,2,1,0:T(8,128)(2,1)S(1)}, u32[]{:S(2)}, u32[]{:S(2)}) collective-permute-start(bf16[4,4,64,768]{3,2,1,0:T(8,128)(2,1)S(1)} %all_to_all.40.own_ref), channel_id=1, source_target_pairs={{0,1},{1,0},{2,3},{3,2},{4,5},{5,4},{6,7},{7,6},{8,9},{9,8},{10,11... | collective-permute-start | bytes 4718600 | tf_op jit(solution)/shard_map/ppermute | solution.py:299
  64.3 1.6 collective-permute-done.4.other_ref
  66.0 2.1 %shard_map.95 = (bf16[1408,768]{1,0:T(8,128)(2,1)S(1)}, bf16[256,1408]{1,0:T(8,128)(2,1)S(1)}, bf16[256,768]{1,0:T(8,128)(2,1)S(1)}, f32[8,768]{1,0:T(8,128)S(1)...) custom-call(f32[1]{0:T(128)S(6)} %copy.10.scale_ref, ...), custom_call_target="tpu_custom_call" | custom-call | flops 700000000 | bytes 8000000 | tf_op jit(solution)/shard_map/pallas_call | solution.py:301
  68.1 1.4 copy-done
  69.5 11.2 %all_to_all.41.rows_ref = f32[16,1,256]{2,1,0:T(1,128)S(1)} all-to-all(f32[16,1,256]{2,1,0:T(1,128)S(1)} %get-tuple-element.38), channel_id=1, replica_groups=mesh['yh'=2,'z'=8,'yl'=4,'x'=4,'core'=2] {'yl','x'}, dimensions={0} | all-to-all | bytes 32768 | tf_op jit(solution)/shard_map/all_to_all | solution.py:25
  80.7 20.2 %all_to_all.42.cols_ref = f32[16,1,256]{2,1,0:T(1,128)S(1)} all-to-all(f32[16,1,256]{2,1,0:T(1,128)S(1)} %get-tuple-element.39), channel_id=1, replica_groups=mesh['yh'=2,'z'=8,'yl'=4,'x'=4,'core'=2] {'yh','z'}, dimensions={0} | all-to-all | bytes 32768 | tf_op jit(solution)/shard_map/all_to_all | solution.py:25
  101.5 11.0 %all_to_all.43.part_ref = bf16[16,8,768]{2,1,0:T(8,128)(2,1)S(1)} all-to-all(bf16[16,8,768]{2,1,0:T(8,128)(2,1)S(1)} %bitcast.12), channel_id=1, replica_groups=mesh['yh'=2,'z'=8,'yl'=4,'x'=4,'core'=2] {'yl','x'}, dimensions={0} | all-to-all | bytes 393216 | tf_op jit(solution)/shard_map/all_to_all | solution.py:25
  112.7 10.9 %all_to_all.44 = bf16[16,8,768]{2,1,0:T(8,128)(2,1)S(1)} all-to-all(bf16[16,8,768]{2,1,0:T(8,128)(2,1)S(1)} %get-tuple-element.44), channel_id=1, replica_groups=mesh['yh'=2,'z'=8,'yl'=4,'x'=4,'core'=2] {'yl','x'}, dimensions={0} | all-to-all | bytes 393216 | tf_op jit(solution)/shard_map/all_to_all | solution.py:25
  123.6 7.5 %collective-permute-start.5 = (bf16[128,768]{1,0:T(8,128)(2,1)S(1)}, bf16[128,768]{1,0:T(8,128)(2,1)S(1)}, u32[]{:S(2)}, u32[]{:S(2)}) collective-permute-start(bf16[128,768]{1,0:T(8,128)(2,1)S(1)} %bitcast.10), channel_id=1, source_target_pairs={{0,1},{1,0},{2,3},{3,2},{4,5},{5,4},{6,7},{7,6},{8,9},{9,8},{10,11... | collective-permute-start | bytes 589832 | tf_op jit(solution)/shard_map/ppermute | solution.py:342
  131.1 1.0 constant_dynamic-slice_fusion
  132.4 15.0 %all_to_all.45.got_ref = bf16[8,24,768]{2,1,0:T(8,128)(2,1)S(1)} all-to-all(bf16[8,24,768]{2,1,0:T(8,128)(2,1)S(1)} %shard_map.98), channel_id=1, replica_groups=mesh['yh'=2,'z'=8,'yl'=4,'x'=4,'core'=2] {'z'}, dimensions={0} | all-to-all | bytes 589824 | tf_op jit(solution)/shard_map/all_to_all | solution.py:25
  147.5 2.2 %collective-permute-start.6 = (bf16[16,768]{1,0:T(8,128)(2,1)S(1)}, bf16[16,768]{1,0:T(8,128)(2,1)S(1)}, u32[]{:S(2)}, u32[]{:S(2)}) collective-permute-start(bf16[16,768]{1,0:T(8,128)(2,1)S(1)} %get-tuple-element.54), channel_id=1, source_target_pairs={{0,256},{256,0},{1,257},{257,1},{2,258},{258,2},{3,259},{259,3},{4... | collective-permute-start | bytes 73736 | tf_op jit(solution)/shard_map/ppermute | solution.py:356
  149.8 2.2 %shard_map.101 = bf16[8,16,1408]{2,1,0:T(8,128)(2,1)} custom-call(bf16[8,768]{1,0:T(8,128)(2,1)S(1)} %get-tuple-element.56.d_own_ref, bf16[1408]{0:T(1024)(128)(2,1)S(1)} %copy-done.4, s32[8]{0:T(128)S(1)} %copy-done.6, bf16[8,16,1408]{2,1,0:T(8,128)(2,1)S(1)} %copy-done.2, bf16[1408,768]{1,0:T(8,128)(2,1)S(1)} %copy-done.1), custom_call_target="tpu_custom_call" | custom-call | flops 20000000 | bytes 3000000 | tf_op jit(solution)/shard_map/pallas_call | solution.py:358
  151.9 4.1 %collective-permute-done.6.got_ref = bf16[16,768]{1,0:T(8,128)(2,1)S(1)} collective-permute-done((bf16[16,768]{1,0:T(8,128)(2,1)S(1)}, bf16[16,768]{1,0:T(8,128)(2,1)S(1)}, u32[]{:S(2)}, u32[]{:S(2)}) %collective-permute-start.6) | collective-permute-done | bytes 24608 | tf_op jit(solution)/shard_map/ppermute | solution.py:356
  156.8 11.1 %all_to_all.46.got_ref = f32[8,8,768]{2,1,0:T(8,128)S(1)} all-to-all(f32[8,8,768]{2,1,0:T(8,128)S(1)} %get-tuple-element.59), channel_id=1, replica_groups=mesh['yh'=2,'z'=8,'yl'=4,'x'=4,'core'=2] {'z'}, dimensions={0} | all-to-all | bytes 393216 | tf_op jit(solution)/shard_map/all_to_all | solution.py:25
  (27 shorter events, 3.5 us)
Async XLA Ops:
  2.7 27.9 %all-to-all-start = ((bf16[16,8,768]{2,1,0:T(8,128)(2,1)}), bf16[16,8,768]{2,1,0:T(8,128)(2,1)S(1)}, u32[]{:S(2)}, u32[]{:S(2)}) async-start(bf16[16,8,768]{2,1,0:T(8,128)(2,1)} %get-tuple-element.33), calls=%async_computation | async-start | bytes 393216 | tf_op jit(solution)/shard_map/all_to_all | solution.py:25
  18.9 15.4 %collective-permute-start = (bf16[64,768]{1,0:T(8,128)(2,1)}, bf16[64,768]{1,0:T(8,128)(2,1)S(1)}, u32[]{:S(2)}, u32[]{:S(2)}) collective-permute-start(bf16[64,768]{1,0:T(8,128)(2,1)} %get-tuple-element.32), channel_id=1, source_target_pairs={{0,8},{8,0},{16,24},{24,16},{1,9},{9,1},{17,25},{25,17},{2,10},{10... | collective-permute-start | bytes 294920 | tf_op jit(solution)/shard_map/ppermute | solution.py:292
  21.2 13.2 %collective-permute-start.1 = (bf16[64,768]{1,0:T(8,128)(2,1)}, bf16[64,768]{1,0:T(8,128)(2,1)S(1)}, u32[]{:S(2)}, u32[]{:S(2)}) collective-permute-start(bf16[64,768]{1,0:T(8,128)(2,1)} %get-tuple-element.32), channel_id=1, source_target_pairs={{0,16},{8,24},{16,0},{24,8},{1,17},{9,25},{17,1},{25,9},{2,18},{10... | collective-permute-start | bytes 294920 | tf_op jit(solution)/shard_map/ppermute | solution.py:292
  23.7 10.8 %collective-permute-start.2 = (bf16[64,768]{1,0:T(8,128)(2,1)}, bf16[64,768]{1,0:T(8,128)(2,1)S(1)}, u32[]{:S(2)}, u32[]{:S(2)}) collective-permute-start(bf16[64,768]{1,0:T(8,128)(2,1)} %get-tuple-element.32), channel_id=1, source_target_pairs={{0,24},{8,16},{16,8},{24,0},{1,25},{9,17},{17,9},{25,1},{2,26},{10... | collective-permute-start | bytes 294920 | tf_op jit(solution)/shard_map/ppermute | solution.py:292
  30.5 4.9 %collective-permute-start.3 = (bf16[128,768]{1,0:T(8,128)(2,1)S(1)}, bf16[128,768]{1,0:T(8,128)(2,1)S(1)}, u32[]{:S(2)}, u32[]{:S(2)}) collective-permute-start(bf16[128,768]{1,0:T(8,128)(2,1)S(1)} %bitcast.7), channel_id=1, source_target_pairs={{0,1},{1,0},{2,3},{3,2},{4,5},{5,4},{6,7},{7,6},{8,9},{9,8},{10,11... | collective-permute-start | bytes 589832 | tf_op jit(solution)/shard_map/ppermute | solution.py:289
  58.3 7.7 %collective-permute-start.4 = (bf16[4,4,64,768]{3,2,1,0:T(8,128)(2,1)S(1)}, bf16[4,4,64,768]{3,2,1,0:T(8,128)(2,1)S(1)}, u32[]{:S(2)}, u32[]{:S(2)}) collective-permute-start(bf16[4,4,64,768]{3,2,1,0:T(8,128)(2,1)S(1)} %all_to_all.40.own_ref), channel_id=1, source_target_pairs={{0,1},{1,0},{2,3},{3,2},{4,5},{5,4},{6,7},{7,6},{8,9},{9,8},{10,11... | collective-permute-start | bytes 4718600 | tf_op jit(solution)/shard_map/ppermute | solution.py:299
  68.1 1.4 copy-start
  69.5 54.1 %copy-start.5 = (bf16[256,1408]{1,0:T(8,128)(2,1)}, bf16[256,1408]{1,0:T(8,128)(2,1)S(1)}, u32[]{:S(2)}) copy-start(bf16[256,1408]{1,0:T(8,128)(2,1)S(1)} %get-tuple-element.47) | copy-start | bytes 2162692
  101.5 48.2 %copy-start.1 = (bf16[1408,768]{1,0:T(8,128)(2,1)S(1)}, bf16[1408,768]{1,0:T(8,128)(2,1)}, u32[]{:S(2)}) copy-start(bf16[1408,768]{1,0:T(8,128)(2,1)} %copy-done) | copy-start | bytes 6488068
  101.5 48.2 %copy-start.2 = (bf16[8,16,1408]{2,1,0:T(8,128)(2,1)S(1)}, bf16[8,16,1408]{2,1,0:T(8,128)(2,1)}, u32[]{:S(2)}) copy-start(bf16[8,16,1408]{2,1,0:T(8,128)(2,1)} %clips_hbm.3) | copy-start | bytes 1081348
  101.5 48.2 %copy-start.4 = (bf16[1408]{0:T(1024)(128)(2,1)S(1)}, bf16[1408]{0:T(1024)(128)(2,1)}, u32[]{:S(2)}) copy-start(bf16[1408]{0:T(1024)(128)(2,1)} %query_hbm.3) | copy-start | bytes 8452
  101.5 48.2 %copy-start.6 = (s32[8]{0:T(128)S(1)}, s32[8]{0:T(128)}, u32[]{:S(2)}) copy-start(s32[8]{0:T(128)} %counts_hbm.3) | copy-start | bytes 100
  123.6 8.6 %collective-permute-start.5 = (bf16[128,768]{1,0:T(8,128)(2,1)S(1)}, bf16[128,768]{1,0:T(8,128)(2,1)S(1)}, u32[]{:S(2)}, u32[]{:S(2)}) collective-permute-start(bf16[128,768]{1,0:T(8,128)(2,1)S(1)} %bitcast.10), channel_id=1, source_target_pairs={{0,1},{1,0},{2,3},{3,2},{4,5},{5,4},{6,7},{7,6},{8,9},{9,8},{10,11... | collective-permute-start | bytes 589832 | tf_op jit(solution)/shard_map/ppermute | solution.py:342
  147.5 8.5 %copy-start.3 = (bf16[8,768]{1,0:T(8,128)(2,1)S(1)}, bf16[8,768]{1,0:T(8,128)(2,1)}, u32[]{:S(2)}) copy-start(bf16[8,768]{1,0:T(8,128)(2,1)} %text_ref.1) | copy-start | bytes 36868
  147.5 8.5 %collective-permute-start.6 = (bf16[16,768]{1,0:T(8,128)(2,1)S(1)}, bf16[16,768]{1,0:T(8,128)(2,1)S(1)}, u32[]{:S(2)}, u32[]{:S(2)}) collective-permute-start(bf16[16,768]{1,0:T(8,128)(2,1)S(1)} %get-tuple-element.54), channel_id=1, source_target_pairs={{0,256},{256,0},{1,257},{257,1},{2,258},{258,2},{3,259},{259,3},{4... | collective-permute-start | bytes 73736 | tf_op jit(solution)/shard_map/ppermute | solution.py:356

commit v5 on v4

--- a/solution.py
+++ b/solution.py
@@ -119,7 +119,7 @@
 
 def logits_body(
     n_loc, w_rows, scale_ref, own_ref, other_ref, text_own_ref, text_other_ref,
-    _, weight_ref, summary_ref, video_ref, unit_ref, norm_ref, expo_ref, rows_ref, cols_ref,
+    _, weight_ref, summary_ref, video_ref, unit_ref, norm_ref, expo_ref, send_ref,
     weight_f, summary_f, unit_f, norm_f,
 ):
     n_x, n_yl, _, joint = own_ref.shape
@@ -160,17 +160,24 @@
     expo = expo_ref[...]
     row_part = jnp.broadcast_to(jnp.sum(expo, axis=1, keepdims=True), (2 * half, 128)).T[:1]
     col_part = jnp.sum(expo, axis=0, keepdims=True)
-    rows_ref[...] = jnp.broadcast_to(row_part[None], rows_ref.shape)
-    cols_ref[...] = jnp.broadcast_to(col_part[None], cols_ref.shape)
+    send_ref[...] = jnp.broadcast_to(jnp.where(first, row_part, col_part)[None], send_ref.shape)
+
+
+def totals_body(got_ref, out_ref):
+    out_ref[...] = jnp.broadcast_to(jnp.sum(got_ref[...], axis=0), out_ref.shape)
 
 
 def grad_body(
-    n_loc, n_clip, scale_ref, expo_ref, rows_ref, cols_ref, pairs_ref, text_own_ref,
+    n_loc, n_clip, scale_ref, expo_ref, totals_ref, totals_other_ref, pairs_ref, text_own_ref,
     text_other_ref, video_ref, part_ref, text_part_ref, grad_ref,
 ):
     n_lane = text_own_ref.shape[0]
-    rows = jnp.sum(rows_ref[...], axis=0)
-    cols = jnp.sum(cols_ref[...], axis=0)
+    own = totals_ref[:1]
+    other = totals_other_ref[:1]
+    first = lax.axis_index("core") == 0
+    swapped = jnp.concatenate([other[:, n_lane:], other[:, :n_lane]], axis=1)
+    rows = jnp.where(first, own, other)
+    cols = jnp.where(first, swapped, own)
     core = lax.axis_index("core")
     plane = lax.axis_index("yl") * lax.axis_size("x") + lax.axis_index("x")
     at = lax.broadcasted_iota(jnp.int32, (1, 2 * n_lane), 1)
@@ -238,18 +245,18 @@
     away_ref[...] = jnp.concatenate([total[n_loc : 2 * n_loc], piece], axis=0).astype(BF16)
 
 
-def yh_sum_body(here_ref, got_ref, text_ref, out_ref, d_texts_ref):
+def yh_sum_body(n_loc, here_ref, got_ref, out_ref, text_ref):
     total = here_ref[...] + got_ref[...].astype(F32)
-    n_loc = text_ref.shape[0]
-    unit, norm = unit_rows(text_ref[...].astype(F32))
-    d_text = total[:n_loc]
-    d_texts_ref[...] = (d_text - unit * jnp.sum(unit * d_text, axis=1, keepdims=True)) / norm
+    text_ref[...] = total[:n_loc]
     out_ref[...] = jnp.broadcast_to(total[None, n_loc:], out_ref.shape)
 
 
-def last_body(piece, got_ref, out_ref):
+def last_body(piece, got_ref, d_text_ref, text_ref, out_ref, d_texts_ref):
     rows = [got_ref[z, :piece, :] for z in range(got_ref.shape[0])]
     out_ref[...] = jnp.concatenate(rows, axis=0)[: out_ref.shape[0]]
+    unit, norm = unit_rows(text_ref[...].astype(F32))
+    d_text = d_text_ref[...]
+    d_texts_ref[...] = (d_text - unit * jnp.sum(unit * d_text, axis=1, keepdims=True)) / norm
 
 
 def shards(clip_embed, clip_counts, pool_query, proj_weight, text_embed, pair_index, logit_scale):
@@ -298,7 +305,7 @@
     pairs = pair_index.reshape(n_dp, group_rows)
     over_x_other = lax.ppermute(over_x, "core", SWAP)
 
-    full_weight, summaries, video_b, unit_own, norm_own, expo, row_send, col_send = local(
+    full_weight, summaries, video_b, unit_own, norm_own, expo, totals_send = local(
         functools.partial(logits_body, n_loc, w_rows),
         [
             ((width, joint), BF16),
@@ -308,7 +315,6 @@
             ((n_loc, 128), F32),
             ((group_rows, 2 * n_lane), F32),
             ((n_plane, 1, group_rows), F32),
-            ((n_dp, 1, 2 * n_lane), F32),
         ],
         1,
         5,
@@ -322,8 +328,18 @@
         moved=8e6,
         mib=20,
     )(logit_scale, over_x, over_x_other, text_own, text_other, pairs)
-    rows = exchange(row_send, PLANE)
-    cols = exchange(col_send, DP)
+    by_plane = [[(d * n_plane + p) * 2 for p in range(n_plane)] for d in range(n_dp)]
+    by_dp = [[(d * n_plane + p) * 2 + 1 for d in range(n_dp)] for p in range(n_plane)]
+    got_totals = lax.all_to_all(
+        totals_send,
+        DP + CLIP,
+        split_axis=0,
+        concat_axis=0,
+        tiled=True,
+        axis_index_groups=by_plane + by_dp,
+    )
+    (totals,) = local(totals_body, [((8, group_rows), F32)], 0, 1)(got_totals)
+    totals_other = lax.ppermute(totals, "core", SWAP)
 
     video_part, text_part = local(
         functools.partial(grad_body, n_loc, n_clip),
@@ -332,7 +348,7 @@
         7,
         scratch=[pltpu.VMEM((group_rows, 2 * n_lane), BF16)],
         flops=2e8,
-    )(logit_scale, expo, rows, cols, pairs, text_own, text_other, video_b)
+    )(logit_scale, expo, totals, totals_other, pairs, text_own, text_other, video_b)
 
     got_video = exchange(video_part.reshape(n_plane, n_loc, joint), PLANE)
     d_send, d_own = local(
@@ -365,13 +381,16 @@
         flops=2e7,
         moved=3e6,
     )(d_own, pool_query, clip_counts, clip_embed, full_weight)
-    piece_send, d_texts = local(
-        yh_sum_body, [((n_z, spare, joint), F32), ((n_loc, joint), F32)], 0, 3
-    )(here, got_yh, text_embed)
+    piece_send, d_text = local(
+        functools.partial(yh_sum_body, n_loc),
+        [((n_z, spare, joint), F32), ((n_loc, joint), F32)],
+        0,
+        2,
+    )(here, got_yh)
     piece_send, d_clips = lax.optimization_barrier((piece_send, d_clips))
-    (d_weight,) = local(functools.partial(last_body, piece), [((w_rows, joint), F32)], 0, 1)(
-        exchange(piece_send, "z")
-    )
+    d_weight, d_texts = local(
+        functools.partial(last_body, piece), [((w_rows, joint), F32), ((n_loc, joint), F32)], 0, 3
+    )(exchange(piece_send, "z"), d_text, text_embed)
     return (d_clips, d_weight, d_texts)
 
 

time: 170 us -> 161 us (0.947)
  blocking collectives: 102 us -> 94.6 us
    all_to_all x7 -> x5, blocking collectives: 102 us -> 74.3 us  [exchange(): return lax.all_to_all(blocks, axes, split_axis=0, concat_axis=0, tiled=True)]
    all_to_all x0 -> x1, blocking collectives: none -> 20.3 us  [shards(): lax.all_to_all(totals_send, DP + CLIP, split_axis=0, concat_axis=0, tiled...]
    ppermute x1, starting transfers between devices: 7.53 us -> 4.22 us  [shards(): d_half_other = lax.ppermute(d_half, 'core', SWAP)]
    ppermute x0 -> x1, starting transfers between devices: none -> 1.92 us  [shards(): totals_other = lax.ppermute(totals, 'core', SWAP)]
  transfers between devices with their start and end apart: 8 -> 9, of which waited for: 4 -> 5; matrix products, arithmetic and copies ran while one was open for 2% -> 2% of each run, Pallas kernels for 1% -> 1%
where the time goes in v5:
time: 161 us; the launch traced here: 160 us
  blocking collectives  94.6 us (59%)
  starting transfers between devices  42.3 us (26%)
  waiting for transfers between devices  9.27 us (6%)
  Pallas kernels  8.09 us (5%)
  local copies, waits for them, and re-layouts  3.28 us (2%)
    all_to_all x5, blocking collectives, exchange(): return lax.all_to_all(blocks, axes, split_axis=0, concat_axis=0, tiled=True)  74.3 us
    all_to_all x1, blocking collectives, shards(): lax.all_to_all(totals_send, DP + CLIP, split_axis=0, concat_axis=0, tiled...  20.3 us
    all_to_all x1, starting transfers between devices, exchange(): return lax.all_to_all(blocks, axes, split_axis=0, concat_axis=0, tiled=True)  16.2 us
    ppermute x3, starting transfers between devices, shards(): lax.ppermute(payload, 'yl', [(i, i ^ k) for i in range(n_yl)])  9.27 us
    ppermute x1, starting transfers between devices, shards(): over_x_other = lax.ppermute(over_x, 'core', SWAP)  4.67 us
    ppermute x1, starting transfers between devices, shards(): d_half_other = lax.ppermute(d_half, 'core', SWAP)  4.22 us
    ppermute x1, waiting for transfers between devices, shards(): got_yh = lax.ppermute(away, 'yh', SWAP)  4.05 us
    ppermute x1, starting transfers between devices, shards(): text_other = lax.ppermute(text_own, 'core', SWAP)  3.8 us
  transfers between devices with their start and end apart: 9, of which 5 were waited for; matrix products, arithmetic and copies ran while one was open for 2% of the time, Pallas kernels for 1%

profile of v5, /device:TPU:1, one launch (start us, length us, event | category | flops | bytes accessed | tf_op | source)
XLA Modules:
  0.0 160.0 jit_solution(17109139007367481934)
XLA Ops:
  0.6 2.0 %shard_map.94 = (bf16[64,768]{1,0:T(8,128)(2,1)}, bf16[16,8,768]{2,1,0:T(8,128)(2,1)}) custom-call(bf16[1408]{0:T(1024)(128)(2,1)} %query_hbm.3, s32[8]{0:T(128)} %counts_hbm.3, bf16[8,16,1408]{2,1,0:T(8,128)(2,1)} %clips_hbm.3, bf16[44,768]{1,0:T(8,128)(2,1)} %rows_hbm.1, bf16[8,768]{1,0:T(8,128)(2,1)} %text_ref.1), custom_call_target="tpu_custom_call" | custom-call | flops 1000000 | bytes 1000000 | tf_op jit(solution)/shard_map/pallas_call | solution.py:281
  2.7 16.2 %all-to-all-start = ((bf16[16,8,768]{2,1,0:T(8,128)(2,1)}), bf16[16,8,768]{2,1,0:T(8,128)(2,1)S(1)}, u32[]{:S(2)}, u32[]{:S(2)}) async-start(bf16[16,8,768]{2,1,0:T(8,128)(2,1)} %get-tuple-element.34), calls=%async_computation | async-start | bytes 393216 | tf_op jit(solution)/shard_map/all_to_all | solution.py:25
  18.9 2.3 %collective-permute-start = (bf16[64,768]{1,0:T(8,128)(2,1)}, bf16[64,768]{1,0:T(8,128)(2,1)S(1)}, u32[]{:S(2)}, u32[]{:S(2)}) collective-permute-start(bf16[64,768]{1,0:T(8,128)(2,1)} %get-tuple-element.33), channel_id=1, source_target_pairs={{0,8},{8,0},{16,24},{24,16},{1,9},{9,1},{17,25},{25,17},{2,10},{10... | collective-permute-start | bytes 294920 | tf_op jit(solution)/shard_map/ppermute | solution.py:299
  21.2 2.4 %collective-permute-start.1 = (bf16[64,768]{1,0:T(8,128)(2,1)}, bf16[64,768]{1,0:T(8,128)(2,1)S(1)}, u32[]{:S(2)}, u32[]{:S(2)}) collective-permute-start(bf16[64,768]{1,0:T(8,128)(2,1)} %get-tuple-element.33), channel_id=1, source_target_pairs={{0,16},{8,24},{16,0},{24,8},{1,17},{9,25},{17,1},{25,9},{2,18},{10... | collective-permute-start | bytes 294920 | tf_op jit(solution)/shard_map/ppermute | solution.py:299
  23.7 4.5 %collective-permute-start.2 = (bf16[64,768]{1,0:T(8,128)(2,1)}, bf16[64,768]{1,0:T(8,128)(2,1)S(1)}, u32[]{:S(2)}, u32[]{:S(2)}) collective-permute-start(bf16[64,768]{1,0:T(8,128)(2,1)} %get-tuple-element.33), channel_id=1, source_target_pairs={{0,24},{8,16},{16,8},{24,0},{1,25},{9,17},{17,9},{25,1},{2,26},{10... | collective-permute-start | bytes 294920 | tf_op jit(solution)/shard_map/ppermute | solution.py:299
  28.2 2.3 %all-to-all-done = bf16[16,8,768]{2,1,0:T(8,128)(2,1)S(1)} async-done(((bf16[16,8,768]{2,1,0:T(8,128)(2,1)}), bf16[16,8,768]{2,1,0:T(8,128)(2,1)S(1)}, u32[]{:S(2)}, u32[]{:S(2)}) %all-to-all-start) | async-done | bytes 196640 | tf_op jit(solution)/shard_map/all_to_all | solution.py:25
  30.5 3.8 %collective-permute-start.3 = (bf16[128,768]{1,0:T(8,128)(2,1)S(1)}, bf16[128,768]{1,0:T(8,128)(2,1)S(1)}, u32[]{:S(2)}, u32[]{:S(2)}) collective-permute-start(bf16[128,768]{1,0:T(8,128)(2,1)S(1)} %bitcast.7), channel_id=1, source_target_pairs={{0,1},{1,0},{2,3},{3,2},{4,5},{5,4},{6,7},{7,6},{8,9},{9,8},{10,11... | collective-permute-start | bytes 589832 | tf_op jit(solution)/shard_map/ppermute | solution.py:296
  35.6 22.7 %all_to_all.35.own_ref = bf16[4,4,64,768]{3,2,1,0:T(8,128)(2,1)S(1)} all-to-all(bf16[4,4,64,768]{3,2,1,0:T(8,128)(2,1)S(1)} %broadcast_in_dim.2), channel_id=1, replica_groups=mesh['yh'=2,'z'=8,'yl'=4,'x'=4,'core'=2] {'x'}, dimensions={0} | all-to-all | bytes 3145728 | tf_op jit(solution)/shard_map/all_to_all | solution.py:25
  58.3 4.7 %collective-permute-start.4 = (bf16[4,4,64,768]{3,2,1,0:T(8,128)(2,1)S(1)}, bf16[4,4,64,768]{3,2,1,0:T(8,128)(2,1)S(1)}, u32[]{:S(2)}, u32[]{:S(2)}) collective-permute-start(bf16[4,4,64,768]{3,2,1,0:T(8,128)(2,1)S(1)} %all_to_all.35.own_ref), channel_id=1, source_target_pairs={{0,1},{1,0},{2,3},{3,2},{4,5},{5,4},{6,7},{7,6},{8,9},{9,8},{10,11... | collective-permute-start | bytes 4718600 | tf_op jit(solution)/shard_map/ppermute | solution.py:306
  64.3 1.6 %collective-permute-done.4.other_ref = bf16[4,4,64,768]{3,2,1,0:T(8,128)(2,1)S(1)} collective-permute-done((bf16[4,4,64,768]{3,2,1,0:T(8,128)(2,1)S(1)}, bf16[4,4,64,768]{3,2,1,0:T(8,128)(2,1)S(1)}, u32[]{:S(2)}, u32[]{:S(2)}) %collective-permute-start.4) | collective-permute-done | bytes 1572896 | tf_op jit(solution)/shard_map/ppermute | solution.py:306
  66.0 2.1 %shard_map.95 = (bf16[1408,768]{1,0:T(8,128)(2,1)S(1)}, bf16[256,1408]{1,0:T(8,128)(2,1)S(1)}, bf16[256,768]{1,0:T(8,128)(2,1)S(1)}, f32[8,768]{1,0:T(8,128)S(1)...) custom-call(f32[1]{0:T(128)S(6)} %copy.10.scale_ref, ...), custom_call_target="tpu_custom_call" | custom-call | flops 700000000 | bytes 8000000 | tf_op jit(solution)/shard_map/pallas_call | solution.py:308
  68.1 1.4 copy-done
  69.5 20.3 %all_to_all.36.got_ref = f32[16,1,256]{2,1,0:T(1,128)S(1)} all-to-all(f32[16,1,256]{2,1,0:T(1,128)S(1)} %get-tuple-element.39), channel_id=1, replica_groups={{0,2,4,6,8,10,12,14,16,18,20,22,24,26,28,30},{32,34,36,38,40,42,44,46,4..., dimensions={0} | all-to-all | bytes 32768 | tf_op jit(solution)/shard_map/all_to_all | solution.py:333
  89.8 1.9 %collective-permute-start.5 = (f32[8,256]{1,0:T(8,128)S(1)}, f32[8,256]{1,0:T(8,128)S(1)}, u32[]{:S(2)}, u32[]{:S(2)}) collective-permute-start(f32[8,256]{1,0:T(8,128)S(1)} %shard_map.96.totals_ref), channel_id=1, source_target_pairs={{0,1},{1,0},{2,3},{3,2},{4,5},{5,4},{6,7},{7,6},{8,9},{9,8},{10,11... | collective-permute-start | bytes 24584 | tf_op jit(solution)/shard_map/ppermute | solution.py:342
  91.7 1.1 collective-permute-done.5.totals_other_ref
  93.5 13.4 %all_to_all.37.part_ref = bf16[16,8,768]{2,1,0:T(8,128)(2,1)S(1)} all-to-all(bf16[16,8,768]{2,1,0:T(8,128)(2,1)S(1)} %bitcast.12), channel_id=1, replica_groups=mesh['yh'=2,'z'=8,'yl'=4,'x'=4,'core'=2] {'yl','x'}, dimensions={0} | all-to-all | bytes 393216 | tf_op jit(solution)/shard_map/all_to_all | solution.py:25
  107.0 12.0 %all_to_all.38 = bf16[16,8,768]{2,1,0:T(8,128)(2,1)S(1)} all-to-all(bf16[16,8,768]{2,1,0:T(8,128)(2,1)S(1)} %get-tuple-element.44), channel_id=1, replica_groups=mesh['yh'=2,'z'=8,'yl'=4,'x'=4,'core'=2] {'yl','x'}, dimensions={0} | all-to-all | bytes 393216 | tf_op jit(solution)/shard_map/all_to_all | solution.py:25
  119.0 4.2 %collective-permute-start.6 = (bf16[128,768]{1,0:T(8,128)(2,1)S(1)}, bf16[128,768]{1,0:T(8,128)(2,1)S(1)}, u32[]{:S(2)}, u32[]{:S(2)}) collective-permute-start(bf16[128,768]{1,0:T(8,128)(2,1)S(1)} %bitcast.10), channel_id=1, source_target_pairs={{0,1},{1,0},{2,3},{3,2},{4,5},{5,4},{6,7},{7,6},{8,9},{9,8},{10,11... | collective-permute-start | bytes 589832 | tf_op jit(solution)/shard_map/ppermute | solution.py:358
  123.2 1.0 constant_dynamic-slice_fusion
  124.5 15.0 %all_to_all.39.got_ref = bf16[8,24,768]{2,1,0:T(8,128)(2,1)S(1)} all-to-all(bf16[8,24,768]{2,1,0:T(8,128)(2,1)S(1)} %shard_map.99), channel_id=1, replica_groups=mesh['yh'=2,'z'=8,'yl'=4,'x'=4,'core'=2] {'z'}, dimensions={0} | all-to-all | bytes 589824 | tf_op jit(solution)/shard_map/all_to_all | solution.py:25
  139.6 2.2 %collective-permute-start.7 = (bf16[16,768]{1,0:T(8,128)(2,1)S(1)}, bf16[16,768]{1,0:T(8,128)(2,1)S(1)}, u32[]{:S(2)}, u32[]{:S(2)}) collective-permute-start(bf16[16,768]{1,0:T(8,128)(2,1)S(1)} %get-tuple-element.54), channel_id=1, source_target_pairs={{0,256},{256,0},{1,257},{257,1},{2,258},{258,2},{3,259},{259,3},{4... | collective-permute-start | bytes 73736 | tf_op jit(solution)/shard_map/ppermute | solution.py:372
  141.9 2.2 %shard_map.102 = bf16[8,16,1408]{2,1,0:T(8,128)(2,1)} custom-call(bf16[8,768]{1,0:T(8,128)(2,1)S(1)} %get-tuple-element.56.d_own_ref, bf16[1408]{0:T(1024)(128)(2,1)S(1)} %copy-done.4, s32[8]{0:T(128)S(1)} %copy-done.6, bf16[8,16,1408]{2,1,0:T(8,128)(2,1)S(1)} %copy-done.2, bf16[1408,768]{1,0:T(8,128)(2,1)S(1)} %copy-done.1), custom_call_target="tpu_custom_call" | custom-call | flops 20000000 | bytes 3000000 | tf_op jit(solution)/shard_map/pallas_call | solution.py:374
  144.0 4.1 %collective-permute-done.7.got_ref = bf16[16,768]{1,0:T(8,128)(2,1)S(1)} collective-permute-done((bf16[16,768]{1,0:T(8,128)(2,1)S(1)}, bf16[16,768]{1,0:T(8,128)(2,1)S(1)}, u32[]{:S(2)}, u32[]{:S(2)}) %collective-permute-start.7) | collective-permute-done | bytes 24608 | tf_op jit(solution)/shard_map/ppermute | solution.py:372
  148.1 11.1 %all_to_all.40.got_ref = f32[8,8,768]{2,1,0:T(8,128)S(1)} all-to-all(f32[8,8,768]{2,1,0:T(8,128)S(1)} %get-tuple-element.59), channel_id=1, replica_groups=mesh['yh'=2,'z'=8,'yl'=4,'x'=4,'core'=2] {'z'}, dimensions={0} | all-to-all | bytes 393216 | tf_op jit(solution)/shard_map/all_to_all | solution.py:25
  (29 shorter events, 3.8 us)
Async XLA Ops:
  2.7 27.9 %all-to-all-start = ((bf16[16,8,768]{2,1,0:T(8,128)(2,1)}), bf16[16,8,768]{2,1,0:T(8,128)(2,1)S(1)}, u32[]{:S(2)}, u32[]{:S(2)}) async-start(bf16[16,8,768]{2,1,0:T(8,128)(2,1)} %get-tuple-element.34), calls=%async_computation | async-start | bytes 393216 | tf_op jit(solution)/shard_map/all_to_all | solution.py:25
  18.9 15.4 %collective-permute-start = (bf16[64,768]{1,0:T(8,128)(2,1)}, bf16[64,768]{1,0:T(8,128)(2,1)S(1)}, u32[]{:S(2)}, u32[]{:S(2)}) collective-permute-start(bf16[64,768]{1,0:T(8,128)(2,1)} %get-tuple-element.33), channel_id=1, source_target_pairs={{0,8},{8,0},{16,24},{24,16},{1,9},{9,1},{17,25},{25,17},{2,10},{10... | collective-permute-start | bytes 294920 | tf_op jit(solution)/shard_map/ppermute | solution.py:299
  21.2 13.2 %collective-permute-start.1 = (bf16[64,768]{1,0:T(8,128)(2,1)}, bf16[64,768]{1,0:T(8,128)(2,1)S(1)}, u32[]{:S(2)}, u32[]{:S(2)}) collective-permute-start(bf16[64,768]{1,0:T(8,128)(2,1)} %get-tuple-element.33), channel_id=1, source_target_pairs={{0,16},{8,24},{16,0},{24,8},{1,17},{9,25},{17,1},{25,9},{2,18},{10... | collective-permute-start | bytes 294920 | tf_op jit(solution)/shard_map/ppermute | solution.py:299
  23.7 10.8 %collective-permute-start.2 = (bf16[64,768]{1,0:T(8,128)(2,1)}, bf16[64,768]{1,0:T(8,128)(2,1)S(1)}, u32[]{:S(2)}, u32[]{:S(2)}) collective-permute-start(bf16[64,768]{1,0:T(8,128)(2,1)} %get-tuple-element.33), channel_id=1, source_target_pairs={{0,24},{8,16},{16,8},{24,0},{1,25},{9,17},{17,9},{25,1},{2,26},{10... | collective-permute-start | bytes 294920 | tf_op jit(solution)/shard_map/ppermute | solution.py:299
  30.5 4.9 %collective-permute-start.3 = (bf16[128,768]{1,0:T(8,128)(2,1)S(1)}, bf16[128,768]{1,0:T(8,128)(2,1)S(1)}, u32[]{:S(2)}, u32[]{:S(2)}) collective-permute-start(bf16[128,768]{1,0:T(8,128)(2,1)S(1)} %bitcast.7), channel_id=1, source_target_pairs={{0,1},{1,0},{2,3},{3,2},{4,5},{5,4},{6,7},{7,6},{8,9},{9,8},{10,11... | collective-permute-start | bytes 589832 | tf_op jit(solution)/shard_map/ppermute | solution.py:296
  58.3 7.7 %collective-permute-start.4 = (bf16[4,4,64,768]{3,2,1,0:T(8,128)(2,1)S(1)}, bf16[4,4,64,768]{3,2,1,0:T(8,128)(2,1)S(1)}, u32[]{:S(2)}, u32[]{:S(2)}) collective-permute-start(bf16[4,4,64,768]{3,2,1,0:T(8,128)(2,1)S(1)} %all_to_all.35.own_ref), channel_id=1, source_target_pairs={{0,1},{1,0},{2,3},{3,2},{4,5},{5,4},{6,7},{7,6},{8,9},{9,8},{10,11... | collective-permute-start | bytes 4718600 | tf_op jit(solution)/shard_map/ppermute | solution.py:306
  68.1 1.4 copy-start
  69.5 49.5 %copy-start.5 = (bf16[256,1408]{1,0:T(8,128)(2,1)}, bf16[256,1408]{1,0:T(8,128)(2,1)S(1)}, u32[]{:S(2)}) copy-start(bf16[256,1408]{1,0:T(8,128)(2,1)S(1)} %get-tuple-element.47) | copy-start | bytes 2162692
  89.8 3.1 %collective-permute-start.5 = (f32[8,256]{1,0:T(8,128)S(1)}, f32[8,256]{1,0:T(8,128)S(1)}, u32[]{:S(2)}, u32[]{:S(2)}) collective-permute-start(f32[8,256]{1,0:T(8,128)S(1)} %shard_map.96.totals_ref), channel_id=1, source_target_pairs={{0,1},{1,0},{2,3},{3,2},{4,5},{5,4},{6,7},{7,6},{8,9},{9,8},{10,11... | collective-permute-start | bytes 24584 | tf_op jit(solution)/shard_map/ppermute | solution.py:342
  93.4 48.4 %copy-start.1 = (bf16[1408,768]{1,0:T(8,128)(2,1)S(1)}, bf16[1408,768]{1,0:T(8,128)(2,1)}, u32[]{:S(2)}) copy-start(bf16[1408,768]{1,0:T(8,128)(2,1)} %copy-done) | copy-start | bytes 6488068
  93.4 48.4 %copy-start.2 = (bf16[8,16,1408]{2,1,0:T(8,128)(2,1)S(1)}, bf16[8,16,1408]{2,1,0:T(8,128)(2,1)}, u32[]{:S(2)}) copy-start(bf16[8,16,1408]{2,1,0:T(8,128)(2,1)} %clips_hbm.3) | copy-start | bytes 1081348
  93.4 48.4 %copy-start.4 = (bf16[1408]{0:T(1024)(128)(2,1)S(1)}, bf16[1408]{0:T(1024)(128)(2,1)}, u32[]{:S(2)}) copy-start(bf16[1408]{0:T(1024)(128)(2,1)} %query_hbm.3) | copy-start | bytes 8452
  93.4 48.4 %copy-start.6 = (s32[8]{0:T(128)S(1)}, s32[8]{0:T(128)}, u32[]{:S(2)}) copy-start(s32[8]{0:T(128)} %counts_hbm.3) | copy-start | bytes 100
  119.0 5.3 %collective-permute-start.6 = (bf16[128,768]{1,0:T(8,128)(2,1)S(1)}, bf16[128,768]{1,0:T(8,128)(2,1)S(1)}, u32[]{:S(2)}, u32[]{:S(2)}) collective-permute-start(bf16[128,768]{1,0:T(8,128)(2,1)S(1)} %bitcast.10), channel_id=1, source_target_pairs={{0,1},{1,0},{2,3},{3,2},{4,5},{5,4},{6,7},{7,6},{8,9},{9,8},{10,11... | collective-permute-start | bytes 589832 | tf_op jit(solution)/shard_map/ppermute | solution.py:358
  139.6 8.5 %collective-permute-start.7 = (bf16[16,768]{1,0:T(8,128)(2,1)S(1)}, bf16[16,768]{1,0:T(8,128)(2,1)S(1)}, u32[]{:S(2)}, u32[]{:S(2)}) collective-permute-start(bf16[16,768]{1,0:T(8,128)(2,1)S(1)} %get-tuple-element.54), channel_id=1, source_target_pairs={{0,256},{256,0},{1,257},{257,1},{2,258},{258,2},{3,259},{259,3},{4... | collective-permute-start | bytes 73736 | tf_op jit(solution)/shard_map/ppermute | solution.py:372
  141.8 17.4 %copy-start.3 = (bf16[8,768]{1,0:T(8,128)(2,1)S(1)}, bf16[8,768]{1,0:T(8,128)(2,1)}, u32[]{:S(2)}) copy-start(bf16[8,768]{1,0:T(8,128)(2,1)} %text_ref.1) | copy-start | bytes 36868

commit v6 on v5

--- a/solution.py
+++ b/solution.py
@@ -248,11 +248,11 @@
 def yh_sum_body(n_loc, here_ref, got_ref, out_ref, text_ref):
     total = here_ref[...] + got_ref[...].astype(F32)
     text_ref[...] = total[:n_loc]
-    out_ref[...] = jnp.broadcast_to(total[None, n_loc:], out_ref.shape)
+    out_ref[...] = jnp.broadcast_to(total[None, n_loc:], out_ref.shape).astype(BF16)
 
 
 def last_body(piece, got_ref, d_text_ref, text_ref, out_ref, d_texts_ref):
-    rows = [got_ref[z, :piece, :] for z in range(got_ref.shape[0])]
+    rows = [got_ref[z].astype(F32)[:piece] for z in range(got_ref.shape[0])]
     out_ref[...] = jnp.concatenate(rows, axis=0)[: out_ref.shape[0]]
     unit, norm = unit_rows(text_ref[...].astype(F32))
     d_text = d_text_ref[...]
@@ -383,7 +383,7 @@
     )(d_own, pool_query, clip_counts, clip_embed, full_weight)
     piece_send, d_text = local(
         functools.partial(yh_sum_body, n_loc),
-        [((n_z, spare, joint), F32), ((n_loc, joint), F32)],
+        [((n_z, spare, joint), BF16), ((n_loc, joint), F32)],
         0,
         2,
     )(here, got_yh)

time: 161 us -> 160 us (level)
  no operation moved by 1% of the time
where the time goes in v6:
time: 160 us; the launch traced here: 159 us
  blocking collectives  93.5 us (58%)
  starting transfers between devices  42.3 us (26%)
  waiting for transfers between devices  9.27 us (6%)
  Pallas kernels  8.08 us (5%)
  local copies, waits for them, and re-layouts  3.28 us (2%)
    all_to_all x5, blocking collectives, exchange(): return lax.all_to_all(blocks, axes, split_axis=0, concat_axis=0, tiled=True)  73.2 us
    all_to_all x1, blocking collectives, shards(): lax.all_to_all(totals_send, DP + CLIP, split_axis=0, concat_axis=0, tiled...  20.3 us
    all_to_all x1, starting transfers between devices, exchange(): return lax.all_to_all(blocks, axes, split_axis=0, concat_axis=0, tiled=True)  16.2 us
    ppermute x3, starting transfers between devices, shards(): lax.ppermute(payload, 'yl', [(i, i ^ k) for i in range(n_yl)])  9.27 us
    ppermute x1, starting transfers between devices, shards(): over_x_other = lax.ppermute(over_x, 'core', SWAP)  4.67 us
    ppermute x1, starting transfers between devices, shards(): d_half_other = lax.ppermute(d_half, 'core', SWAP)  4.22 us
    ppermute x1, waiting for transfers between devices, shards(): got_yh = lax.ppermute(away, 'yh', SWAP)  4.05 us
    ppermute x1, starting transfers between devices, shards(): text_other = lax.ppermute(text_own, 'core', SWAP)  3.8 us
  transfers between devices with their start and end apart: 9, of which 5 were waited for; matrix products, arithmetic and copies ran while one was open for 2% of the time, Pallas kernels for 1%

profile of v6, /device:TPU:1, one launch (start us, length us, event | category | flops | bytes accessed | tf_op | source)
XLA Modules:
  0.0 159.0 jit_solution(8942886573644012929)
XLA Ops:
  0.6 2.0 %shard_map.94 = (bf16[64,768]{1,0:T(8,128)(2,1)}, bf16[16,8,768]{2,1,0:T(8,128)(2,1)}) custom-call(bf16[1408]{0:T(1024)(128)(2,1)} %query_hbm.3, s32[8]{0:T(128)} %counts_hbm.3, bf16[8,16,1408]{2,1,0:T(8,128)(2,1)} %clips_hbm.3, bf16[44,768]{1,0:T(8,128)(2,1)} %rows_hbm.1, bf16[8,768]{1,0:T(8,128)(2,1)} %text_ref.1), custom_call_target="tpu_custom_call" | custom-call | flops 1000000 | bytes 1000000 | tf_op jit(solution)/shard_map/pallas_call | solution.py:281
  2.7 16.2 %all-to-all-start = ((bf16[16,8,768]{2,1,0:T(8,128)(2,1)}), bf16[16,8,768]{2,1,0:T(8,128)(2,1)S(1)}, u32[]{:S(2)}, u32[]{:S(2)}) async-start(bf16[16,8,768]{2,1,0:T(8,128)(2,1)} %get-tuple-element.34), calls=%async_computation | async-start | bytes 393216 | tf_op jit(solution)/shard_map/all_to_all | solution.py:25
  18.9 2.3 %collective-permute-start = (bf16[64,768]{1,0:T(8,128)(2,1)}, bf16[64,768]{1,0:T(8,128)(2,1)S(1)}, u32[]{:S(2)}, u32[]{:S(2)}) collective-permute-start(bf16[64,768]{1,0:T(8,128)(2,1)} %get-tuple-element.33), channel_id=1, source_target_pairs={{0,8},{8,0},{16,24},{24,16},{1,9},{9,1},{17,25},{25,17},{2,10},{10... | collective-permute-start | bytes 294920 | tf_op jit(solution)/shard_map/ppermute | solution.py:299
  21.2 2.4 %collective-permute-start.1 = (bf16[64,768]{1,0:T(8,128)(2,1)}, bf16[64,768]{1,0:T(8,128)(2,1)S(1)}, u32[]{:S(2)}, u32[]{:S(2)}) collective-permute-start(bf16[64,768]{1,0:T(8,128)(2,1)} %get-tuple-element.33), channel_id=1, source_target_pairs={{0,16},{8,24},{16,0},{24,8},{1,17},{9,25},{17,1},{25,9},{2,18},{10... | collective-permute-start | bytes 294920 | tf_op jit(solution)/shard_map/ppermute | solution.py:299
  23.7 4.5 %collective-permute-start.2 = (bf16[64,768]{1,0:T(8,128)(2,1)}, bf16[64,768]{1,0:T(8,128)(2,1)S(1)}, u32[]{:S(2)}, u32[]{:S(2)}) collective-permute-start(bf16[64,768]{1,0:T(8,128)(2,1)} %get-tuple-element.33), channel_id=1, source_target_pairs={{0,24},{8,16},{16,8},{24,0},{1,25},{9,17},{17,9},{25,1},{2,26},{10... | collective-permute-start | bytes 294920 | tf_op jit(solution)/shard_map/ppermute | solution.py:299
  28.2 2.3 %all-to-all-done = bf16[16,8,768]{2,1,0:T(8,128)(2,1)S(1)} async-done(((bf16[16,8,768]{2,1,0:T(8,128)(2,1)}), bf16[16,8,768]{2,1,0:T(8,128)(2,1)S(1)}, u32[]{:S(2)}, u32[]{:S(2)}) %all-to-all-start) | async-done | bytes 196640 | tf_op jit(solution)/shard_map/all_to_all | solution.py:25
  30.5 3.8 %collective-permute-start.3 = (bf16[128,768]{1,0:T(8,128)(2,1)S(1)}, bf16[128,768]{1,0:T(8,128)(2,1)S(1)}, u32[]{:S(2)}, u32[]{:S(2)}) collective-permute-start(bf16[128,768]{1,0:T(8,128)(2,1)S(1)} %bitcast.7), channel_id=1, source_target_pairs={{0,1},{1,0},{2,3},{3,2},{4,5},{5,4},{6,7},{7,6},{8,9},{9,8},{10,11... | collective-permute-start | bytes 589832 | tf_op jit(solution)/shard_map/ppermute | solution.py:296
  35.6 22.7 %all_to_all.35.own_ref = bf16[4,4,64,768]{3,2,1,0:T(8,128)(2,1)S(1)} all-to-all(bf16[4,4,64,768]{3,2,1,0:T(8,128)(2,1)S(1)} %broadcast_in_dim.2), channel_id=1, replica_groups=mesh['yh'=2,'z'=8,'yl'=4,'x'=4,'core'=2] {'x'}, dimensions={0} | all-to-all | bytes 3145728 | tf_op jit(solution)/shard_map/all_to_all | solution.py:25
  58.3 4.7 %collective-permute-start.4 = (bf16[4,4,64,768]{3,2,1,0:T(8,128)(2,1)S(1)}, bf16[4,4,64,768]{3,2,1,0:T(8,128)(2,1)S(1)}, u32[]{:S(2)}, u32[]{:S(2)}) collective-permute-start(bf16[4,4,64,768]{3,2,1,0:T(8,128)(2,1)S(1)} %all_to_all.35.own_ref), channel_id=1, source_target_pairs={{0,1},{1,0},{2,3},{3,2},{4,5},{5,4},{6,7},{7,6},{8,9},{9,8},{10,11... | collective-permute-start | bytes 4718600 | tf_op jit(solution)/shard_map/ppermute | solution.py:306
  64.3 1.6 %collective-permute-done.4.other_ref = bf16[4,4,64,768]{3,2,1,0:T(8,128)(2,1)S(1)} collective-permute-done((bf16[4,4,64,768]{3,2,1,0:T(8,128)(2,1)S(1)}, bf16[4,4,64,768]{3,2,1,0:T(8,128)(2,1)S(1)}, u32[]{:S(2)}, u32[]{:S(2)}) %collective-permute-start.4) | collective-permute-done | bytes 1572896 | tf_op jit(solution)/shard_map/ppermute | solution.py:306
  66.0 2.1 %shard_map.95 = (bf16[1408,768]{1,0:T(8,128)(2,1)S(1)}, bf16[256,1408]{1,0:T(8,128)(2,1)S(1)}, bf16[256,768]{1,0:T(8,128)(2,1)S(1)}, f32[8,768]{1,0:T(8,128)S(1)...) custom-call(f32[1]{0:T(128)S(6)} %copy.10.scale_ref, ...), custom_call_target="tpu_custom_call" | custom-call | flops 700000000 | bytes 8000000 | tf_op jit(solution)/shard_map/pallas_call | solution.py:308
  68.1 1.4 copy-done
  69.5 20.3 %all_to_all.36.got_ref = f32[16,1,256]{2,1,0:T(1,128)S(1)} all-to-all(f32[16,1,256]{2,1,0:T(1,128)S(1)} %get-tuple-element.39), channel_id=1, replica_groups={{0,2,4,6,8,10,12,14,16,18,20,22,24,26,28,30},{32,34,36,38,40,42,44,46,4..., dimensions={0} | all-to-all | bytes 32768 | tf_op jit(solution)/shard_map/all_to_all | solution.py:333
  89.8 1.9 %collective-permute-start.5 = (f32[8,256]{1,0:T(8,128)S(1)}, f32[8,256]{1,0:T(8,128)S(1)}, u32[]{:S(2)}, u32[]{:S(2)}) collective-permute-start(f32[8,256]{1,0:T(8,128)S(1)} %shard_map.96.totals_ref), channel_id=1, source_target_pairs={{0,1},{1,0},{2,3},{3,2},{4,5},{5,4},{6,7},{7,6},{8,9},{9,8},{10,11... | collective-permute-start | bytes 24584 | tf_op jit(solution)/shard_map/ppermute | solution.py:342
  91.7 1.1 collective-permute-done.5.totals_other_ref
  93.5 13.4 %all_to_all.37.part_ref = bf16[16,8,768]{2,1,0:T(8,128)(2,1)S(1)} all-to-all(bf16[16,8,768]{2,1,0:T(8,128)(2,1)S(1)} %bitcast.12), channel_id=1, replica_groups=mesh['yh'=2,'z'=8,'yl'=4,'x'=4,'core'=2] {'yl','x'}, dimensions={0} | all-to-all | bytes 393216 | tf_op jit(solution)/shard_map/all_to_all | solution.py:25
  107.0 12.0 %all_to_all.38 = bf16[16,8,768]{2,1,0:T(8,128)(2,1)S(1)} all-to-all(bf16[16,8,768]{2,1,0:T(8,128)(2,1)S(1)} %get-tuple-element.44), channel_id=1, replica_groups=mesh['yh'=2,'z'=8,'yl'=4,'x'=4,'core'=2] {'yl','x'}, dimensions={0} | all-to-all | bytes 393216 | tf_op jit(solution)/shard_map/all_to_all | solution.py:25
  119.0 4.2 %collective-permute-start.6 = (bf16[128,768]{1,0:T(8,128)(2,1)S(1)}, bf16[128,768]{1,0:T(8,128)(2,1)S(1)}, u32[]{:S(2)}, u32[]{:S(2)}) collective-permute-start(bf16[128,768]{1,0:T(8,128)(2,1)S(1)} %bitcast.10), channel_id=1, source_target_pairs={{0,1},{1,0},{2,3},{3,2},{4,5},{5,4},{6,7},{7,6},{8,9},{9,8},{10,11... | collective-permute-start | bytes 589832 | tf_op jit(solution)/shard_map/ppermute | solution.py:358
  123.2 1.0 constant_dynamic-slice_fusion
  124.5 15.0 %all_to_all.39.got_ref = bf16[8,24,768]{2,1,0:T(8,128)(2,1)S(1)} all-to-all(bf16[8,24,768]{2,1,0:T(8,128)(2,1)S(1)} %shard_map.99), channel_id=1, replica_groups=mesh['yh'=2,'z'=8,'yl'=4,'x'=4,'core'=2] {'z'}, dimensions={0} | all-to-all | bytes 589824 | tf_op jit(solution)/shard_map/all_to_all | solution.py:25
  139.6 2.2 %collective-permute-start.7 = (bf16[16,768]{1,0:T(8,128)(2,1)S(1)}, bf16[16,768]{1,0:T(8,128)(2,1)S(1)}, u32[]{:S(2)}, u32[]{:S(2)}) collective-permute-start(bf16[16,768]{1,0:T(8,128)(2,1)S(1)} %get-tuple-element.54), channel_id=1, source_target_pairs={{0,256},{256,0},{1,257},{257,1},{2,258},{258,2},{3,259},{259,3},{4... | collective-permute-start | bytes 73736 | tf_op jit(solution)/shard_map/ppermute | solution.py:372
  141.9 2.2 %shard_map.102 = bf16[8,16,1408]{2,1,0:T(8,128)(2,1)} custom-call(bf16[8,768]{1,0:T(8,128)(2,1)S(1)} %get-tuple-element.56.d_own_ref, bf16[1408]{0:T(1024)(128)(2,1)S(1)} %copy-done.4, s32[8]{0:T(128)S(1)} %copy-done.6, bf16[8,16,1408]{2,1,0:T(8,128)(2,1)S(1)} %copy-done.2, bf16[1408,768]{1,0:T(8,128)(2,1)S(1)} %copy-done.1), custom_call_target="tpu_custom_call" | custom-call | flops 20000000 | bytes 3000000 | tf_op jit(solution)/shard_map/pallas_call | solution.py:374
  144.0 4.1 %collective-permute-done.7.got_ref = bf16[16,768]{1,0:T(8,128)(2,1)S(1)} collective-permute-done((bf16[16,768]{1,0:T(8,128)(2,1)S(1)}, bf16[16,768]{1,0:T(8,128)(2,1)S(1)}, u32[]{:S(2)}, u32[]{:S(2)}) %collective-permute-start.7) | collective-permute-done | bytes 24608 | tf_op jit(solution)/shard_map/ppermute | solution.py:372
  148.1 10.1 %all_to_all.40.got_ref = bf16[8,8,768]{2,1,0:T(8,128)(2,1)S(1)} all-to-all(bf16[8,8,768]{2,1,0:T(8,128)(2,1)S(1)} %get-tuple-element.59), channel_id=1, replica_groups=mesh['yh'=2,'z'=8,'yl'=4,'x'=4,'core'=2] {'z'}, dimensions={0} | all-to-all | bytes 196608 | tf_op jit(solution)/shard_map/all_to_all | solution.py:25
  (29 shorter events, 3.8 us)
Async XLA Ops:
  2.7 27.9 %all-to-all-start = ((bf16[16,8,768]{2,1,0:T(8,128)(2,1)}), bf16[16,8,768]{2,1,0:T(8,128)(2,1)S(1)}, u32[]{:S(2)}, u32[]{:S(2)}) async-start(bf16[16,8,768]{2,1,0:T(8,128)(2,1)} %get-tuple-element.34), calls=%async_computation | async-start | bytes 393216 | tf_op jit(solution)/shard_map/all_to_all | solution.py:25
  18.9 15.4 %collective-permute-start = (bf16[64,768]{1,0:T(8,128)(2,1)}, bf16[64,768]{1,0:T(8,128)(2,1)S(1)}, u32[]{:S(2)}, u32[]{:S(2)}) collective-permute-start(bf16[64,768]{1,0:T(8,128)(2,1)} %get-tuple-element.33), channel_id=1, source_target_pairs={{0,8},{8,0},{16,24},{24,16},{1,9},{9,1},{17,25},{25,17},{2,10},{10... | collective-permute-start | bytes 294920 | tf_op jit(solution)/shard_map/ppermute | solution.py:299
  21.2 13.2 %collective-permute-start.1 = (bf16[64,768]{1,0:T(8,128)(2,1)}, bf16[64,768]{1,0:T(8,128)(2,1)S(1)}, u32[]{:S(2)}, u32[]{:S(2)}) collective-permute-start(bf16[64,768]{1,0:T(8,128)(2,1)} %get-tuple-element.33), channel_id=1, source_target_pairs={{0,16},{8,24},{16,0},{24,8},{1,17},{9,25},{17,1},{25,9},{2,18},{10... | collective-permute-start | bytes 294920 | tf_op jit(solution)/shard_map/ppermute | solution.py:299
  23.7 10.8 %collective-permute-start.2 = (bf16[64,768]{1,0:T(8,128)(2,1)}, bf16[64,768]{1,0:T(8,128)(2,1)S(1)}, u32[]{:S(2)}, u32[]{:S(2)}) collective-permute-start(bf16[64,768]{1,0:T(8,128)(2,1)} %get-tuple-element.33), channel_id=1, source_target_pairs={{0,24},{8,16},{16,8},{24,0},{1,25},{9,17},{17,9},{25,1},{2,26},{10... | collective-permute-start | bytes 294920 | tf_op jit(solution)/shard_map/ppermute | solution.py:299
  30.5 4.9 %collective-permute-start.3 = (bf16[128,768]{1,0:T(8,128)(2,1)S(1)}, bf16[128,768]{1,0:T(8,128)(2,1)S(1)}, u32[]{:S(2)}, u32[]{:S(2)}) collective-permute-start(bf16[128,768]{1,0:T(8,128)(2,1)S(1)} %bitcast.7), channel_id=1, source_target_pairs={{0,1},{1,0},{2,3},{3,2},{4,5},{5,4},{6,7},{7,6},{8,9},{9,8},{10,11... | collective-permute-start | bytes 589832 | tf_op jit(solution)/shard_map/ppermute | solution.py:296
  58.3 7.7 %collective-permute-start.4 = (bf16[4,4,64,768]{3,2,1,0:T(8,128)(2,1)S(1)}, bf16[4,4,64,768]{3,2,1,0:T(8,128)(2,1)S(1)}, u32[]{:S(2)}, u32[]{:S(2)}) collective-permute-start(bf16[4,4,64,768]{3,2,1,0:T(8,128)(2,1)S(1)} %all_to_all.35.own_ref), channel_id=1, source_target_pairs={{0,1},{1,0},{2,3},{3,2},{4,5},{5,4},{6,7},{7,6},{8,9},{9,8},{10,11... | collective-permute-start | bytes 4718600 | tf_op jit(solution)/shard_map/ppermute | solution.py:306
  68.1 1.4 copy-start
  69.5 49.5 %copy-start.5 = (bf16[256,1408]{1,0:T(8,128)(2,1)}, bf16[256,1408]{1,0:T(8,128)(2,1)S(1)}, u32[]{:S(2)}) copy-start(bf16[256,1408]{1,0:T(8,128)(2,1)S(1)} %get-tuple-element.47) | copy-start | bytes 2162692
  89.8 3.1 %collective-permute-start.5 = (f32[8,256]{1,0:T(8,128)S(1)}, f32[8,256]{1,0:T(8,128)S(1)}, u32[]{:S(2)}, u32[]{:S(2)}) collective-permute-start(f32[8,256]{1,0:T(8,128)S(1)} %shard_map.96.totals_ref), channel_id=1, source_target_pairs={{0,1},{1,0},{2,3},{3,2},{4,5},{5,4},{6,7},{7,6},{8,9},{9,8},{10,11... | collective-permute-start | bytes 24584 | tf_op jit(solution)/shard_map/ppermute | solution.py:342
  93.4 48.4 %copy-start.1 = (bf16[1408,768]{1,0:T(8,128)(2,1)S(1)}, bf16[1408,768]{1,0:T(8,128)(2,1)}, u32[]{:S(2)}) copy-start(bf16[1408,768]{1,0:T(8,128)(2,1)} %copy-done) | copy-start | bytes 6488068
  93.4 48.4 %copy-start.2 = (bf16[8,16,1408]{2,1,0:T(8,128)(2,1)S(1)}, bf16[8,16,1408]{2,1,0:T(8,128)(2,1)}, u32[]{:S(2)}) copy-start(bf16[8,16,1408]{2,1,0:T(8,128)(2,1)} %clips_hbm.3) | copy-start | bytes 1081348
  93.4 48.4 %copy-start.4 = (bf16[1408]{0:T(1024)(128)(2,1)S(1)}, bf16[1408]{0:T(1024)(128)(2,1)}, u32[]{:S(2)}) copy-start(bf16[1408]{0:T(1024)(128)(2,1)} %query_hbm.3) | copy-start | bytes 8452
  93.4 48.4 %copy-start.6 = (s32[8]{0:T(128)S(1)}, s32[8]{0:T(128)}, u32[]{:S(2)}) copy-start(s32[8]{0:T(128)} %counts_hbm.3) | copy-start | bytes 100
  119.0 5.3 %collective-permute-start.6 = (bf16[128,768]{1,0:T(8,128)(2,1)S(1)}, bf16[128,768]{1,0:T(8,128)(2,1)S(1)}, u32[]{:S(2)}, u32[]{:S(2)}) collective-permute-start(bf16[128,768]{1,0:T(8,128)(2,1)S(1)} %bitcast.10), channel_id=1, source_target_pairs={{0,1},{1,0},{2,3},{3,2},{4,5},{5,4},{6,7},{7,6},{8,9},{9,8},{10,11... | collective-permute-start | bytes 589832 | tf_op jit(solution)/shard_map/ppermute | solution.py:358
  139.6 8.5 %collective-permute-start.7 = (bf16[16,768]{1,0:T(8,128)(2,1)S(1)}, bf16[16,768]{1,0:T(8,128)(2,1)S(1)}, u32[]{:S(2)}, u32[]{:S(2)}) collective-permute-start(bf16[16,768]{1,0:T(8,128)(2,1)S(1)} %get-tuple-element.54), channel_id=1, source_target_pairs={{0,256},{256,0},{1,257},{257,1},{2,258},{258,2},{3,259},{259,3},{4... | collective-permute-start | bytes 73736 | tf_op jit(solution)/shard_map/ppermute | solution.py:372
  141.8 16.3 %copy-start.3 = (bf16[8,768]{1,0:T(8,128)(2,1)S(1)}, bf16[8,768]{1,0:T(8,128)(2,1)}, u32[]{:S(2)}) copy-start(bf16[8,768]{1,0:T(8,128)(2,1)} %text_ref.1) | copy-start | bytes 36868

commit v7 on v6

--- a/solution.py
+++ b/solution.py
@@ -295,11 +295,11 @@
     text_own = exchange(text_send, DP).reshape(n_lane, joint)
     text_other = lax.ppermute(text_own, "core", SWAP)
 
-    near = [payload] + [
-        lax.ppermute(payload, "yl", [(i, i ^ k) for i in range(n_yl)]) for k in range(1, n_yl)
-    ]
-    over_y = jnp.stack(near)
-    over_y, text_own, text_other = lax.optimization_barrier((over_y, text_own, text_other))
+    near = {0: payload}
+    for k in range(n_yl - 1, 0, -1):
+        near[k] = lax.ppermute(payload, "yl", [(i, i ^ k) for i in range(n_yl)])
+    over_y = jnp.stack([near[k] for k in range(n_yl)])
+    over_y, text_own = lax.optimization_barrier((over_y, text_own))
     over_x = exchange(jnp.broadcast_to(over_y[None], (n_x, *over_y.shape)), "x")
 
     pairs = pair_index.reshape(n_dp, group_rows)

time: 160 us -> 161 us (level)
  waiting for transfers between devices: 9.27 us -> 11.5 us
  starting transfers between devices: 42.3 us -> 40.4 us
    ppermute x3, waiting for transfers between devices: 0.12 us -> 6.23 us  [shards(): near[k] = lax.ppermute(payload, 'yl', [(i, i ^ k) for i in range(n_yl)])]
    all_to_all x1, waiting for transfers between devices: 2.31 us -> 0.01 us  [exchange(): return lax.all_to_all(blocks, axes, split_axis=0, concat_axis=0, tiled=True)]
    ppermute x1, starting transfers between devices: 3.8 us -> 1.92 us  [shards(): text_other = lax.ppermute(text_own, 'core', SWAP)]
    ppermute x1, waiting for transfers between devices: 1.64 us -> 0.01 us  [shards(): over_x_other = lax.ppermute(over_x, 'core', SWAP)]
  transfers between devices with their start and end apart: 9 -> 9, of which waited for: 5 -> 3; matrix products, arithmetic and copies ran while one was open for 2% -> 2% of each run, Pallas kernels for 1% -> 1%
where the time goes in v7:
time: 161 us; the launch traced here: 159 us
  blocking collectives  93.5 us (58%)
  starting transfers between devices  40.4 us (25%)
  waiting for transfers between devices  11.5 us (7%)
  Pallas kernels  8.08 us (5%)
  local copies, waits for them, and re-layouts  3.28 us (2%)
    all_to_all x5, blocking collectives, exchange(): return lax.all_to_all(blocks, axes, split_axis=0, concat_axis=0, tiled=True)  73.9 us
    all_to_all x1, blocking collectives, shards(): lax.all_to_all(totals_send, DP + CLIP, split_axis=0, concat_axis=0, tiled...  19.7 us
    all_to_all x1, starting transfers between devices, exchange(): return lax.all_to_all(blocks, axes, split_axis=0, concat_axis=0, tiled=True)  16.2 us
    ppermute x3, starting transfers between devices, shards(): near[k] = lax.ppermute(payload, 'yl', [(i, i ^ k) for i in range(n_yl)])  9.27 us
    ppermute x3, waiting for transfers between devices, shards(): near[k] = lax.ppermute(payload, 'yl', [(i, i ^ k) for i in range(n_yl)])  6.23 us
    ppermute x1, starting transfers between devices, shards(): over_x_other = lax.ppermute(over_x, 'core', SWAP)  4.67 us
    ppermute x1, starting transfers between devices, shards(): d_half_other = lax.ppermute(d_half, 'core', SWAP)  4.22 us
    ppermute x1, waiting for transfers between devices, shards(): got_yh = lax.ppermute(away, 'yh', SWAP)  4.05 us
  transfers between devices with their start and end apart: 9, of which 3 were waited for; matrix products, arithmetic and copies ran while one was open for 2% of the time, Pallas kernels for 1%

profile of v7, /device:TPU:1, one launch (start us, length us, event | category | flops | bytes accessed | tf_op | source)
XLA Modules:
  0.0 159.3 jit_solution(2186383029723114405)
XLA Ops:
  0.6 2.0 %shard_map.94 = (bf16[64,768]{1,0:T(8,128)(2,1)}, bf16[16,8,768]{2,1,0:T(8,128)(2,1)}) custom-call(bf16[1408]{0:T(1024)(128)(2,1)} %query_hbm.3, s32[8]{0:T(128)} %counts_hbm.3, bf16[8,16,1408]{2,1,0:T(8,128)(2,1)} %clips_hbm.3, bf16[44,768]{1,0:T(8,128)(2,1)} %rows_hbm.1, bf16[8,768]{1,0:T(8,128)(2,1)} %text_ref.1), custom_call_target="tpu_custom_call" | custom-call | flops 1000000 | bytes 1000000 | tf_op jit(solution)/shard_map/pallas_call | solution.py:281
  2.7 16.2 %all-to-all-start = ((bf16[16,8,768]{2,1,0:T(8,128)(2,1)}), bf16[16,8,768]{2,1,0:T(8,128)(2,1)S(1)}, u32[]{:S(2)}, u32[]{:S(2)}) async-start(bf16[16,8,768]{2,1,0:T(8,128)(2,1)} %get-tuple-element.33), calls=%async_computation | async-start | bytes 393216 | tf_op jit(solution)/shard_map/all_to_all | solution.py:25
  18.9 2.3 %collective-permute-start = (bf16[64,768]{1,0:T(8,128)(2,1)}, bf16[64,768]{1,0:T(8,128)(2,1)S(1)}, u32[]{:S(2)}, u32[]{:S(2)}) collective-permute-start(bf16[64,768]{1,0:T(8,128)(2,1)} %get-tuple-element.32), channel_id=1, source_target_pairs={{0,8},{8,0},{16,24},{24,16},{1,9},{9,1},{17,25},{25,17},{2,10},{10... | collective-permute-start | bytes 294920 | tf_op jit(solution)/shard_map/ppermute | solution.py:300
  21.2 2.4 %collective-permute-start.1 = (bf16[64,768]{1,0:T(8,128)(2,1)}, bf16[64,768]{1,0:T(8,128)(2,1)S(1)}, u32[]{:S(2)}, u32[]{:S(2)}) collective-permute-start(bf16[64,768]{1,0:T(8,128)(2,1)} %get-tuple-element.32), channel_id=1, source_target_pairs={{0,16},{8,24},{16,0},{24,8},{1,17},{9,25},{17,1},{25,9},{2,18},{10... | collective-permute-start | bytes 294920 | tf_op jit(solution)/shard_map/ppermute | solution.py:300
  23.7 4.5 %collective-permute-start.2 = (bf16[64,768]{1,0:T(8,128)(2,1)}, bf16[64,768]{1,0:T(8,128)(2,1)S(1)}, u32[]{:S(2)}, u32[]{:S(2)}) collective-permute-start(bf16[64,768]{1,0:T(8,128)(2,1)} %get-tuple-element.32), channel_id=1, source_target_pairs={{0,24},{8,16},{16,8},{24,0},{1,25},{9,17},{17,9},{25,1},{2,26},{10... | collective-permute-start | bytes 294920 | tf_op jit(solution)/shard_map/ppermute | solution.py:300
  28.2 6.2 %collective-permute-done.1 = bf16[64,768]{1,0:T(8,128)(2,1)S(1)} collective-permute-done((bf16[64,768]{1,0:T(8,128)(2,1)}, bf16[64,768]{1,0:T(8,128)(2,1)S(1)}, u32[]{:S(2)}, u32[]{:S(2)}) %collective-permute-start.1) | collective-permute-done | bytes 98336 | tf_op jit(solution)/shard_map/ppermute | solution.py:300
  34.5 0.9 pad_maximum_fusion
  35.6 22.7 %all_to_all.35.own_ref = bf16[4,4,64,768]{3,2,1,0:T(8,128)(2,1)S(1)} all-to-all(bf16[4,4,64,768]{3,2,1,0:T(8,128)(2,1)S(1)} %broadcast_in_dim.2), channel_id=1, replica_groups=mesh['yh'=2,'z'=8,'yl'=4,'x'=4,'core'=2] {'x'}, dimensions={0} | all-to-all | bytes 3145728 | tf_op jit(solution)/shard_map/all_to_all | solution.py:25
  58.3 4.7 %collective-permute-start.3 = (bf16[4,4,64,768]{3,2,1,0:T(8,128)(2,1)S(1)}, bf16[4,4,64,768]{3,2,1,0:T(8,128)(2,1)S(1)}, u32[]{:S(2)}, u32[]{:S(2)}) collective-permute-start(bf16[4,4,64,768]{3,2,1,0:T(8,128)(2,1)S(1)} %all_to_all.35.own_ref), channel_id=1, source_target_pairs={{0,1},{1,0},{2,3},{3,2},{4,5},{5,4},{6,7},{7,6},{8,9},{9,8},{10,11... | collective-permute-start | bytes 4718600 | tf_op jit(solution)/shard_map/ppermute | solution.py:306
  63.0 1.9 %collective-permute-start.4 = (bf16[128,768]{1,0:T(8,128)(2,1)S(1)}, bf16[128,768]{1,0:T(8,128)(2,1)S(1)}, u32[]{:S(2)}, u32[]{:S(2)}) collective-permute-start(bf16[128,768]{1,0:T(8,128)(2,1)S(1)} %bitcast.7), channel_id=1, source_target_pairs={{0,1},{1,0},{2,3},{3,2},{4,5},{5,4},{6,7},{7,6},{8,9},{9,8},{10,11... | collective-permute-start | bytes 589832 | tf_op jit(solution)/shard_map/ppermute | solution.py:296
  66.3 2.1 %shard_map.95 = (bf16[1408,768]{1,0:T(8,128)(2,1)S(1)}, bf16[256,1408]{1,0:T(8,128)(2,1)S(1)}, bf16[256,768]{1,0:T(8,128)(2,1)S(1)}, f32[8,768]{1,0:T(8,128)S(1)...) custom-call(f32[1]{0:T(128)S(6)} %copy.10.scale_ref, ...), custom_call_target="tpu_custom_call" | custom-call | flops 700000000 | bytes 8000000 | tf_op jit(solution)/shard_map/pallas_call | solution.py:308
  68.4 1.4 copy-done
  69.8 19.7 %all_to_all.36.got_ref = f32[16,1,256]{2,1,0:T(1,128)S(1)} all-to-all(f32[16,1,256]{2,1,0:T(1,128)S(1)} %get-tuple-element.37), channel_id=1, replica_groups={{0,2,4,6,8,10,12,14,16,18,20,22,24,26,28,30},{32,34,36,38,40,42,44,46,4..., dimensions={0} | all-to-all | bytes 32768 | tf_op jit(solution)/shard_map/all_to_all | solution.py:333
  89.5 1.9 %collective-permute-start.5 = (f32[8,256]{1,0:T(8,128)S(1)}, f32[8,256]{1,0:T(8,128)S(1)}, u32[]{:S(2)}, u32[]{:S(2)}) collective-permute-start(f32[8,256]{1,0:T(8,128)S(1)} %shard_map.96.totals_ref), channel_id=1, source_target_pairs={{0,1},{1,0},{2,3},{3,2},{4,5},{5,4},{6,7},{7,6},{8,9},{9,8},{10,11... | collective-permute-start | bytes 24584 | tf_op jit(solution)/shard_map/ppermute | solution.py:342
  91.4 1.1 collective-permute-done.5.totals_other_ref
  93.1 14.1 %all_to_all.37.part_ref = bf16[16,8,768]{2,1,0:T(8,128)(2,1)S(1)} all-to-all(bf16[16,8,768]{2,1,0:T(8,128)(2,1)S(1)} %bitcast.12), channel_id=1, replica_groups=mesh['yh'=2,'z'=8,'yl'=4,'x'=4,'core'=2] {'yl','x'}, dimensions={0} | all-to-all | bytes 393216 | tf_op jit(solution)/shard_map/all_to_all | solution.py:25
  107.3 12.0 %all_to_all.38 = bf16[16,8,768]{2,1,0:T(8,128)(2,1)S(1)} all-to-all(bf16[16,8,768]{2,1,0:T(8,128)(2,1)S(1)} %get-tuple-element.42), channel_id=1, replica_groups=mesh['yh'=2,'z'=8,'yl'=4,'x'=4,'core'=2] {'yl','x'}, dimensions={0} | all-to-all | bytes 393216 | tf_op jit(solution)/shard_map/all_to_all | solution.py:25
  119.3 4.2 %collective-permute-start.6 = (bf16[128,768]{1,0:T(8,128)(2,1)S(1)}, bf16[128,768]{1,0:T(8,128)(2,1)S(1)}, u32[]{:S(2)}, u32[]{:S(2)}) collective-permute-start(bf16[128,768]{1,0:T(8,128)(2,1)S(1)} %bitcast.10), channel_id=1, source_target_pairs={{0,1},{1,0},{2,3},{3,2},{4,5},{5,4},{6,7},{7,6},{8,9},{9,8},{10,11... | collective-permute-start | bytes 589832 | tf_op jit(solution)/shard_map/ppermute | solution.py:358
  123.6 1.0 constant_dynamic-slice_fusion
  124.8 15.0 %all_to_all.39.got_ref = bf16[8,24,768]{2,1,0:T(8,128)(2,1)S(1)} all-to-all(bf16[8,24,768]{2,1,0:T(8,128)(2,1)S(1)} %shard_map.99), channel_id=1, replica_groups=mesh['yh'=2,'z'=8,'yl'=4,'x'=4,'core'=2] {'z'}, dimensions={0} | all-to-all | bytes 589824 | tf_op jit(solution)/shard_map/all_to_all | solution.py:25
  139.9 2.2 %collective-permute-start.7 = (bf16[16,768]{1,0:T(8,128)(2,1)S(1)}, bf16[16,768]{1,0:T(8,128)(2,1)S(1)}, u32[]{:S(2)}, u32[]{:S(2)}) collective-permute-start(bf16[16,768]{1,0:T(8,128)(2,1)S(1)} %get-tuple-element.52), channel_id=1, source_target_pairs={{0,256},{256,0},{1,257},{257,1},{2,258},{258,2},{3,259},{259,3},{4... | collective-permute-start | bytes 73736 | tf_op jit(solution)/shard_map/ppermute | solution.py:372
  142.2 2.2 %shard_map.102 = bf16[8,16,1408]{2,1,0:T(8,128)(2,1)} custom-call(bf16[8,768]{1,0:T(8,128)(2,1)S(1)} %get-tuple-element.54.d_own_ref, bf16[1408]{0:T(1024)(128)(2,1)S(1)} %copy-done.4, s32[8]{0:T(128)S(1)} %copy-done.6, bf16[8,16,1408]{2,1,0:T(8,128)(2,1)S(1)} %copy-done.2, bf16[1408,768]{1,0:T(8,128)(2,1)S(1)} %copy-done.1), custom_call_target="tpu_custom_call" | custom-call | flops 20000000 | bytes 3000000 | tf_op jit(solution)/shard_map/pallas_call | solution.py:374
  144.4 4.0 %collective-permute-done.7.got_ref = bf16[16,768]{1,0:T(8,128)(2,1)S(1)} collective-permute-done((bf16[16,768]{1,0:T(8,128)(2,1)S(1)}, bf16[16,768]{1,0:T(8,128)(2,1)S(1)}, u32[]{:S(2)}, u32[]{:S(2)}) %collective-permute-start.7) | collective-permute-done | bytes 24608 | tf_op jit(solution)/shard_map/ppermute | solution.py:372
  148.4 10.1 %all_to_all.40.got_ref = bf16[8,8,768]{2,1,0:T(8,128)(2,1)S(1)} all-to-all(bf16[8,8,768]{2,1,0:T(8,128)(2,1)S(1)} %get-tuple-element.57), channel_id=1, replica_groups=mesh['yh'=2,'z'=8,'yl'=4,'x'=4,'core'=2] {'z'}, dimensions={0} | all-to-all | bytes 196608 | tf_op jit(solution)/shard_map/all_to_all | solution.py:25
  (29 shorter events, 2.7 us)
Async XLA Ops:
  2.7 32.7 %all-to-all-start = ((bf16[16,8,768]{2,1,0:T(8,128)(2,1)}), bf16[16,8,768]{2,1,0:T(8,128)(2,1)S(1)}, u32[]{:S(2)}, u32[]{:S(2)}) async-start(bf16[16,8,768]{2,1,0:T(8,128)(2,1)} %get-tuple-element.33), calls=%async_computation | async-start | bytes 393216 | tf_op jit(solution)/shard_map/all_to_all | solution.py:25
  18.9 9.3 %collective-permute-start = (bf16[64,768]{1,0:T(8,128)(2,1)}, bf16[64,768]{1,0:T(8,128)(2,1)S(1)}, u32[]{:S(2)}, u32[]{:S(2)}) collective-permute-start(bf16[64,768]{1,0:T(8,128)(2,1)} %get-tuple-element.32), channel_id=1, source_target_pairs={{0,8},{8,0},{16,24},{24,16},{1,9},{9,1},{17,25},{25,17},{2,10},{10... | collective-permute-start | bytes 294920 | tf_op jit(solution)/shard_map/ppermute | solution.py:300
  21.2 13.2 %collective-permute-start.1 = (bf16[64,768]{1,0:T(8,128)(2,1)}, bf16[64,768]{1,0:T(8,128)(2,1)S(1)}, u32[]{:S(2)}, u32[]{:S(2)}) collective-permute-start(bf16[64,768]{1,0:T(8,128)(2,1)} %get-tuple-element.32), channel_id=1, source_target_pairs={{0,16},{8,24},{16,0},{24,8},{1,17},{9,25},{17,1},{25,9},{2,18},{10... | collective-permute-start | bytes 294920 | tf_op jit(solution)/shard_map/ppermute | solution.py:300
  23.7 10.8 %collective-permute-start.2 = (bf16[64,768]{1,0:T(8,128)(2,1)}, bf16[64,768]{1,0:T(8,128)(2,1)S(1)}, u32[]{:S(2)}, u32[]{:S(2)}) collective-permute-start(bf16[64,768]{1,0:T(8,128)(2,1)} %get-tuple-element.32), channel_id=1, source_target_pairs={{0,24},{8,16},{16,8},{24,0},{1,25},{9,17},{17,9},{25,1},{2,26},{10... | collective-permute-start | bytes 294920 | tf_op jit(solution)/shard_map/ppermute | solution.py:300
  58.3 8.0 %collective-permute-start.3 = (bf16[4,4,64,768]{3,2,1,0:T(8,128)(2,1)S(1)}, bf16[4,4,64,768]{3,2,1,0:T(8,128)(2,1)S(1)}, u32[]{:S(2)}, u32[]{:S(2)}) collective-permute-start(bf16[4,4,64,768]{3,2,1,0:T(8,128)(2,1)S(1)} %all_to_all.35.own_ref), channel_id=1, source_target_pairs={{0,1},{1,0},{2,3},{3,2},{4,5},{5,4},{6,7},{7,6},{8,9},{9,8},{10,11... | collective-permute-start | bytes 4718600 | tf_op jit(solution)/shard_map/ppermute | solution.py:306
  63.0 3.3 %collective-permute-start.4 = (bf16[128,768]{1,0:T(8,128)(2,1)S(1)}, bf16[128,768]{1,0:T(8,128)(2,1)S(1)}, u32[]{:S(2)}, u32[]{:S(2)}) collective-permute-start(bf16[128,768]{1,0:T(8,128)(2,1)S(1)} %bitcast.7), channel_id=1, source_target_pairs={{0,1},{1,0},{2,3},{3,2},{4,5},{5,4},{6,7},{7,6},{8,9},{9,8},{10,11... | collective-permute-start | bytes 589832 | tf_op jit(solution)/shard_map/ppermute | solution.py:296
  68.4 1.4 copy-start
  69.8 49.5 %copy-start.5 = (bf16[256,1408]{1,0:T(8,128)(2,1)}, bf16[256,1408]{1,0:T(8,128)(2,1)S(1)}, u32[]{:S(2)}) copy-start(bf16[256,1408]{1,0:T(8,128)(2,1)S(1)} %get-tuple-element.45) | copy-start | bytes 2162692
  89.5 3.1 %collective-permute-start.5 = (f32[8,256]{1,0:T(8,128)S(1)}, f32[8,256]{1,0:T(8,128)S(1)}, u32[]{:S(2)}, u32[]{:S(2)}) collective-permute-start(f32[8,256]{1,0:T(8,128)S(1)} %shard_map.96.totals_ref), channel_id=1, source_target_pairs={{0,1},{1,0},{2,3},{3,2},{4,5},{5,4},{6,7},{7,6},{8,9},{9,8},{10,11... | collective-permute-start | bytes 24584 | tf_op jit(solution)/shard_map/ppermute | solution.py:342
  93.0 49.1 %copy-start.1 = (bf16[1408,768]{1,0:T(8,128)(2,1)S(1)}, bf16[1408,768]{1,0:T(8,128)(2,1)}, u32[]{:S(2)}) copy-start(bf16[1408,768]{1,0:T(8,128)(2,1)} %copy-done) | copy-start | bytes 6488068
  93.1 49.1 %copy-start.2 = (bf16[8,16,1408]{2,1,0:T(8,128)(2,1)S(1)}, bf16[8,16,1408]{2,1,0:T(8,128)(2,1)}, u32[]{:S(2)}) copy-start(bf16[8,16,1408]{2,1,0:T(8,128)(2,1)} %clips_hbm.3) | copy-start | bytes 1081348
  93.1 49.1 %copy-start.4 = (bf16[1408]{0:T(1024)(128)(2,1)S(1)}, bf16[1408]{0:T(1024)(128)(2,1)}, u32[]{:S(2)}) copy-start(bf16[1408]{0:T(1024)(128)(2,1)} %query_hbm.3) | copy-start | bytes 8452
  93.1 49.1 %copy-start.6 = (s32[8]{0:T(128)S(1)}, s32[8]{0:T(128)}, u32[]{:S(2)}) copy-start(s32[8]{0:T(128)} %counts_hbm.3) | copy-start | bytes 100
  119.3 5.3 %collective-permute-start.6 = (bf16[128,768]{1,0:T(8,128)(2,1)S(1)}, bf16[128,768]{1,0:T(8,128)(2,1)S(1)}, u32[]{:S(2)}, u32[]{:S(2)}) collective-permute-start(bf16[128,768]{1,0:T(8,128)(2,1)S(1)} %bitcast.10), channel_id=1, source_target_pairs={{0,1},{1,0},{2,3},{3,2},{4,5},{5,4},{6,7},{7,6},{8,9},{9,8},{10,11... | collective-permute-start | bytes 589832 | tf_op jit(solution)/shard_map/ppermute | solution.py:358
  139.9 8.5 %collective-permute-start.7 = (bf16[16,768]{1,0:T(8,128)(2,1)S(1)}, bf16[16,768]{1,0:T(8,128)(2,1)S(1)}, u32[]{:S(2)}, u32[]{:S(2)}) collective-permute-start(bf16[16,768]{1,0:T(8,128)(2,1)S(1)} %get-tuple-element.52), channel_id=1, source_target_pairs={{0,256},{256,0},{1,257},{257,1},{2,258},{258,2},{3,259},{259,3},{4... | collective-permute-start | bytes 73736 | tf_op jit(solution)/shard_map/ppermute | solution.py:372
  142.2 16.3 %copy-start.3 = (bf16[8,768]{1,0:T(8,128)(2,1)S(1)}, bf16[8,768]{1,0:T(8,128)(2,1)}, u32[]{:S(2)}) copy-start(bf16[8,768]{1,0:T(8,128)(2,1)} %text_ref.1) | copy-start | bytes 36868
